TPU v7x, 32 devices: a whole 2x2x4 slice. The times are simulated.
32 devices in a mesh: smp: 4 (over y, core), gx: 4 (over z), gz: 2 (over x).
Axes of the slice: x: 2, y: 2, z: 4, core: 2. Of those that a mesh axis runs over, the one named last changes fastest.
Arguments:
- features: bfloat16 [4, 32, 20, 8, 256], P('smp', None, 'gx', None, 'gz'), may hold values from -6 to 6
- first_weight: bfloat16 [32, 3, 3, 3, 32], replicated, may hold values from -0.21875 to 0.21875
- first_bias: float32 [32], replicated, may hold values from -1 to 1
- second_weight: bfloat16 [32, 3, 3, 3, 32], replicated, may hold values from -0.21875 to 0.21875
- second_bias: float32 [32], replicated, may hold values from -1 to 1
- cotangent: bfloat16 [4, 32, 20, 8, 256], P('smp', None, 'gx', None, 'gz'), may hold values from -6 to 6
Outputs:
- output: bfloat16 [4, 32, 20, 8, 256], P('smp', None, 'gx', None, 'gz')
- first_grad: float32 [32, 3, 3, 3, 32], replicated
- first_bias_grad: float32 [32], replicated
- second_grad: float32 [32, 3, 3, 3, 32], replicated
- second_bias_grad: float32 [32], replicated
All inputs are finite; a program needn't handle non-finite values.
Results may differ from a plain program's by a relative error of at most 0.011.
Values may be sent and summed in bfloat16 or wider, within the bound.
No kernel may reach another device: no remote copies, remote signals or barrier semaphores. Data moves between devices by JAX's collectives and lax.ppermute only.
A program may use at most 128 MiB of HBM per device.

v0:
```python
import jax
import jax.numpy as jnp
from jax import lax
from jax.sharding import PartitionSpec as P


def extended(array, sides, width):
    for axis, dim in sides:
        size, length = (lax.axis_size(axis), array.shape[dim])
        up = [(i, (i + 1) % size) for i in range(size)]
        down = [(j, i) for i, j in up]
        last = lax.slice_in_dim(array, length - width, length, axis=dim)
        initial = lax.slice_in_dim(array, 0, width, axis=dim)
        before = lax.ppermute(last, axis, up)
        after = lax.ppermute(initial, axis, down)
        array = jnp.concatenate([before, array, after], axis=dim)
    return array


def wall_pad(field_in):
    return jnp.pad(field_in, ((0, 0), (0, 0), (0, 0), (1, 1), (0, 0)))


def extend(field_in, depth_cells):
    both_wide = extended(field_in, (("gx", 2), ("gz", 4)), depth_cells)
    return wall_pad(both_wide)


def stack_taps(padded, offset_x, offset_y, cells_x, cells_y, cells_z):
    return jnp.concatenate(
        [
            padded[
                :,
                :,
                offset_x : offset_x + cells_x,
                offset_y : offset_y + cells_y,
                offset_z : offset_z + cells_z,
            ]
            for offset_z in range(3)
        ],
        axis=1,
    )


def convolve(padded, weight):
    cells_x = padded.shape[2] - 2
    cells_y = padded.shape[3] - 2
    cells_z = padded.shape[4] - 2
    summed = jnp.zeros((padded.shape[0], weight.shape[0], cells_x, cells_y, cells_z), jnp.float32)
    for offset_x in range(3):
        for offset_y in range(3):
            stacked = stack_taps(padded, offset_x, offset_y, cells_x, cells_y, cells_z)
            tap_block = weight[:, offset_x, offset_y].reshape(weight.shape[0], -1)
            summed = summed + jnp.einsum(
                "ok,skxyz->soxyz", tap_block, stacked, preferred_element_type=jnp.float32
            )
    return summed


def correlate(upstream, padded):
    cells_x = upstream.shape[2]
    cells_y = upstream.shape[3]
    cells_z = upstream.shape[4]
    outer_terms = []
    for offset_x in range(3):
        inner_terms = []
        for offset_y in range(3):
            stacked = stack_taps(padded, offset_x, offset_y, cells_x, cells_y, cells_z)
            local_term = jnp.einsum(
                "soxyz,skxyz->ok", upstream, stacked, preferred_element_type=jnp.float32
            )
            inner_terms.append(local_term.reshape(upstream.shape[1], 3, -1))
        outer_terms.append(jnp.stack(inner_terms, axis=1))
    return jnp.stack(outer_terms, axis=1)


def shards(features, first_weight, first_bias, second_weight, second_bias, cotangent):
    input_pad = extend(features, 1)
    preact = convolve(input_pad, first_weight) + first_bias[None, :, None, None, None]
    hidden = jax.nn.silu(preact).astype(jnp.bfloat16)
    hidden_pad = extend(hidden, 1)
    residual_term = convolve(hidden_pad, second_weight) + second_bias[None, :, None, None, None]
    output = (features.astype(jnp.float32) + residual_term).astype(jnp.bfloat16)
    cells_all = (
        features.shape[0]
        * lax.axis_size("smp")
        * features.shape[2]
        * lax.axis_size("gx")
        * features.shape[3]
        * features.shape[4]
        * lax.axis_size("gz")
    )
    grad_scale = 1.0 / cells_all**0.5
    second_grad = correlate(cotangent, hidden_pad) * grad_scale
    second_bgrad = jnp.sum(cotangent, axis=(0, 2, 3, 4), dtype=jnp.float32) * grad_scale
    flipped = jnp.transpose(jnp.flip(second_weight, (1, 2, 3)), (4, 1, 2, 3, 0))
    upstream_pad = extend(cotangent, 1)
    hidden_grad = convolve(upstream_pad, flipped)
    logistic = jax.nn.sigmoid(preact)
    preact_grad = (hidden_grad * logistic * (1.0 + preact * (1.0 - logistic))).astype(jnp.bfloat16)
    first_grad = correlate(preact_grad, input_pad) * grad_scale
    first_bgrad = jnp.sum(preact_grad, axis=(0, 2, 3, 4), dtype=jnp.float32) * grad_scale
    first_grad, first_bgrad, second_grad, second_bgrad = lax.psum(
        (first_grad, first_bgrad, second_grad, second_bgrad), ("smp", "gx", "gz")
    )
    return (output, first_grad, first_bgrad, second_grad, second_bgrad)


def solution(mesh):
    in_specs = (
        P("smp", None, "gx", None, "gz"),
        P(),
        P(),
        P(),
        P(),
        P("smp", None, "gx", None, "gz"),
    )
    out_specs = (P("smp", None, "gx", None, "gz"), P(), P(), P(), P())
    return jax.shard_map(shards, mesh=mesh, in_specs=in_specs, out_specs=out_specs, check_vma=False)
```

profile of v0, /device:TPU:0, one launch (start us, length us, event | category | flops | bytes accessed | tf_op | source)
XLA Modules:
  0.0 293.5 jit_solution(12234768736398439717)
XLA Ops:
  7.2 1.1 copy.113
  8.3 5.1 %collective-permute-start.9 = (bf16[1,32,1,8,128]{4,1,3,2,0:T(8,128)(2,1)S(1)}, bf16[1,32,1,8,128]{4,1,3,2,0:T(8,128)(2,1)S(1)}, u32[]{:S(2)}, u32[]{:S(2)}) collective-permute-start(bf16[1,32,1,8,128]{4,1,3,2,0:T(8,128)(2,1)S(1)} %get-tuple-element.105), channel_id=1, source_target_pairs={{2,0},{4,2},{6,4},{0,6},{3,1},{5,3},{7,5},{1,7},{10,8},{12,10},{14... | collective-permute-start | bytes 196616 | tf_op jit(solution)/shard_map/ppermute | solution.py:15
  13.4 1.1 copy.88
  14.5 3.8 %collective-permute-start.1 = (bf16[1,32,1,8,128]{4,1,3,2,0:T(8,128)(2,1)S(1)}, bf16[1,32,1,8,128]{4,1,3,2,0:T(8,128)(2,1)S(1)}, u32[]{:S(2)}, u32[]{:S(2)}) collective-permute-start(bf16[1,32,1,8,128]{4,1,3,2,0:T(8,128)(2,1)S(1)} %get-tuple-element.109), channel_id=1, source_target_pairs={{2,0},{4,2},{6,4},{0,6},{3,1},{5,3},{7,5},{1,7},{10,8},{12,10},{14... | collective-permute-start | bytes 196616 | tf_op jit(solution)/shard_map/ppermute | solution.py:15
  21.2 3.2 %collective-permute-done = bf16[1,32,1,8,128]{4,1,3,2,0:T(8,128)(2,1)S(1)} collective-permute-done((bf16[1,32,1,8,128]{4,1,3,2,0:T(8,128)(2,1)S(1)}, bf16[1,32,1,8,128]{4,1,3,2,0:T(8,128)(2,1)S(1)}, u32[]{:S(2)}, u32[]{:S(2)}) %collective-permute-start) | collective-permute-done | bytes 65568 | tf_op jit(solution)/shard_map/ppermute | solution.py:14
  24.5 1.6 collective-permute-start.10
  26.9 1.6 collective-permute-start.2
  28.9 9.1 %collective-permute-done.10 = bf16[1,32,7,8,1]{4,1,3,2,0:T(8,128)(2,1)S(1)} collective-permute-done((bf16[1,32,7,8,1]{4,1,3,2,0:T(8,128)(2,1)S(1)}, bf16[1,32,7,8,1]{4,1,3,2,0:T(8,128)(2,1)S(1)}, u32[]{:S(2)}, u32[]{:S(2)}) %collective-permute-start.10) | collective-permute-done | bytes 3616 | tf_op jit(solution)/shard_map/ppermute | solution.py:14
  38.0 9.8 %collective-permute-done.11 = bf16[1,32,7,8,1]{4,1,3,2,0:T(8,128)(2,1)S(1)} collective-permute-done((bf16[1,32,7,8,1]{4,1,3,2,0:T(8,128)(2,1)S(1)}, bf16[1,32,7,8,1]{4,1,3,2,0:T(8,128)(2,1)S(1)}, u32[]{:S(2)}, u32[]{:S(2)}) %collective-permute-start.11) | collective-permute-done | bytes 3616 | tf_op jit(solution)/shard_map/ppermute | solution.py:15
  48.5 1.5 fusion.148
  50.0 7.7 %collective-permute-done.2 = bf16[1,32,7,8,1]{4,1,3,2,0:T(8,128)(2,1)S(1)} collective-permute-done((bf16[1,32,7,8,1]{4,1,3,2,0:T(8,128)(2,1)S(1)}, bf16[1,32,7,8,1]{4,1,3,2,0:T(8,128)(2,1)S(1)}, u32[]{:S(2)}, u32[]{:S(2)}) %collective-permute-start.2) | collective-permute-done | bytes 3616 | tf_op jit(solution)/shard_map/ppermute | solution.py:14
  57.7 6.6 %collective-permute-done.3 = bf16[1,32,7,8,1]{4,1,3,2,0:T(8,128)(2,1)S(1)} collective-permute-done((bf16[1,32,7,8,1]{4,1,3,2,0:T(8,128)(2,1)S(1)}, bf16[1,32,7,8,1]{4,1,3,2,0:T(8,128)(2,1)S(1)}, u32[]{:S(2)}, u32[]{:S(2)}) %collective-permute-start.3) | collective-permute-done | bytes 3616 | tf_op jit(solution)/shard_map/ppermute | solution.py:15
  64.9 1.5 fusion.150
  67.4 1.1 pad_maximum_fusion.14
  74.6 1.0 convolution_add_fusion.1
  76.9 0.7 convolution_bitcast_fusion.5
  79.0 0.7 convolution_bitcast_fusion.1
  79.7 0.7 convolution_bitcast_fusion.7
  80.5 0.7 convolution_bitcast_fusion.8
  81.9 0.7 convolution_bitcast_fusion
  82.7 3.8 %collective-permute-start.5 = (bf16[1,32,1,8,128]{4,1,3,2,0:T(8,128)(2,1)S(1)}, bf16[1,32,1,8,128]{4,1,3,2,0:T(8,128)(2,1)S(1)}, u32[]{:S(2)}, u32[]{:S(2)}) collective-permute-start(bf16[1,32,1,8,128]{4,1,3,2,0:T(8,128)(2,1)S(1)} %get-tuple-element.108), channel_id=1, source_target_pairs={{2,0},{4,2},{6,4},{0,6},{3,1},{5,3},{7,5},{1,7},{10,8},{12,10},{14... | collective-permute-start | bytes 196616 | tf_op jit(solution)/shard_map/ppermute | solution.py:15
  86.6 2.2 collective-permute-done.4
  89.0 1.6 collective-permute-start.6
  91.1 0.8 maximum_multiply_fusion
  92.0 49.9 %all-reduce.3 = (f32[32]{0:T(128)}, f32[32]{0:T(128)}) all-reduce(f32[32]{0:T(128)S(1)} %broadcast_multiply_fusion.1, f32[32]{0:T(128)S(1)} %broadcast_multiply_fusion), channel_id=1, replica_groups=mesh['smp'=4,'gx'=4,'gz'=2] {'smp','gx','gz'}, use_global_device_ids=true, to_apply=%region_2.3 | all-reduce | flops 64 | bytes 512 | tf_op jit(solution)/shard_map/psum | solution.py:103
  146.2 1.4 fusion.149
  150.1 0.7 convolution_bitcast_fusion.12
  154.7 0.8 maximum_multiply_fusion.1
  155.9 0.9 copy.164
  156.7 127.3 %all-reduce.7.cloned.1.call-done = (f32[32,3,3,3,32]{4,0,3,2,1:T(8,128)}, f32[32,3,3,3,32]{4,0,3,2,1:T(8,128)}) async-done(((f32[32,3,3,3,32]{4,0,3,2,1:T(8,128)}, f32[32,3,3,3,32]{4,0,3,2,1:T(8,128)}), (f32[32,3,3,3,32]{4,0,3,2,1:T(8,128)}, f32[32,3,3,3,32]{4,0,3,2,1:T(8,128)})) %all-reduce.7.cloned.1.call-update) | async-done | bytes 221200 | tf_op jit(solution)/shard_map/psum | solution.py:103
  284.0 1.9 copy.328
  285.9 0.8 copy.329
  (142 shorter events, 27.4 us)
Async XLA Ops:
  7.2 11.2 %copy-start = (bf16[1,32,5,8,128]{4,3,2,1,0:T(8,128)(2,1)S(1)}, bf16[1,32,5,8,128]{4,3,2,1,0:T(8,128)(2,1)}, u32[]{:S(2)}) copy-start(bf16[1,32,5,8,128]{4,3,2,1,0:T(8,128)(2,1)} %param.11) | copy-start | bytes 983044
  7.2 11.5 %copy-start.2 = (bf16[32,3,3,3,32]{4,0,3,2,1:T(8,128)(2,1)S(1)}, bf16[32,3,3,3,32]{4,0,3,2,1:T(8,128)(2,1)}, u32[]{:S(2)}) copy-start(bf16[32,3,3,3,32]{4,0,3,2,1:T(8,128)(2,1)} %param.9) | copy-start | bytes 165892
  7.2 276.8 %all-reduce.7.cloned.1.call-start = ((), (), s32[]{:S(2)}) async-start(), calls=%async_computation | async-start | bytes 1769472 | tf_op jit(solution)/shard_map/psum | solution.py:103
  8.3 12.6 %collective-permute-start.9 = (bf16[1,32,1,8,128]{4,1,3,2,0:T(8,128)(2,1)S(1)}, bf16[1,32,1,8,128]{4,1,3,2,0:T(8,128)(2,1)S(1)}, u32[]{:S(2)}, u32[]{:S(2)}) collective-permute-start(bf16[1,32,1,8,128]{4,1,3,2,0:T(8,128)(2,1)S(1)} %get-tuple-element.105), channel_id=1, source_target_pairs={{2,0},{4,2},{6,4},{0,6},{3,1},{5,3},{7,5},{1,7},{10,8},{12,10},{14... | collective-permute-start | bytes 196616 | tf_op jit(solution)/shard_map/ppermute | solution.py:15
  13.4 5.3 %copy-start.4 = (bf16[32,3,3,3,32]{4,0,3,2,1:T(8,128)(2,1)S(1)}, bf16[32,3,3,3,32]{4,0,3,2,1:T(8,128)(2,1)}, u32[]{:S(2)}) copy-start(bf16[32,3,3,3,32]{4,0,3,2,1:T(8,128)(2,1)} %param.7) | copy-start | bytes 165892
  13.4 7.4 %collective-permute-start.8 = (bf16[1,32,1,8,128]{4,1,3,2,0:T(8,128)(2,1)S(1)}, bf16[1,32,1,8,128]{4,1,3,2,0:T(8,128)(2,1)S(1)}, u32[]{:S(2)}, u32[]{:S(2)}) collective-permute-start(bf16[1,32,1,8,128]{4,1,3,2,0:T(8,128)(2,1)S(1)} %get-tuple-element.106), channel_id=1, source_target_pairs={{0,2},{2,4},{4,6},{6,0},{1,3},{3,5},{5,7},{7,1},{8,10},{10,12},{12... | collective-permute-start | bytes 196616 | tf_op jit(solution)/shard_map/ppermute | solution.py:14
  14.5 12.1 %collective-permute-start.1 = (bf16[1,32,1,8,128]{4,1,3,2,0:T(8,128)(2,1)S(1)}, bf16[1,32,1,8,128]{4,1,3,2,0:T(8,128)(2,1)S(1)}, u32[]{:S(2)}, u32[]{:S(2)}) collective-permute-start(bf16[1,32,1,8,128]{4,1,3,2,0:T(8,128)(2,1)S(1)} %get-tuple-element.109), channel_id=1, source_target_pairs={{2,0},{4,2},{6,4},{0,6},{3,1},{5,3},{7,5},{1,7},{10,8},{12,10},{14... | collective-permute-start | bytes 196616 | tf_op jit(solution)/shard_map/ppermute | solution.py:15
  18.4 6.1 %collective-permute-start = (bf16[1,32,1,8,128]{4,1,3,2,0:T(8,128)(2,1)S(1)}, bf16[1,32,1,8,128]{4,1,3,2,0:T(8,128)(2,1)S(1)}, u32[]{:S(2)}, u32[]{:S(2)}) collective-permute-start(bf16[1,32,1,8,128]{4,1,3,2,0:T(8,128)(2,1)S(1)} %get-tuple-element.110), channel_id=1, source_target_pairs={{0,2},{2,4},{4,6},{6,0},{1,3},{3,5},{5,7},{7,1},{8,10},{10,12},{12... | collective-permute-start | bytes 196616 | tf_op jit(solution)/shard_map/ppermute | solution.py:14
  20.9 3.5 %copy-start.1 = (bf16[1,32,5,8,128]{4,3,2,1,0:T(8,128)(2,1)S(1)}, bf16[1,32,5,8,128]{4,3,2,1,0:T(8,128)(2,1)}, u32[]{:S(2)}) copy-start(bf16[1,32,5,8,128]{4,3,2,1,0:T(8,128)(2,1)} %param.6) | copy-start | bytes 983044
  24.5 13.5 %collective-permute-start.10 = (bf16[1,32,7,8,1]{4,1,3,2,0:T(8,128)(2,1)S(1)}, bf16[1,32,7,8,1]{4,1,3,2,0:T(8,128)(2,1)S(1)}, u32[]{:S(2)}, u32[]{:S(2)}) collective-permute-start(bf16[1,32,7,8,1]{4,1,3,2,0:T(8,128)(2,1)S(1)} %get-tuple-element.89), channel_id=1, source_target_pairs={{0,1},{1,0},{2,3},{3,2},{4,5},{5,4},{6,7},{7,6},{8,9},{9,8},{10,11... | collective-permute-start | bytes 10760 | tf_op jit(solution)/shard_map/ppermute | solution.py:14
  26.1 21.8 %collective-permute-start.11 = (bf16[1,32,7,8,1]{4,1,3,2,0:T(8,128)(2,1)S(1)}, bf16[1,32,7,8,1]{4,1,3,2,0:T(8,128)(2,1)S(1)}, u32[]{:S(2)}, u32[]{:S(2)}) collective-permute-start(bf16[1,32,7,8,1]{4,1,3,2,0:T(8,128)(2,1)S(1)} %get-tuple-element.90), channel_id=1, source_target_pairs={{1,0},{0,1},{3,2},{2,3},{5,4},{4,5},{7,6},{6,7},{9,8},{8,9},{11,10... | collective-permute-start | bytes 10760 | tf_op jit(solution)/shard_map/ppermute | solution.py:15
  26.9 30.9 %collective-permute-start.2 = (bf16[1,32,7,8,1]{4,1,3,2,0:T(8,128)(2,1)S(1)}, bf16[1,32,7,8,1]{4,1,3,2,0:T(8,128)(2,1)S(1)}, u32[]{:S(2)}, u32[]{:S(2)}) collective-permute-start(bf16[1,32,7,8,1]{4,1,3,2,0:T(8,128)(2,1)S(1)} %get-tuple-element.97), channel_id=1, source_target_pairs={{0,1},{1,0},{2,3},{3,2},{4,5},{5,4},{6,7},{7,6},{8,9},{9,8},{10,11... | collective-permute-start | bytes 10760 | tf_op jit(solution)/shard_map/ppermute | solution.py:14
  28.4 35.9 %collective-permute-start.3 = (bf16[1,32,7,8,1]{4,1,3,2,0:T(8,128)(2,1)S(1)}, bf16[1,32,7,8,1]{4,1,3,2,0:T(8,128)(2,1)S(1)}, u32[]{:S(2)}, u32[]{:S(2)}) collective-permute-start(bf16[1,32,7,8,1]{4,1,3,2,0:T(8,128)(2,1)S(1)} %get-tuple-element.98), channel_id=1, source_target_pairs={{1,0},{0,1},{3,2},{2,3},{5,4},{4,5},{7,6},{6,7},{9,8},{8,9},{11,10... | collective-permute-start | bytes 10760 | tf_op jit(solution)/shard_map/ppermute | solution.py:15
  70.8 0.7 copy-start.5
  82.6 6.1 %collective-permute-start.4 = (bf16[1,32,1,8,128]{4,1,3,2,0:T(8,128)(2,1)S(1)}, bf16[1,32,1,8,128]{4,1,3,2,0:T(8,128)(2,1)S(1)}, u32[]{:S(2)}, u32[]{:S(2)}) collective-permute-start(bf16[1,32,1,8,128]{4,1,3,2,0:T(8,128)(2,1)S(1)} %get-tuple-element.107), channel_id=1, source_target_pairs={{0,2},{2,4},{4,6},{6,0},{1,3},{3,5},{5,7},{7,1},{8,10},{10,12},{12... | collective-permute-start | bytes 196616 | tf_op jit(solution)/shard_map/ppermute | solution.py:14
  82.7 6.1 %collective-permute-start.5 = (bf16[1,32,1,8,128]{4,1,3,2,0:T(8,128)(2,1)S(1)}, bf16[1,32,1,8,128]{4,1,3,2,0:T(8,128)(2,1)S(1)}, u32[]{:S(2)}, u32[]{:S(2)}) collective-permute-start(bf16[1,32,1,8,128]{4,1,3,2,0:T(8,128)(2,1)S(1)} %get-tuple-element.108), channel_id=1, source_target_pairs={{2,0},{4,2},{6,4},{0,6},{3,1},{5,3},{7,5},{1,7},{10,8},{12,10},{14... | collective-permute-start | bytes 196616 | tf_op jit(solution)/shard_map/ppermute | solution.py:15
  89.0 52.8 %collective-permute-start.6 = (bf16[1,32,7,8,1]{4,1,3,2,0:T(8,128)(2,1)S(1)}, bf16[1,32,7,8,1]{4,1,3,2,0:T(8,128)(2,1)S(1)}, u32[]{:S(2)}, u32[]{:S(2)}) collective-permute-start(bf16[1,32,7,8,1]{4,1,3,2,0:T(8,128)(2,1)S(1)} %get-tuple-element.93), channel_id=1, source_target_pairs={{0,1},{1,0},{2,3},{3,2},{4,5},{5,4},{6,7},{7,6},{8,9},{9,8},{10,11... | collective-permute-start | bytes 10760 | tf_op jit(solution)/shard_map/ppermute | solution.py:14
  90.6 51.3 %collective-permute-start.7 = (bf16[1,32,7,8,1]{4,1,3,2,0:T(8,128)(2,1)S(1)}, bf16[1,32,7,8,1]{4,1,3,2,0:T(8,128)(2,1)S(1)}, u32[]{:S(2)}, u32[]{:S(2)}) collective-permute-start(bf16[1,32,7,8,1]{4,1,3,2,0:T(8,128)(2,1)S(1)} %get-tuple-element.94), channel_id=1, source_target_pairs={{1,0},{0,1},{3,2},{2,3},{5,4},{4,5},{7,6},{6,7},{9,8},{8,9},{11,10... | collective-permute-start | bytes 10760 | tf_op jit(solution)/shard_map/ppermute | solution.py:15
  154.7 0.9 copy-start.6
  284.0 1.9 copy-start.3
Sparse Core Ops, SparseCore 0:
  155.7 128.2 all-reduce.6
where the time goes:
time: 294 us; the launch traced here: 293 us
  waiting for transfers between devices  166 us (56%)
  blocking collectives  49.9 us (17%)
  matrix products  21.5 us (7%)
  starting transfers between devices  19.1 us (6%)
  between operations  14.6 us (5%)
  local copies, waits for them, and re-layouts  14 us (5%)
  other arithmetic  8.32 us (3%)
    psum x1, waiting for transfers between devices, shards(): lax.psum((first_grad, first_bgrad, second_grad, second_bgrad), ('smp', 'g...  127 us
    psum x1, blocking collectives, shards(): lax.psum((first_grad, first_bgrad, second_grad, second_bgrad), ('smp', 'g...  49.9 us
    ppermute x6, waiting for transfers between devices, extended(): before = lax.ppermute(last, axis, up)  22.2 us
    ppermute x6, waiting for transfers between devices, extended(): after = lax.ppermute(initial, axis, down)  16.5 us
    ppermute x6, starting transfers between devices, extended(): after = lax.ppermute(initial, axis, down)  14.4 us
    dot_general x18, matrix products, correlate(): jnp.einsum('soxyz,skxyz->ok', upstream, stacked, preferred_element_type=j...  12.8 us
    dot_general x27, matrix products, convolve(): jnp.einsum('ok,skxyz->soxyz', tap_block, stacked, preferred_element_type=...  8.76 us
    unnamed x23, local copies, waits for them, and re-layouts  6.27 us
  transfers between devices with their start and end apart: 13, of which 7 were waited for; matrix products, arithmetic and copies ran while one was open for 3% of the time, Pallas kernels for 0%

commit v1 on v0

v1 whole, which is shorter than its diff:
```python
import functools

import jax
import jax.numpy as jnp
from jax import lax
from jax.experimental import pallas as pl
from jax.experimental.pallas import tpu as pltpu
from jax.sharding import PartitionSpec as P

AXES = ("smp", "gx", "gz")
BF = jnp.bfloat16
F32 = jnp.float32
LANES = 128
TERMS = 896


def mm(a, b):
    return lax.dot_general(a, b, (((1,), (0,)), ((), ())), preferred_element_type=F32)


def mm_nt(a, b):
    return lax.dot_general(a, b, (((1,), (1,)), ((), ())), preferred_element_type=F32)


def iota(shape, dim):
    return lax.broadcasted_iota(jnp.int32, shape, dim)


def one_hot(hit):
    return jnp.where(hit, 1.0, 0.0).astype(BF)


def params():
    return pltpu.CompilerParams(vmem_limit_bytes=50 * 2**20)


def pack_kernel(nx, ch, ny, f_ref, g_ref, fo_ref, go_ref, up_ref, dn_ref, edge_ref, raw):
    rows = ch * ny
    r, k = iota((rows, rows), 0), iota((rows, rows), 1)
    perm = one_hot(k == (r % ch) * ny + r // ch)
    for src, dst in ((f_ref, fo_ref), (g_ref, go_ref)):
        for x in range(nx):
            block = src[0, :, x].astype(F32).reshape(rows, LANES)
            raw[:, x * LANES : (x + 1) * LANES] = block.astype(BF)
        dst[...] = mm(perm, raw[...]).astype(BF)
    last = (nx - 1) * LANES
    up_ref[0:rows] = fo_ref[:, last - LANES : last]
    up_ref[rows : 2 * rows] = fo_ref[:, last:]
    up_ref[2 * rows :] = go_ref[:, last:]
    dn_ref[0:rows] = fo_ref[:, 0:LANES]
    dn_ref[rows : 2 * rows] = fo_ref[:, LANES : 2 * LANES]
    dn_ref[2 * rows :] = go_ref[:, 0:LANES]
    n = edge_ref.shape[0]
    j, m = iota((n, nx * LANES), 0), iota((n, nx * LANES), 1)
    c, x = j // nx, j % nx
    zf = jnp.where(c < 2, c, LANES - 4 + c)
    pick_f = one_hot((c < 4) & (m == x * LANES + zf))
    zg = jnp.where(c == 4, 0, LANES - 1)
    pick_g = one_hot((c >= 4) & (c < 6) & (m == x * LANES + zg))
    edge_ref[...] = (mm_nt(pick_f, fo_ref[...]) + mm_nt(pick_g, go_ref[...])).astype(BF)


def pack(features, cotangent):
    _, ch, nx, ny, _ = features.shape
    rows = ch * ny
    edge_rows = -(-6 * nx // 32) * 32
    sds = jax.ShapeDtypeStruct
    return pl.pallas_call(
        functools.partial(pack_kernel, nx, ch, ny),
        out_shape=(
            sds((rows, nx * LANES), BF),
            sds((rows, nx * LANES), BF),
            sds((3 * rows, LANES), BF),
            sds((3 * rows, LANES), BF),
            sds((edge_rows, rows), BF),
        ),
        scratch_shapes=[pltpu.VMEM((rows, nx * LANES), BF)],
        compiler_params=params(),
        name="pack",
    )(features, cotangent)


def bands_kernel(ny, w_ref, t_ref):
    ch = w_ref.shape[2]
    rows = ny * ch
    lane = iota((ch, rows), 1)
    for kind in range(w_ref.shape[0]):
        for tap in range(9):
            a, c = tap // 3, tap % 3
            wide = jnp.concatenate([w_ref[kind, tap], jnp.zeros((ch, rows - LANES), F32)], axis=1)
            for y in range(ny):
                block = wide if y == 1 else pltpu.roll(wide, (ch * (y - 1)) % rows, 1)
                if y == 0:
                    block = jnp.where(lane >= rows - ch, 0.0, block)
                if y == ny - 1:
                    block = jnp.where(lane < ch, 0.0, block)
                t_ref[kind, a, y * ch : (y + 1) * ch, c * rows : (c + 1) * rows] = block.astype(BF)


def bands(first_weight, second_weight, ny):
    ch = first_weight.shape[0]
    rows = ch * ny
    flipped = jnp.transpose(jnp.flip(second_weight, (1, 2, 3)), (4, 1, 2, 3, 0))
    stacked = jnp.stack([first_weight, flipped, second_weight])
    laid = jnp.transpose(stacked, (0, 2, 4, 1, 3, 5)).reshape(3, 9, ch, 3 * ch).astype(F32)
    laid = jnp.pad(laid, ((0, 0), (0, 0), (0, 0), (0, LANES - 3 * ch)))
    return pl.pallas_call(
        functools.partial(bands_kernel, ny),
        out_shape=jax.ShapeDtypeStruct((3, 3, rows, 3 * rows), BF),
        compiler_params=params(),
        cost_estimate=pl.CostEstimate(flops=2_000_000_000, bytes_accessed=4_000_000, transcendentals=0),
        name="bands",
    )(laid)


def shifted_rows(out, row, block, before, after, rows):
    lane = iota(block.shape, 1)
    at = slice(row * LANES, (row + 1) * LANES)
    wide = block.astype(F32)
    out[0:rows, at] = jnp.where(lane == 0, before, pltpu.roll(wide, 1, 1)).astype(BF)
    out[rows : 2 * rows, at] = block
    out[2 * rows :, at] = jnp.where(lane == LANES - 1, after, pltpu.roll(wide, LANES - 1, 1)).astype(BF)


def lane_to(edges, source, target):
    shift = (target - source) % LANES
    return edges if shift == 0 else pltpu.roll(edges, shift, 1)


def fold_taps(product, ch, ny):
    rows = ch * ny
    lane = iota((ch, rows), 1)
    total = None
    for y in range(ny):
        block = product[y * ch : (y + 1) * ch]
        if y == 0:
            block = jnp.where(lane >= rows - ch, 0.0, block)
        if y == ny - 1:
            block = jnp.where(lane < ch, 0.0, block)
        if y != 1:
            block = pltpu.roll(block, (ch * (1 - y)) % rows, 1)
        total = block if total is None else total + block
    return total[:, :LANES]


def place_taps(columns, folded, a, c, ch):
    lane = iota(folded.shape, 1)
    for b in range(3):
        target = ch * ((a * 3 + b) * 3 + c)
        col, offset = target // LANES, target % LANES
        moved = lane_to(folded, b * ch, offset)
        columns[col] = jnp.where((lane >= offset) & (lane < offset + ch), moved, columns[col])


def bias_terms(field, ch, ny):
    nx = field.shape[1] // LANES
    wide = field.astype(F32)
    total = wide[:, 0:LANES]
    for x in range(1, nx):
        total = total + wide[:, x * LANES : (x + 1) * LANES]
    folded = total[0:ch]
    for y in range(1, ny):
        folded = folded + total[y * ch : (y + 1) * ch]
    return jnp.sum(folded, axis=1, keepdims=True)


def main_kernel(
    nx, ch, ny, right, scale,
    t_ref, f_ref, g_ref, above_ref, below_ref, edge_ref, bias_ref,
    hid_ref, hid_edge_ref, second_ref, first_ref,
    fs, gs, es, pre,
):
    rows = ch * ny
    per = edge_ref.shape[0] // (6 if right else 3)
    n_src = edge_ref.shape[0]
    j, k = iota((LANES, n_src), 0), iota((LANES, n_src), 1)
    s, xx = j // 16, j % 16
    column = jnp.where(s == 0, 2, jnp.where(s == 1, 3, jnp.where(s == 5, 0, jnp.where(s == 6, 1, jnp.where(s == 3, 5, jnp.where(s == 7, 4, -1))))))
    base = jnp.where(s >= 4, right, 0)
    row = jnp.where(xx < 2, per + nx - 2 + xx, jnp.where(xx < nx + 2, xx - 2, 2 * per + xx - nx - 2))
    place = one_hot((column >= 0) & (xx < nx + 4) & (k == base + column * nx + row))
    edges_t = mm(place, edge_ref[...])
    field = jnp.concatenate([above_ref[0:rows], above_ref[rows : 2 * rows], f_ref[...], below_ref[0:rows], below_ref[rows : 2 * rows]], axis=1)
    wide_n = (nx + 4) * LANES
    j, k = iota((LANES, wide_n), 0), iota((LANES, wide_n), 1)
    s, xx = j // 16, j % 16
    target = jnp.where(s == 2, xx * LANES, jnp.where(s == 4, xx * LANES + LANES - 1, -1))
    own = one_hot((xx < nx + 4) & (k == target))
    edges = (edges_t + mm_nt(own, field)).T

    for x in range(nx + 4):
        block = field[:, x * LANES : (x + 1) * LANES]
        shifted_rows(fs, x, block, lane_to(edges, 16 + x, 0), lane_to(edges, 80 + x, LANES - 1), rows)
    for x in range(nx + 2):
        if x == 0:
            block = above_ref[2 * rows :]
        elif x == nx + 1:
            block = below_ref[2 * rows :]
        else:
            block = g_ref[:, (x - 1) * LANES : x * LANES]
        shifted_rows(gs, x, block, lane_to(edges, 48 + x + 1, 0), lane_to(edges, 112 + x + 1, LANES - 1), rows)
    for a in range(3):
        for c in range(3):
            es[a, c * rows : (c + 1) * rows] = lane_to(edges, 16 * c + a, 0).astype(BF)

    bias = bias_ref[...]
    n7 = (nx + 2) * LANES
    acc = mm(t_ref[0, 0], fs[:, 0:n7])
    for a in range(1, 3):
        acc = acc + mm(t_ref[0, a], fs[:, a * LANES : a * LANES + n7])
    preact = acc + bias
    pre[...] = preact
    hid_ref[...] = (preact / (1.0 + jnp.exp(-preact))).astype(BF)
    acc = mm(t_ref[0, 0], es[0])
    for a in range(1, 3):
        acc = acc + mm(t_ref[0, a], es[a])
    preact = acc + bias
    hid_edge_ref[...] = (preact / (1.0 + jnp.exp(-preact))).astype(BF)

    n5 = nx * LANES
    hidden = hid_ref[:, LANES : LANES + n5]
    columns = [jnp.zeros((ch, LANES), F32) for _ in range(TERMS // LANES)]
    for a in range(3):
        for c in range(3):
            left = gs[(2 - c) * rows : (3 - c) * rows, (2 - a) * LANES : (2 - a) * LANES + n5]
            place_taps(columns, fold_taps(mm_nt(left, hidden), ch, ny), a, c, ch)
    lane = iota((ch, LANES), 1)
    spare = 27 * ch % LANES
    columns[-1] = jnp.where(lane == spare, bias_terms(g_ref[...], ch, ny), columns[-1])
    for i, part in enumerate(columns):
        second_ref[:, i * LANES : (i + 1) * LANES] = part * scale

    acc = mm(t_ref[1, 0], gs[:, 0:n5])
    for a in range(1, 3):
        acc = acc + mm(t_ref[1, a], gs[:, a * LANES : a * LANES + n5])
    preact = pre[:, LANES : LANES + n5]
    logistic = 1.0 / (1.0 + jnp.exp(-preact))
    preact_grad = (acc * logistic * (1.0 + preact * (1.0 - logistic))).astype(BF)

    columns = [jnp.zeros((ch, LANES), F32) for _ in range(TERMS // LANES)]
    for a in range(3):
        for c in range(3):
            taps = fs[c * rows : (c + 1) * rows, (a + 1) * LANES : (a + 1) * LANES + n5]
            place_taps(columns, fold_taps(mm_nt(preact_grad, taps), ch, ny), a, c, ch)
    columns[-1] = jnp.where(lane == spare, bias_terms(preact_grad, ch, ny), columns[-1])
    for i, part in enumerate(columns):
        first_ref[:, i * LANES : (i + 1) * LANES] = part * scale


def main(taps, field, cot, above, below, edge, right, bias, ch, ny, scale):
    rows = ch * ny
    nx = field.shape[1] // LANES
    sds = jax.ShapeDtypeStruct
    return pl.pallas_call(
        functools.partial(main_kernel, nx, ch, ny, right, scale),
        out_shape=(
            sds((rows, (nx + 2) * LANES), BF),
            sds((rows, LANES), BF),
            sds((ch, TERMS), F32),
            sds((ch, TERMS), F32),
        ),
        scratch_shapes=[
            pltpu.VMEM((3 * rows, (nx + 4) * LANES), BF),
            pltpu.VMEM((3 * rows, (nx + 2) * LANES), BF),
            pltpu.VMEM((3, 3 * rows, LANES), BF),
            pltpu.VMEM((rows, (nx + 2) * LANES), F32),
        ],
        compiler_params=params(),
        name="main",
    )(taps, field, cot, above, below, edge, bias)


def output_kernel(nx, ch, ny, t_ref, h_ref, e_ref, f_ref, bias_ref, o_ref, hs):
    rows = ch * ny
    edges = e_ref[...].astype(F32)
    for x in range(nx + 2):
        block = h_ref[:, x * LANES : (x + 1) * LANES]
        shifted_rows(hs, x, block, lane_to(edges, x, 0), lane_to(edges, 64 + x, LANES - 1), rows)
    n5 = nx * LANES
    acc = mm(t_ref[2, 0], hs[:, 0:n5])
    for a in range(1, 3):
        acc = acc + mm(t_ref[2, a], hs[:, a * LANES : a * LANES + n5])
    total = (f_ref[...].astype(F32) + (acc + bias_ref[...])).astype(BF)
    r, k = iota((rows, rows), 0), iota((rows, rows), 1)
    back = one_hot(k == (r % ny) * ch + r // ny)
    ordered = mm(back, total)
    for x in range(nx):
        o_ref[0, :, x] = ordered[:, x * LANES : (x + 1) * LANES].reshape(ch, ny, LANES).astype(BF)


def residual(taps, hidden, hidden_edge, field, bias, ch, ny):
    rows = ch * ny
    nx = field.shape[1] // LANES
    return pl.pallas_call(
        functools.partial(output_kernel, nx, ch, ny),
        out_shape=jax.ShapeDtypeStruct((1, ch, nx, ny, LANES), BF),
        scratch_shapes=[pltpu.VMEM((3 * rows, (nx + 2) * LANES), BF)],
        compiler_params=params(),
        cost_estimate=pl.CostEstimate(flops=3_000_000_000, bytes_accessed=3_000_000, transcendentals=0),
        name="residual",
    )(taps, hidden, hidden_edge, field, bias)


def moved(array, sizes, step):
    ns, nx, nz = sizes
    pairs = []
    for s in range(ns):
        for x in range(nx):
            for z in range(nz):
                t, u, v = step(s, x, z)
                pairs.append(((s * nx + x) * nz + z, (t * nx + u) * nz + v))
    return lax.ppermute(array, AXES, pairs)


def around(array, sizes, dx, dz):
    ns, nx, nz = sizes
    return moved(array, sizes, lambda s, x, z: (s, (x + dx) % nx, (z + dz) % nz))


def swapped(array, sizes, bits):
    return moved(array, sizes, lambda s, x, z: (s ^ bits[0], x ^ bits[1], z ^ bits[2]))


def pair_sums(terms):
    while len(terms) > 1:
        terms = [terms[i] + terms[i + 1] for i in range(0, len(terms), 2)]
    return terms[0]


def sum_over(array, sizes, pair):
    steps = [(0, 0, 0)]
    for bits in pair:
        steps = steps + [tuple(p ^ q for p, q in zip(bits, step)) for step in steps]
    sent = array.astype(BF)
    terms = [sent] + [swapped(sent, sizes, step) for step in steps[1:]]
    return pair_sums([term.astype(F32) for term in terms])


def sum_all(second, first, sizes):
    if any(n & (n - 1) for n in sizes) or sizes[0] == 1:
        return lax.psum((second, first), AXES)
    even = lax.axis_index("smp") % 2 == 0
    near = (1, 0, 0)
    mine = jnp.where(even, second, first) + swapped(jnp.where(even, first, second), sizes, near)
    bits = [(1 << i, 0, 0) for i in range(1, sizes[0].bit_length() - 1)]
    bits += [(0, 0, 1 << i) for i in range(sizes[2].bit_length() - 1)]
    bits += [(0, 1 << i, 0) for i in range(sizes[1].bit_length() - 1)]
    for i in range(0, len(bits), 2):
        mine = sum_over(mine, sizes, bits[i : i + 2])
    other = swapped(mine, sizes, near)
    return jnp.where(even, mine, other), jnp.where(even, other, mine)


def shards(sizes, features, first_weight, first_bias, second_weight, second_bias, cotangent):
    ns, ngx, ngz = sizes
    _, ch, nx, ny, nz = features.shape
    assert features.shape[0] == 1 and nz == LANES
    scale = float((ns * nx * ngx * ny * nz * ngz) ** -0.5)
    field, cot, up, down, edge = pack(features, cotangent)
    above = around(up, sizes, 1, 0)
    below = around(down, sizes, -1, 0)
    sides = [[around(edge, sizes, dx, 1) for dx in (0, 1, -1)]]
    if ngz != 2:
        sides.append([around(edge, sizes, dx, -1) for dx in (0, 1, -1)])
    taps = bands(first_weight, second_weight, ny)
    edges = jnp.concatenate([part for side in sides for part in side], axis=0)
    right = edges.shape[0] // 2 if ngz != 2 else 0
    column = lambda bias: jnp.tile(bias, ny)[:, None]
    hidden, hidden_edge, second, first = main(
        taps, field, cot, above, below, edges, right, column(first_bias), ch, ny, scale
    )
    output = residual(taps, hidden, hidden_edge, field, column(second_bias), ch, ny)
    second, first = sum_all(second, first, sizes)
    spread = lambda terms: (terms[:, : 27 * ch].reshape(ch, 3, 3, 3, ch), terms[:, 27 * ch])
    first_grad, first_bgrad = spread(first)
    second_grad, second_bgrad = spread(second)
    return output, first_grad, first_bgrad, second_grad, second_bgrad


def solution(mesh):
    sizes = tuple(mesh.shape[axis] for axis in AXES)
    split = P("smp", None, "gx", None, "gz")
    return jax.shard_map(
        functools.partial(shards, sizes),
        mesh=mesh,
        in_specs=(split, P(), P(), P(), P(), split),
        out_specs=(split, P(), P(), P(), P()),
        check_vma=False,
    )
```

time: 294 us -> 54 us (0.18)
  waiting for transfers between devices: 166 us -> 10.2 us
  blocking collectives: 49.9 us -> 0 us
  matrix products: 21.5 us -> 0 us
  between operations: 14.6 us -> 0.83 us
  Pallas kernels: 0 us -> 13 us
  other arithmetic: 8.32 us -> 1.38 us
  local copies, waits for them, and re-layouts: 14 us -> 8.8 us
    psum x1 -> x0, waiting for transfers between devices: 127 us -> none  [shards(): lax.psum((first_grad, first_bgrad, second_grad, second_bgrad), ('smp', 'g...]
    psum x1 -> x0, blocking collectives: 49.9 us -> none  [shards(): lax.psum((first_grad, first_bgrad, second_grad, second_bgrad), ('smp', 'g...]
    ppermute x12 -> x13, waiting for transfers between devices: 38.7 us -> 10.2 us  [moved(): return lax.ppermute(array, AXES, pairs)]
    dot_general x45 -> x0, matrix products: 21.5 us -> none  [the longest x18 12.8 us: correlate(): jnp.einsum('soxyz,skxyz->ok', upstream, stacked, preferred_element_type=j...]
    pallas_call x0 -> x4, Pallas kernels: none -> 13 us  [the longest x1 7.46 us: main(): pl.pallas_call(functools.partial(main_kernel, nx, ch, ny, right, scale),...]
    concatenate x15 -> x1, other arithmetic: 6.25 us -> 0.01 us  [shards(): edges = jnp.concatenate([part for side in sides for part in side], axis=0)]
    slice x31 -> x1, local copies, waits for them, and re-layouts: 6.08 us -> 0.7 us  [shards(): terms[:, 27 * ch]]
    ppermute x12 -> x13, starting transfers between devices: 19.1 us -> 19.5 us  [moved(): return lax.ppermute(array, AXES, pairs)]
  transfers between devices with their start and end apart: 13 -> 13, of which waited for: 7 -> 8; matrix products, arithmetic and copies ran while one was open for 3% -> 6% of each run, Pallas kernels for 0% -> 9%
where the time goes in v1:
time: 54 us; the launch traced here: 53.7 us
  starting transfers between devices  19.5 us (36%)
  Pallas kernels  13 us (24%)
  waiting for transfers between devices  10.2 us (19%)
  local copies, waits for them, and re-layouts  8.8 us (16%)
  other arithmetic  1.38 us (3%)
  between operations  0.83 us (2%)
    ppermute x13, starting transfers between devices, moved(): return lax.ppermute(array, AXES, pairs)  19.5 us
    ppermute x13, waiting for transfers between devices, moved(): return lax.ppermute(array, AXES, pairs)  10.2 us
    pallas_call x1, Pallas kernels, main(): pl.pallas_call(functools.partial(main_kernel, nx, ch, ny, right, scale),...  7.46 us
    unnamed x13, local copies, waits for them, and re-layouts  6.4 us
    pallas_call x1, Pallas kernels, residual(): pl.pallas_call(functools.partial(output_kernel, nx, ch, ny), out_shape=ja...  4.32 us
    convert_element_type x1, other arithmetic, bands(): jnp.transpose(stacked, (0, 2, 4, 1, 3, 5)).reshape(3, 9, ch, 3 * ch)  1.21 us
  transfers between devices with their start and end apart: 13, of which 8 were waited for; matrix products, arithmetic and copies ran while one was open for 6% of the time, Pallas kernels for 9%

profile of v1, /device:TPU:0, one launch (start us, length us, event | category | flops | bytes accessed | tf_op | source)
XLA Modules:
  0.0 53.7 jit_solution(1038954506776851296)
XLA Ops:
  0.6 1.0 %copy-done.1 = bf16[1,32,5,8,128]{4,3,2,1,0:T(8,128)(2,1)S(1)} copy-done((bf16[1,32,5,8,128]{4,3,2,1,0:T(8,128)(2,1)S(1)}, bf16[1,32,5,8,128]{4,3,2,1,0:T(8,128)(2,1)}, u32[]{:S(2)}) %copy-start.1) | copy-done | bytes 327704
  1.6 1.0 %copy-done.2 = bf16[1,32,5,8,128]{4,3,2,1,0:T(8,128)(2,1)S(1)} copy-done((bf16[1,32,5,8,128]{4,3,2,1,0:T(8,128)(2,1)S(1)}, bf16[1,32,5,8,128]{4,3,2,1,0:T(8,128)(2,1)}, u32[]{:S(2)}) %copy-start.2) | copy-done | bytes 327704
  2.6 0.9 %pack.1 = (bf16[256,640]{1,0:T(8,128)(2,1)S(1)}, bf16[256,640]{1,0:T(8,128)(2,1)S(1)}, bf16[768,128]{1,0:T(8,128)(2,1)S(1)}, bf16[768,128]{1,0:T(8,128)(2,1)S(1)}, bf16[32,256]{1,0:T(8,128)(2,1)S(1)}) custom-call(bf16[1,32,5,8,128]{4,3,2,1,0:T(8,128)(2,1)S(1)} %copy-done.1, bf16[1,32,5,8,128]{4,3,2,1,0:T(8,128)(2,1)S(1)} %copy-done.2), custom_call_target="tpu_custom_call" | custom-call | tf_op jit(solution)/shard_map/pack/pallas_call | solution.py:68
  3.5 6.0 %collective-permute-start.4 = (bf16[32,256]{1,0:T(8,128)(2,1)S(1)}, bf16[32,256]{1,0:T(8,128)(2,1)S(1)}, u32[]{:S(2)}, u32[]{:S(2)}) collective-permute-start(bf16[32,256]{1,0:T(8,128)(2,1)S(1)} %get-tuple-element.18), channel_id=1, source_target_pairs={{0,7},{1,6},{2,1},{3,0},{4,3},{5,2},{6,5},{7,4},{8,15},{9,14},{10,... | collective-permute-start | bytes 49160 | tf_op jit(solution)/shard_map/ppermute | solution.py:312
  9.5 0.5 collective-permute-start.2
  10.0 0.9 %collective-permute-start = (bf16[768,128]{1,0:T(8,128)(2,1)S(1)}, bf16[768,128]{1,0:T(8,128)(2,1)S(1)}, u32[]{:S(2)}, u32[]{:S(2)}) collective-permute-start(bf16[768,128]{1,0:T(8,128)(2,1)S(1)} %get-tuple-element.16), channel_id=1, source_target_pairs={{0,2},{1,3},{2,4},{3,5},{4,6},{5,7},{6,0},{7,1},{8,10},{9,11},{10,... | collective-permute-start | bytes 589832 | tf_op jit(solution)/shard_map/ppermute | solution.py:312
  11.0 3.8 %collective-permute-start.1 = (bf16[768,128]{1,0:T(8,128)(2,1)S(1)}, bf16[768,128]{1,0:T(8,128)(2,1)S(1)}, u32[]{:S(2)}, u32[]{:S(2)}) collective-permute-start(bf16[768,128]{1,0:T(8,128)(2,1)S(1)} %get-tuple-element.17), channel_id=1, source_target_pairs={{0,6},{1,7},{2,0},{3,1},{4,2},{5,3},{6,4},{7,5},{8,14},{9,15},{10,... | collective-permute-start | bytes 589832 | tf_op jit(solution)/shard_map/ppermute | solution.py:312
  14.8 1.1 %copy.15 = bf16[32,3,3,3,32]{0,4,3,2,1:T(8,128)(2,1)S(1)} copy(bf16[32,3,3,3,32]{4,0,3,2,1:T(8,128)(2,1)} %param.9) | data formatting | bytes 110592 | tf_op args[3]
  15.9 1.2 %maximum_bitcast_fusion = bf16[3,3,3,32,3,32]{5,3,2,4,1,0:T(8,128)(2,1)S(1)} fusion(bf16[1,32,3,3,3,32]{5,1,4,3,2,0:T(8,128)(2,1)} %bitcast.10, bf16[1,32,3,3,3,32]{5,1,4,3,2,0:T(8,128)(2,1)S(1)} %reverse_bitcast_fusion, bf16[1,32,3,3,3,32]{5,1,4,3,2,0:T(8,128)(2,1)} %bitcast.13), kind=kLoop, calls=%fused_computation | loop fusion | flops 165888 | bytes 331776 | tf_op jit(solution)/shard_map/convert_element_type | solution.py:105
  17.1 0.5 copy.16
  17.6 0.4 convert_element_type.40
  18.0 0.3 bands.1.t_ref
  18.4 1.7 %copy-done = bf16[3,3,256,768]{3,2,1,0:T(8,128)(2,1)} copy-done((bf16[3,3,256,768]{3,2,1,0:T(8,128)(2,1)}, bf16[3,3,256,768]{3,2,1,0:T(8,128)(2,1)S(1)}, u32[]{:S(2)}) %copy-start) | copy-done | bytes 3538968
  20.3 0.3 collective-permute-done.above_ref
  20.7 0.4 collective-permute-done.1.below_ref
  21.1 7.5 %main.1 = (bf16[256,896]{1,0:T(8,128)(2,1)S(1)}, bf16[256,128]{1,0:T(8,128)(2,1)S(1)}, f32[32,896]{1,0:T(8,128)S(1)}, f32[32,896]{1,0:T(8,128)S(1)}) custom-call(bf16[3,3,256,768]{3,2,1,0:T(8,128)(2,1)} %copy-done, bf16[256,640]{1,0:T(8,128)(2,1)S(1)} %get-tuple-element.14.f_ref, bf16[256,640]{1,0:T(8,128)(2,1)S(1)} %get-tuple-element.15.g_ref, ...), custom_call_target="tpu_custom_call" | custom-call | tf_op jit(solution)/shard_map/main/pallas_call | solution.py:254
  28.6 1.3 %collective-permute-done.5 = f32[32,896]{1,0:T(8,128)S(1)} collective-permute-done((f32[32,896]{1,0:T(8,128)S(1)}, f32[32,896]{1,0:T(8,128)S(1)}, u32[]{:S(2)}, u32[]{:S(2)}) %collective-permute-start.5) | collective-permute-done | bytes 114720 | tf_op jit(solution)/shard_map/ppermute | solution.py:312
  29.9 2.2 %collective-permute-start.8 = (bf16[32,896]{1,0:T(8,128)(2,1)S(1)}, bf16[32,896]{1,0:T(8,128)(2,1)S(1)}, u32[]{:S(2)}, u32[]{:S(2)}) collective-permute-start(bf16[32,896]{1,0:T(8,128)(2,1)S(1)} %add_convert_fusion.1), channel_id=1, source_target_pairs={{0,17},{1,16},{2,19},{3,18},{4,21},{5,20},{6,23},{7,22},{8,25},{9,... | collective-permute-start | bytes 172040 | tf_op jit(solution)/shard_map/ppermute | solution.py:312
  32.1 0.9 %collective-permute-start.7 = (bf16[32,896]{1,0:T(8,128)(2,1)S(1)}, bf16[32,896]{1,0:T(8,128)(2,1)S(1)}, u32[]{:S(2)}, u32[]{:S(2)}) collective-permute-start(bf16[32,896]{1,0:T(8,128)(2,1)S(1)} %add_convert_fusion.1), channel_id=1, source_target_pairs={{0,1},{1,0},{2,3},{3,2},{4,5},{5,4},{6,7},{7,6},{8,9},{9,8},{10,11... | collective-permute-start | bytes 172040 | tf_op jit(solution)/shard_map/ppermute | solution.py:312
  33.0 0.5 collective-permute-start.6
  33.5 2.2 %collective-permute-done.8 = bf16[32,896]{1,0:T(8,128)(2,1)S(1)} collective-permute-done((bf16[32,896]{1,0:T(8,128)(2,1)S(1)}, bf16[32,896]{1,0:T(8,128)(2,1)S(1)}, u32[]{:S(2)}, u32[]{:S(2)}) %collective-permute-start.8) | collective-permute-done | bytes 57376 | tf_op jit(solution)/shard_map/ppermute | solution.py:312
  35.7 0.7 %collective-permute-done.7 = bf16[32,896]{1,0:T(8,128)(2,1)S(1)} collective-permute-done((bf16[32,896]{1,0:T(8,128)(2,1)S(1)}, bf16[32,896]{1,0:T(8,128)(2,1)S(1)}, u32[]{:S(2)}, u32[]{:S(2)}) %collective-permute-start.7) | collective-permute-done | bytes 57376 | tf_op jit(solution)/shard_map/ppermute | solution.py:312
  36.4 0.8 %collective-permute-done.6 = bf16[32,896]{1,0:T(8,128)(2,1)S(1)} collective-permute-done((bf16[32,896]{1,0:T(8,128)(2,1)S(1)}, bf16[32,896]{1,0:T(8,128)(2,1)S(1)}, u32[]{:S(2)}, u32[]{:S(2)}) %collective-permute-start.6) | collective-permute-done | bytes 57376 | tf_op jit(solution)/shard_map/ppermute | solution.py:312
  37.2 3.8 %collective-permute-start.11 = (bf16[32,896]{1,0:T(8,128)(2,1)S(1)}, bf16[32,896]{1,0:T(8,128)(2,1)S(1)}, u32[]{:S(2)}, u32[]{:S(2)}) collective-permute-start(bf16[32,896]{1,0:T(8,128)(2,1)S(1)} %add_convert_fusion), channel_id=1, source_target_pairs={{0,6},{1,7},{2,4},{3,5},{4,2},{5,3},{6,0},{7,1},{8,14},{9,15},{10,... | collective-permute-start | bytes 172040 | tf_op jit(solution)/shard_map/ppermute | solution.py:312
  41.0 0.5 collective-permute-start.10
  41.8 1.7 %collective-permute-done.11 = bf16[32,896]{1,0:T(8,128)(2,1)S(1)} collective-permute-done((bf16[32,896]{1,0:T(8,128)(2,1)S(1)}, bf16[32,896]{1,0:T(8,128)(2,1)S(1)}, u32[]{:S(2)}, u32[]{:S(2)}) %collective-permute-start.11) | collective-permute-done | bytes 57376 | tf_op jit(solution)/shard_map/ppermute | solution.py:312
  43.6 2.7 %collective-permute-done.10 = bf16[32,896]{1,0:T(8,128)(2,1)S(1)} collective-permute-done((bf16[32,896]{1,0:T(8,128)(2,1)S(1)}, bf16[32,896]{1,0:T(8,128)(2,1)S(1)}, u32[]{:S(2)}, u32[]{:S(2)}) %collective-permute-start.10) | collective-permute-done | bytes 57376 | tf_op jit(solution)/shard_map/ppermute | solution.py:312
  46.4 4.3 %residual.1 = bf16[1,32,5,8,128]{4,3,2,1,0:T(8,128)(2,1)} custom-call(bf16[3,3,256,768]{3,2,1,0:T(8,128)(2,1)} %copy-done, bf16[256,896]{1,0:T(8,128)(2,1)S(1)} %get-tuple-element.19.h_ref, bf16[256,128]{1,0:T(8,128)(2,1)S(1)} %get-tuple-element.20.e_ref, bf16[256,640]{1,0:T(8,128)(2,1)S(1)} %get-tuple-element.14.f_ref, ...), custom_call_target="tpu_custom_call" | custom-call | flops 3000000000 | bytes 3000000 | tf_op jit(solution)/shard_map/residual/pallas_call | solution.py:294
  50.8 0.3 reshape.21
  51.1 0.8 %copy.19 = f32[32,3,3,3,32]{4,0,3,2,1:T(8,128)} copy(f32[32,3,3,3,32]{4,3,2,1,0:T(4,128)S(1)} %reshape.21) | data formatting | bytes 221184
  51.9 0.7 %slice_reduce_fusion = (f32[32]{0:T(128)}, f32[32]{0:T(128)}) fusion(f32[32,896]{1,0:T(8,128)S(1)} %get-tuple-element.33, f32[32,896]{1,0:T(8,128)S(1)} %get-tuple-element.34), kind=kLoop, calls=%fused_computation.10 | loop fusion | bytes 512 | tf_op jit(solution)/shard_map/slice | solution.py:374
  52.9 0.8 %copy.20 = f32[32,3,3,3,32]{4,0,3,2,1:T(8,128)} copy(f32[32,3,3,3,32]{4,3,2,1,0:T(4,128)S(1)} %reshape.22) | data formatting | bytes 221184
  (29 shorter events, 1.1 us)
Async XLA Ops:
  0.6 1.0 %copy-start.1 = (bf16[1,32,5,8,128]{4,3,2,1,0:T(8,128)(2,1)S(1)}, bf16[1,32,5,8,128]{4,3,2,1,0:T(8,128)(2,1)}, u32[]{:S(2)}) copy-start(bf16[1,32,5,8,128]{4,3,2,1,0:T(8,128)(2,1)} %f_ref.1) | copy-start | bytes 983044
  1.6 1.0 %copy-start.2 = (bf16[1,32,5,8,128]{4,3,2,1,0:T(8,128)(2,1)S(1)}, bf16[1,32,5,8,128]{4,3,2,1,0:T(8,128)(2,1)}, u32[]{:S(2)}) copy-start(bf16[1,32,5,8,128]{4,3,2,1,0:T(8,128)(2,1)} %g_ref.1) | copy-start | bytes 983044
  3.5 16.8 %collective-permute-start.4 = (bf16[32,256]{1,0:T(8,128)(2,1)S(1)}, bf16[32,256]{1,0:T(8,128)(2,1)S(1)}, u32[]{:S(2)}, u32[]{:S(2)}) collective-permute-start(bf16[32,256]{1,0:T(8,128)(2,1)S(1)} %get-tuple-element.18), channel_id=1, source_target_pairs={{0,7},{1,6},{2,1},{3,0},{4,3},{5,2},{6,5},{7,4},{8,15},{9,14},{10,... | collective-permute-start | bytes 49160 | tf_op jit(solution)/shard_map/ppermute | solution.py:312
  9.5 10.8 %collective-permute-start.3 = (bf16[32,256]{1,0:T(8,128)(2,1)S(1)}, bf16[32,256]{1,0:T(8,128)(2,1)S(1)}, u32[]{:S(2)}, u32[]{:S(2)}) collective-permute-start(bf16[32,256]{1,0:T(8,128)(2,1)S(1)} %get-tuple-element.18), channel_id=1, source_target_pairs={{0,3},{1,2},{2,5},{3,4},{4,7},{5,6},{6,1},{7,0},{8,11},{9,10},{10,... | collective-permute-start | bytes 49160 | tf_op jit(solution)/shard_map/ppermute | solution.py:312
  9.5 10.8 %collective-permute-start.2 = (bf16[32,256]{1,0:T(8,128)(2,1)S(1)}, bf16[32,256]{1,0:T(8,128)(2,1)S(1)}, u32[]{:S(2)}, u32[]{:S(2)}) collective-permute-start(bf16[32,256]{1,0:T(8,128)(2,1)S(1)} %get-tuple-element.18), channel_id=1, source_target_pairs={{0,1},{1,0},{2,3},{3,2},{4,5},{5,4},{6,7},{7,6},{8,9},{9,8},{10,11... | collective-permute-start | bytes 49160 | tf_op jit(solution)/shard_map/ppermute | solution.py:312
  10.0 10.6 %collective-permute-start = (bf16[768,128]{1,0:T(8,128)(2,1)S(1)}, bf16[768,128]{1,0:T(8,128)(2,1)S(1)}, u32[]{:S(2)}, u32[]{:S(2)}) collective-permute-start(bf16[768,128]{1,0:T(8,128)(2,1)S(1)} %get-tuple-element.16), channel_id=1, source_target_pairs={{0,2},{1,3},{2,4},{3,5},{4,6},{5,7},{6,0},{7,1},{8,10},{9,11},{10,... | collective-permute-start | bytes 589832 | tf_op jit(solution)/shard_map/ppermute | solution.py:312
  11.0 10.1 %collective-permute-start.1 = (bf16[768,128]{1,0:T(8,128)(2,1)S(1)}, bf16[768,128]{1,0:T(8,128)(2,1)S(1)}, u32[]{:S(2)}, u32[]{:S(2)}) collective-permute-start(bf16[768,128]{1,0:T(8,128)(2,1)S(1)} %get-tuple-element.17), channel_id=1, source_target_pairs={{0,6},{1,7},{2,0},{3,1},{4,2},{5,3},{6,4},{7,5},{8,14},{9,15},{10,... | collective-permute-start | bytes 589832 | tf_op jit(solution)/shard_map/ppermute | solution.py:312
  18.0 2.1 %copy-start.3 = (f32[32]{0:T(128)S(1)}, f32[32]{0:T(128)}, u32[]{:S(2)}) copy-start(f32[32]{0:T(128)} %param.8) | copy-start | bytes 388
  18.4 1.7 %copy-start = (bf16[3,3,256,768]{3,2,1,0:T(8,128)(2,1)}, bf16[3,3,256,768]{3,2,1,0:T(8,128)(2,1)S(1)}, u32[]{:S(2)}) copy-start(bf16[3,3,256,768]{3,2,1,0:T(8,128)(2,1)S(1)} %bands.1.t_ref) | copy-start | bytes 10616836
  20.1 21.6 %copy-start.4 = (f32[32]{0:T(128)S(1)}, f32[32]{0:T(128)}, u32[]{:S(2)}) copy-start(f32[32]{0:T(128)} %param.10) | copy-start | bytes 388
  28.5 1.4 %collective-permute-start.5 = (f32[32,896]{1,0:T(8,128)S(1)}, f32[32,896]{1,0:T(8,128)S(1)}, u32[]{:S(2)}, u32[]{:S(2)}) collective-permute-start(f32[32,896]{1,0:T(8,128)S(1)} %broadcast_select_fusion.2), channel_id=1, source_target_pairs={{0,8},{1,9},{2,10},{3,11},{4,12},{5,13},{6,14},{7,15},{8,0},{9,1},... | collective-permute-start | bytes 344072 | tf_op jit(solution)/shard_map/ppermute | solution.py:312
  29.9 5.7 %collective-permute-start.8 = (bf16[32,896]{1,0:T(8,128)(2,1)S(1)}, bf16[32,896]{1,0:T(8,128)(2,1)S(1)}, u32[]{:S(2)}, u32[]{:S(2)}) collective-permute-start(bf16[32,896]{1,0:T(8,128)(2,1)S(1)} %add_convert_fusion.1), channel_id=1, source_target_pairs={{0,17},{1,16},{2,19},{3,18},{4,21},{5,20},{6,23},{7,22},{8,25},{9,... | collective-permute-start | bytes 172040 | tf_op jit(solution)/shard_map/ppermute | solution.py:312
  32.1 4.3 %collective-permute-start.7 = (bf16[32,896]{1,0:T(8,128)(2,1)S(1)}, bf16[32,896]{1,0:T(8,128)(2,1)S(1)}, u32[]{:S(2)}, u32[]{:S(2)}) collective-permute-start(bf16[32,896]{1,0:T(8,128)(2,1)S(1)} %add_convert_fusion.1), channel_id=1, source_target_pairs={{0,1},{1,0},{2,3},{3,2},{4,5},{5,4},{6,7},{7,6},{8,9},{9,8},{10,11... | collective-permute-start | bytes 172040 | tf_op jit(solution)/shard_map/ppermute | solution.py:312
  33.0 4.2 %collective-permute-start.6 = (bf16[32,896]{1,0:T(8,128)(2,1)S(1)}, bf16[32,896]{1,0:T(8,128)(2,1)S(1)}, u32[]{:S(2)}, u32[]{:S(2)}) collective-permute-start(bf16[32,896]{1,0:T(8,128)(2,1)S(1)} %add_convert_fusion.1), channel_id=1, source_target_pairs={{0,16},{1,17},{2,18},{3,19},{4,20},{5,21},{6,22},{7,23},{8,24},{9,... | collective-permute-start | bytes 172040 | tf_op jit(solution)/shard_map/ppermute | solution.py:312
  37.2 6.3 %collective-permute-start.11 = (bf16[32,896]{1,0:T(8,128)(2,1)S(1)}, bf16[32,896]{1,0:T(8,128)(2,1)S(1)}, u32[]{:S(2)}, u32[]{:S(2)}) collective-permute-start(bf16[32,896]{1,0:T(8,128)(2,1)S(1)} %add_convert_fusion), channel_id=1, source_target_pairs={{0,6},{1,7},{2,4},{3,5},{4,2},{5,3},{6,0},{7,1},{8,14},{9,15},{10,... | collective-permute-start | bytes 172040 | tf_op jit(solution)/shard_map/ppermute | solution.py:312
  41.0 5.2 %collective-permute-start.10 = (bf16[32,896]{1,0:T(8,128)(2,1)S(1)}, bf16[32,896]{1,0:T(8,128)(2,1)S(1)}, u32[]{:S(2)}, u32[]{:S(2)}) collective-permute-start(bf16[32,896]{1,0:T(8,128)(2,1)S(1)} %add_convert_fusion), channel_id=1, source_target_pairs={{0,4},{1,5},{2,6},{3,7},{4,0},{5,1},{6,2},{7,3},{8,12},{9,13},{10,... | collective-permute-start | bytes 172040 | tf_op jit(solution)/shard_map/ppermute | solution.py:312
  41.5 4.8 %collective-permute-start.9 = (bf16[32,896]{1,0:T(8,128)(2,1)S(1)}, bf16[32,896]{1,0:T(8,128)(2,1)S(1)}, u32[]{:S(2)}, u32[]{:S(2)}) collective-permute-start(bf16[32,896]{1,0:T(8,128)(2,1)S(1)} %add_convert_fusion), channel_id=1, source_target_pairs={{0,2},{1,3},{2,0},{3,1},{4,6},{5,7},{6,4},{7,5},{8,10},{9,11},{10,... | collective-permute-start | bytes 172040 | tf_op jit(solution)/shard_map/ppermute | solution.py:312
  46.3 4.4 %collective-permute-start.12 = (f32[32,896]{1,0:T(8,128)S(1)}, f32[32,896]{1,0:T(8,128)S(1)}, u32[]{:S(2)}, u32[]{:S(2)}) collective-permute-start(f32[32,896]{1,0:T(8,128)S(1)} %add_add_fusion), channel_id=1, source_target_pairs={{0,8},{1,9},{2,10},{3,11},{4,12},{5,13},{6,14},{7,15},{8,0},{9,1},... | collective-permute-start | bytes 344072 | tf_op jit(solution)/shard_map/ppermute | solution.py:312

commit v2 on v1

v2 whole, which is shorter than its diff:
```python
import functools

import jax
import jax.numpy as jnp
from jax import lax
from jax.experimental import pallas as pl
from jax.experimental.pallas import tpu as pltpu
from jax.sharding import PartitionSpec as P

AXES = ("smp", "gx", "gz")
BF = jnp.bfloat16
F32 = jnp.float32
LANES = 128
TERMS = 896


def mm(a, b):
    return lax.dot_general(a, b, (((1,), (0,)), ((), ())), preferred_element_type=F32)


def mm_nt(a, b):
    return lax.dot_general(a, b, (((1,), (1,)), ((), ())), preferred_element_type=F32)


def iota(shape, dim):
    return lax.broadcasted_iota(jnp.int32, shape, dim)


def one_hot(hit):
    return jnp.where(hit, 1.0, 0.0).astype(BF)


def params():
    return pltpu.CompilerParams(vmem_limit_bytes=20 * 2**20)


def is_even(axis):
    return lax.axis_index(axis) % 2 == 0


def pack_kernel(
    nx, ch, ny, f_any, g_any, fo_ref, go_ref, one_ref, two_ref, far_one_ref, far_two_ref, edge_ref, held, raw, sems
):
    rows = ch * ny
    part = ch // 4
    copies = []
    for i, src in enumerate((f_any, g_any)):
        for q in range(4):
            at = pl.ds(q * part, part)
            copies.append(pltpu.make_async_copy(src.at[0, at], held.at[i, at], sems.at[i * 4 + q]))
    for copy in copies:
        copy.start()
    r, k = iota((rows, rows), 0), iota((rows, rows), 1)
    perm = one_hot(k == (r % ch) * ny + r // ch)
    for i, dst in enumerate((fo_ref, go_ref)):
        for copy in copies[i * 4 : i * 4 + 4]:
            copy.wait()
        for x in range(nx):
            block = held[i, :, x].astype(F32).reshape(rows, LANES)
            raw[:, x * LANES : (x + 1) * LANES] = block.astype(BF)
        dst[...] = mm(perm, raw[...]).astype(BF)
    even = is_even("gx")
    last = (nx - 1) * LANES
    for i, src in enumerate((fo_ref, go_ref)):
        up, down = src[:, last:], src[:, 0:LANES]
        one_ref[i * rows : (i + 1) * rows] = jnp.where(even, up, down)
        two_ref[i * rows : (i + 1) * rows] = jnp.where(even, down, up)
    up, down = fo_ref[:, last - LANES : last], fo_ref[:, LANES : 2 * LANES]
    far_one_ref[...] = jnp.where(even, up, down)
    far_two_ref[...] = jnp.where(even, down, up)
    n = edge_ref.shape[0]
    j, m = iota((n, nx * LANES), 0), iota((n, nx * LANES), 1)
    c, x = j // nx, j % nx
    zf = jnp.where(c < 2, c, LANES - 4 + c)
    pick_f = one_hot((c < 4) & (m == x * LANES + zf))
    zg = jnp.where(c == 4, 0, LANES - 1)
    pick_g = one_hot((c >= 4) & (c < 6) & (m == x * LANES + zg))
    edge_ref[...] = (mm_nt(pick_f, fo_ref[...]) + mm_nt(pick_g, go_ref[...])).astype(BF)


def pack(features, cotangent):
    _, ch, nx, ny, _ = features.shape
    rows = ch * ny
    edge_rows = -(-6 * nx // 32) * 32
    sds = jax.ShapeDtypeStruct
    anywhere = pl.BlockSpec(memory_space=pl.ANY)
    return pl.pallas_call(
        functools.partial(pack_kernel, nx, ch, ny),
        out_shape=(
            sds((rows, nx * LANES), BF),
            sds((rows, nx * LANES), BF),
            sds((2 * rows, LANES), BF),
            sds((2 * rows, LANES), BF),
            sds((rows, LANES), BF),
            sds((rows, LANES), BF),
            sds((edge_rows, rows), BF),
        ),
        in_specs=[anywhere, anywhere],
        scratch_shapes=[
            pltpu.VMEM((2, ch, nx, ny, LANES), BF),
            pltpu.VMEM((rows, nx * LANES), BF),
            pltpu.SemaphoreType.DMA((8,)),
        ],
        compiler_params=params(),
        name="pack",
    )(features, cotangent)


def bands_kernel(ny, w1_ref, w2_ref, t1_ref, tv_ref, t2_ref):
    ch = w1_ref.shape[-1]
    rows = ny * ch
    lane = iota((ch, rows), 1)
    r, k = iota((ch, ch), 0), iota((ch, ch), 1)
    turned = mm_nt(one_hot(r == k), w2_ref[...].reshape(27 * ch, ch))
    rest = jnp.zeros((ch, rows - 3 * ch), F32)

    def flipped(a, b, c):
        at = ch * ((2 - a) * 9 + (2 - b) * 3 + (2 - c))
        return turned[:, at : at + ch]

    first = lambda a, b, c: w1_ref[a, b, c].astype(F32)
    second = lambda a, b, c: w2_ref[a, b, c].astype(F32)
    for tap, out in ((first, t1_ref), (flipped, tv_ref), (second, t2_ref)):
        for a in range(3):
            for c in range(3):
                wide = jnp.concatenate([tap(a, 0, c), tap(a, 1, c), tap(a, 2, c), rest], axis=1)
                for y in range(ny):
                    block = wide if y == 1 else pltpu.roll(wide, (ch * (y - 1)) % rows, 1)
                    if y == 0:
                        block = jnp.where(lane >= rows - ch, 0.0, block)
                    if y == ny - 1:
                        block = jnp.where(lane < ch, 0.0, block)
                    out[a, y * ch : (y + 1) * ch, c * rows : (c + 1) * rows] = block.astype(BF)


def bands(first_weight, second_weight, ny):
    ch = first_weight.shape[0]
    rows = ch * ny
    laid = lambda weight: jnp.transpose(weight, (1, 2, 3, 0, 4))
    return pl.pallas_call(
        functools.partial(bands_kernel, ny),
        out_shape=(jax.ShapeDtypeStruct((3, rows, 3 * rows), BF),) * 3,
        compiler_params=params(),
        cost_estimate=pl.CostEstimate(flops=1_000_000_000, bytes_accessed=4_000_000, transcendentals=0),
        name="bands",
    )(laid(first_weight), laid(second_weight))


def shifted_rows(out, row, block, before, after, rows):
    lane = iota(block.shape, 1)
    at = slice(row * LANES, (row + 1) * LANES)
    wide = block.astype(F32)
    out[0:rows, at] = jnp.where(lane == 0, before, pltpu.roll(wide, 1, 1)).astype(BF)
    out[rows : 2 * rows, at] = block
    out[2 * rows :, at] = jnp.where(lane == LANES - 1, after, pltpu.roll(wide, LANES - 1, 1)).astype(BF)


def lane_to(edges, source, target):
    shift = (target - source) % LANES
    return edges if shift == 0 else pltpu.roll(edges, shift, 1)


def fold_taps(product, ch, ny):
    rows = ch * ny
    lane = iota((ch, rows), 1)
    total = None
    for y in range(ny):
        block = product[y * ch : (y + 1) * ch]
        if y == 0:
            block = jnp.where(lane >= rows - ch, 0.0, block)
        if y == ny - 1:
            block = jnp.where(lane < ch, 0.0, block)
        if y != 1:
            block = pltpu.roll(block, (ch * (1 - y)) % rows, 1)
        total = block if total is None else total + block
    return total[:, :LANES]


def place_taps(columns, folded, a, c, ch):
    lane = iota(folded.shape, 1)
    for b in range(3):
        target = ch * ((a * 3 + b) * 3 + c)
        col, offset = target // LANES, target % LANES
        moved = lane_to(folded, b * ch, offset)
        columns[col] = jnp.where((lane >= offset) & (lane < offset + ch), moved, columns[col])


def bias_terms(field, ch, ny):
    nx = field.shape[1] // LANES
    wide = field.astype(F32)
    total = wide[:, 0:LANES]
    for x in range(1, nx):
        total = total + wide[:, x * LANES : (x + 1) * LANES]
    folded = total[0:ch]
    for y in range(1, ny):
        folded = folded + total[y * ch : (y + 1) * ch]
    return jnp.sum(folded, axis=1, keepdims=True)


def silu(preact):
    return (preact / (1.0 + jnp.exp(-preact))).astype(BF)


def sides(even, one, two):
    return jnp.where(even, two, one), jnp.where(even, one, two)


def edge_columns(nx, even, near_ref, one_ref, two_ref):
    n = near_ref.shape[0]
    j, k = iota((LANES, n), 0), iota((LANES, n), 1)
    s, xx = j // 16, j % 16
    column = jnp.where(s == 0, 2, jnp.where(s == 1, 3, jnp.where(s == 5, 0, jnp.where(s == 6, 1, jnp.where(s == 3, 5, jnp.where(s == 7, 4, -1))))))
    first = column * nx
    hit = lambda low, high, offset: one_hot((column >= 0) & (xx >= low) & (xx < high) & (k == first + xx - low + offset))
    before, after = sides(even, one_ref[...], two_ref[...])
    out = mm(hit(2, nx + 2, 0), near_ref[...])
    out = out + mm(hit(0, 2, nx - 2), before)
    return out + mm(hit(nx + 2, nx + 4, 0), after)


def main_kernel(
    nx, ch, ny, scale,
    t1_ref, tv_ref, f_ref, g_ref, one_ref, two_ref, near_ref, edge_one_ref, edge_two_ref, bias_ref,
    hid_ref, fs, keep_ref, give_ref,
    gs, pre,
):
    rows = ch * ny
    even = is_even("gx")
    edges = edge_columns(nx, even, near_ref, edge_one_ref, edge_two_ref).T
    for i, (src, dst, left, right) in enumerate(((f_ref, fs, 16, 80), (g_ref, gs, 48, 112))):
        above, below = sides(even, one_ref[i * rows : (i + 1) * rows], two_ref[i * rows : (i + 1) * rows])
        for x in range(nx + 2):
            if x == 0:
                block = above
            elif x == nx + 1:
                block = below
            else:
                block = src[:, (x - 1) * LANES : x * LANES]
            shifted_rows(dst, x, block, lane_to(edges, left + x + 1, 0), lane_to(edges, right + x + 1, LANES - 1), rows)

    n5 = nx * LANES
    acc = mm(t1_ref[0], fs[:, 0:n5])
    for a in range(1, 3):
        acc = acc + mm(t1_ref[a], fs[:, a * LANES : a * LANES + n5])
    preact = acc + bias_ref[...]
    pre[...] = preact
    hid_ref[...] = silu(preact)
    hidden = hid_ref[...]

    lane = iota((ch, LANES), 1)
    spare = 27 * ch % LANES
    mine = is_even("smp")
    columns = [jnp.zeros((ch, LANES), F32) for _ in range(TERMS // LANES)]
    for a in range(3):
        for c in range(3):
            left = gs[(2 - c) * rows : (3 - c) * rows, (2 - a) * LANES : (2 - a) * LANES + n5]
            place_taps(columns, fold_taps(mm_nt(left, hidden), ch, ny), a, c, ch)
    columns[-1] = jnp.where(lane == spare, bias_terms(g_ref[...], ch, ny), columns[-1])
    second = [part * scale for part in columns]

    acc = mm(tv_ref[0], gs[:, 0:n5])
    for a in range(1, 3):
        acc = acc + mm(tv_ref[a], gs[:, a * LANES : a * LANES + n5])
    preact = pre[...]
    logistic = 1.0 / (1.0 + jnp.exp(-preact))
    preact_grad = (acc * logistic * (1.0 + preact * (1.0 - logistic))).astype(BF)

    columns = [jnp.zeros((ch, LANES), F32) for _ in range(TERMS // LANES)]
    for a in range(3):
        for c in range(3):
            taps = fs[c * rows : (c + 1) * rows, a * LANES : a * LANES + n5]
            place_taps(columns, fold_taps(mm_nt(preact_grad, taps), ch, ny), a, c, ch)
    columns[-1] = jnp.where(lane == spare, bias_terms(preact_grad, ch, ny), columns[-1])
    first = [part * scale for part in columns]
    for i in range(TERMS // LANES):
        at = slice(i * LANES, (i + 1) * LANES)
        keep_ref[:, at] = jnp.where(mine, second[i], first[i])
        give_ref[:, at] = jnp.where(mine, first[i], second[i])


def main(t1, tv, field, cot, one, two, near, edge_one, edge_two, bias, ch, ny, scale):
    rows = ch * ny
    nx = field.shape[1] // LANES
    sds = jax.ShapeDtypeStruct
    return pl.pallas_call(
        functools.partial(main_kernel, nx, ch, ny, scale),
        out_shape=(
            sds((rows, nx * LANES), BF),
            sds((3 * rows, (nx + 2) * LANES), BF),
            sds((ch, TERMS), F32),
            sds((ch, TERMS), F32),
        ),
        scratch_shapes=[
            pltpu.VMEM((3 * rows, (nx + 2) * LANES), BF),
            pltpu.VMEM((rows, nx * LANES), F32),
        ],
        compiler_params=params(),
        name="main",
    )(t1, tv, field, cot, one, two, near, edge_one, edge_two, bias)


def residual_kernel(
    nx, ch, ny,
    t1_ref, t2_ref, h_ref, fs_ref, f_ref, far_one_ref, far_two_ref, near_ref, edge_one_ref, edge_two_ref, bias1_ref, bias2_ref,
    o_ref,
    ends, hs,
):
    rows = ch * ny
    even = is_even("gx")
    above, below = sides(even, far_one_ref[...], far_two_ref[...])
    middle = fs_ref[rows : 2 * rows]
    edges_t = edge_columns(nx, even, near_ref, edge_one_ref, edge_two_ref)
    j, k = iota((LANES, LANES), 0), iota((LANES, LANES), 1)
    own_end = jnp.where(j // 16 == 2, 0, jnp.where(j // 16 == 4, LANES - 1, -1))
    for x in range(nx + 4):
        block = above if x == 0 else below if x == nx + 3 else middle[:, (x - 1) * LANES : x * LANES]
        edges_t = edges_t + mm_nt(one_hot((j % 16 == x) & (k == own_end)), block)
    edges = edges_t.T
    shifted_rows(ends, 0, above, lane_to(edges, 16, 0), lane_to(edges, 80, LANES - 1), rows)
    shifted_rows(ends, 1, below, lane_to(edges, 16 + nx + 3, 0), lane_to(edges, 80 + nx + 3, LANES - 1), rows)
    acc = None
    row = lambda x: fs_ref[:, (x + 1) * LANES : (x + 2) * LANES]
    pairs = ((ends[:, 0:LANES], row(nx - 1)), (row(-1), row(nx)), (row(0), ends[:, LANES:]))
    for a in range(3):
        columns = [lane_to(edges, 16 * c + a, 0).astype(BF) for c in range(3)]
        term = mm(t1_ref[a], jnp.concatenate([*pairs[a], jnp.concatenate(columns, axis=0)], axis=1))
        acc = term if acc is None else acc + term
    hidden = silu(acc + bias1_ref[...])
    outer = hidden[:, 2 * LANES :].astype(F32)
    for x in range(nx + 2):
        if x == 0:
            block = hidden[:, 0:LANES]
        elif x == nx + 1:
            block = hidden[:, LANES : 2 * LANES]
        else:
            block = h_ref[:, (x - 1) * LANES : x * LANES]
        shifted_rows(hs, x, block, lane_to(outer, x, 0), lane_to(outer, 64 + x, LANES - 1), rows)
    n5 = nx * LANES
    acc = mm(t2_ref[0], hs[:, 0:n5])
    for a in range(1, 3):
        acc = acc + mm(t2_ref[a], hs[:, a * LANES : a * LANES + n5])
    total = (f_ref[...].astype(F32) + (acc + bias2_ref[...])).astype(BF)
    r, k = iota((rows, rows), 0), iota((rows, rows), 1)
    back = one_hot(k == (r % ny) * ch + r // ny)
    ordered = mm(back, total)
    for x in range(nx):
        o_ref[0, :, x] = ordered[:, x * LANES : (x + 1) * LANES].reshape(ch, ny, LANES).astype(BF)


def residual(t1, t2, hidden, fs, field, far_one, far_two, near, edge_one, edge_two, bias1, bias2, ch, ny):
    rows = ch * ny
    nx = field.shape[1] // LANES
    return pl.pallas_call(
        functools.partial(residual_kernel, nx, ch, ny),
        out_shape=jax.ShapeDtypeStruct((1, ch, nx, ny, LANES), BF),
        scratch_shapes=[pltpu.VMEM((3 * rows, 2 * LANES), BF), pltpu.VMEM((3 * rows, (nx + 2) * LANES), BF)],
        compiler_params=params(),
        cost_estimate=pl.CostEstimate(flops=3_000_000_000, bytes_accessed=3_000_000, transcendentals=0),
        name="residual",
    )(t1, t2, hidden, fs, field, far_one, far_two, near, edge_one, edge_two, bias1, bias2)


def moved(array, sizes, step):
    ns, nx, nz = sizes
    pairs = []
    for s in range(ns):
        for x in range(nx):
            for z in range(nz):
                t, u, v = step(s, x, z)
                pairs.append(((s * nx + x) * nz + z, (t * nx + u) * nz + v))
    return lax.ppermute(array, AXES, pairs)


def paired(array, sizes, turn, dz):
    ns, nx, nz = sizes
    return moved(array, sizes, lambda s, x, z: (s, (x + (1 if x % 2 == turn else -1)) % nx, (z + dz) % nz))


def swapped(array, sizes, bits):
    return moved(array, sizes, lambda s, x, z: (s ^ bits[0], x ^ bits[1], z ^ bits[2]))


def add_kernel(n_in, *refs):
    terms = [ref[...].astype(F32) for ref in refs[:n_in]]
    out = refs[n_in]
    while len(terms) > 1:
        terms = [terms[i] + terms[i + 1] for i in range(0, len(terms), 2)]
    total = terms[0]
    n = total.shape[1] - LANES
    out[:, :n] = total[:, :n].astype(out.dtype)
    tail = total[:, n:]
    lane = iota(tail.shape, 1)
    spare = 864 % LANES
    joined = tail + pltpu.roll(tail, LANES - 1, 1)
    if out.dtype == BF:
        low = joined - joined.astype(BF).astype(F32)
        tail = jnp.where(lane == spare + 1, pltpu.roll(low, 1, 1), tail)
    out[:, n:] = jnp.where(lane == spare, joined, tail).astype(out.dtype)


def add(terms, dtype):
    return pl.pallas_call(
        functools.partial(add_kernel, len(terms)),
        out_shape=jax.ShapeDtypeStruct(terms[0].shape, dtype),
        compiler_params=params(),
        name="add",
    )(*terms)


def exchange(sent, sizes, pair):
    steps = [(0, 0, 0)]
    for bits in pair:
        steps = steps + [tuple(p ^ q for p, q in zip(bits, step)) for step in steps]
    return [sent] + [swapped(sent, sizes, step) for step in steps[1:]]


def sum_all(keep, give, sizes, output):
    near = (1, 0, 0)
    bits = [(1 << i, 0, 0) for i in range(1, sizes[0].bit_length() - 1)]
    bits += [(0, 0, 1 << i) for i in range(sizes[2].bit_length() - 1)]
    bits += [(0, 1 << i, 0) for i in range(sizes[1].bit_length() - 1)]
    terms = [keep, swapped(give, sizes, near)]
    for i in range(0, len(bits), 2):
        terms = exchange(add(terms, BF), sizes, bits[i : i + 2])
        if i == 0:
            *terms, output = lax.optimization_barrier((*terms, output))
    mine = add(terms, F32)
    return mine, swapped(mine, sizes, near), output


def spread_kernel(ch, mine_ref, other_ref, first_ref, first_bias_ref, second_ref, second_bias_ref):
    even = is_even("smp")
    mine, other = mine_ref[...], other_ref[...]
    r, k = iota((ch, LANES), 0), iota((ch, LANES), 1)
    for terms, out, bias in (
        (jnp.where(even, other, mine), first_ref, first_bias_ref),
        (jnp.where(even, mine, other), second_ref, second_bias_ref),
    ):
        for tap in range(27):
            at = tap * ch
            block = terms[:, at // LANES * LANES : (at // LANES + 1) * LANES]
            out[tap // 9, tap // 3 % 3, tap % 3] = lane_to(block, at % LANES, 0)[:, :ch]
        tail = lane_to(terms[:, TERMS - LANES :], 27 * ch % LANES, 0)[:, 0:1]
        bias[...] = jnp.sum(jnp.where(r == k, tail, 0.0), axis=0, keepdims=True)[:, :ch]


def spread(mine, other, ch):
    sds = jax.ShapeDtypeStruct
    taps, bias = sds((3, 3, 3, ch, ch), F32), sds((1, ch), F32)
    first, first_bias, second, second_bias = pl.pallas_call(
        functools.partial(spread_kernel, ch),
        out_shape=(taps, bias, taps, bias),
        compiler_params=params(),
        name="spread",
    )(mine, other)
    laid = lambda grad: jnp.transpose(grad, (3, 0, 1, 2, 4))
    return laid(first), first_bias.reshape(ch), laid(second), second_bias.reshape(ch)


def shards(sizes, features, first_weight, first_bias, second_weight, second_bias, cotangent):
    ns, ngx, ngz = sizes
    _, ch, nx, ny, nz = features.shape
    assert features.shape[0] == 1 and nz == LANES and ngz == 2 and ngx % 2 == 0
    assert not any(n & (n - 1) for n in sizes) and ns > 1
    scale = float((ns * nx * ngx * ny * nz * ngz) ** -0.5)
    field, cot, one, two, far_one, far_two, edge = pack(features, cotangent)
    one, two = paired(one, sizes, 0, 0), paired(two, sizes, 1, 0)
    near = swapped(edge, sizes, (0, 0, 1))
    edge_one, edge_two = paired(edge, sizes, 0, 1), paired(edge, sizes, 1, 1)
    far_one, far_two = paired(far_one, sizes, 0, 0), paired(far_two, sizes, 1, 0)
    t1, tv, t2 = bands(first_weight, second_weight, ny)
    column = lambda bias: jnp.tile(bias, ny)[:, None]
    bias1, bias2 = column(first_bias), column(second_bias)
    hidden, fs, keep, give = main(t1, tv, field, cot, one, two, near, edge_one, edge_two, bias1, ch, ny, scale)
    output = residual(t1, t2, hidden, fs, field, far_one, far_two, near, edge_one, edge_two, bias1, bias2, ch, ny)
    mine, other, output = sum_all(keep, give, sizes, output)
    return output, *spread(mine, other, ch)


def solution(mesh):
    sizes = tuple(mesh.shape[axis] for axis in AXES)
    split = P("smp", None, "gx", None, "gz")
    return jax.shard_map(
        functools.partial(shards, sizes),
        mesh=mesh,
        in_specs=(split, P(), P(), P(), P(), split),
        out_specs=(split, P(), P(), P(), P()),
        check_vma=False,
    )
```

time: 54 us -> 55.8 us (1.033)
  local copies, waits for them, and re-layouts: 8.8 us -> 12.5 us
  waiting for transfers between devices: 10.2 us -> 6.69 us
  Pallas kernels: 13 us -> 15 us
  other arithmetic: 1.38 us -> 0 us
  starting transfers between devices: 19.5 us -> 20.4 us
    unnamed x13 -> x30, local copies, waits for them, and re-layouts: 6.4 us -> 12.3 us
    ppermute x13 -> x15, waiting for transfers between devices: 10.2 us -> 6.69 us  [moved(): return lax.ppermute(array, AXES, pairs)]
    pallas_call x1, Pallas kernels: 0.92 us -> 2.57 us  [pack(): pl.pallas_call(functools.partial(pack_kernel, nx, ch, ny), out_shape=(sds...]
    convert_element_type x3 -> x0, other arithmetic: 1.27 us -> none  [the longest x1 1.21 us: bands(): jnp.transpose(stacked, (0, 2, 4, 1, 3, 5)).reshape(3, 9, ch, 3 * ch)]
    ppermute x13 -> x15, starting transfers between devices: 19.5 us -> 20.4 us  [moved(): return lax.ppermute(array, AXES, pairs)]
    convert_element_type x2 -> x0, local copies, waits for them, and re-layouts: 0.82 us -> none  [bands(): jnp.transpose(stacked, (0, 2, 4, 1, 3, 5)).reshape(3, 9, ch, 3 * ch)]
    slice x1 -> x0, local copies, waits for them, and re-layouts: 0.7 us -> none  [shards(): terms[:, 27 * ch]]
    reshape x2 -> x0, local copies, waits for them, and re-layouts: 0.6 us -> none  [shards(): terms[:, :27 * ch].reshape(ch, 3, 3, 3, ch)]
  transfers between devices with their start and end apart: 13 -> 15, of which waited for: 8 -> 6; matrix products, arithmetic and copies ran while one was open for 6% -> 0% of each run, Pallas kernels for 9% -> 10%
where the time goes in v2:
time: 55.8 us; the launch traced here: 55.4 us
  starting transfers between devices  20.4 us (37%)
  Pallas kernels  15 us (27%)
  local copies, waits for them, and re-layouts  12.5 us (22%)
  waiting for transfers between devices  6.69 us (12%)
  between operations  0.76 us (1%)
    ppermute x15, starting transfers between devices, moved(): return lax.ppermute(array, AXES, pairs)  20.4 us
    unnamed x30, local copies, waits for them, and re-layouts  12.3 us
    ppermute x15, waiting for transfers between devices, moved(): return lax.ppermute(array, AXES, pairs)  6.69 us
    pallas_call x1, Pallas kernels, main(): pl.pallas_call(functools.partial(main_kernel, nx, ch, ny, scale), out_sha...  5.47 us
    pallas_call x1, Pallas kernels, residual(): pl.pallas_call(functools.partial(residual_kernel, nx, ch, ny), out_shape=...  3.48 us
    pallas_call x1, Pallas kernels, pack(): pl.pallas_call(functools.partial(pack_kernel, nx, ch, ny), out_shape=(sds...  2.57 us
    pallas_call x1, Pallas kernels, bands(): pl.pallas_call(functools.partial(bands_kernel, ny), out_shape=(jax.ShapeD...  1.89 us
    pallas_call x1, Pallas kernels, spread(): pl.pallas_call(functools.partial(spread_kernel, ch), out_shape=(taps, bia...  1.2 us
  transfers between devices with their start and end apart: 15, of which 6 were waited for; matrix products, arithmetic and copies ran while one was open for 0% of the time, Pallas kernels for 10%

profile of v2, /device:TPU:0, one launch (start us, length us, event | category | flops | bytes accessed | tf_op | source)
XLA Modules:
  0.0 55.4 jit_solution(17699083317817232183)
XLA Ops:
  0.6 1.0 %copy-done = bf16[1,32,5,8,128]{4,3,2,1,0:T(8,128)(2,1)S(1)} copy-done((bf16[1,32,5,8,128]{4,3,2,1,0:T(8,128)(2,1)S(1)}, bf16[1,32,5,8,128]{4,3,2,1,0:T(8,128)(2,1)}, u32[]{:S(2)}) %copy-start) | copy-done | bytes 327704
  1.6 1.0 %copy-done.1 = bf16[1,32,5,8,128]{4,3,2,1,0:T(8,128)(2,1)S(1)} copy-done((bf16[1,32,5,8,128]{4,3,2,1,0:T(8,128)(2,1)S(1)}, bf16[1,32,5,8,128]{4,3,2,1,0:T(8,128)(2,1)}, u32[]{:S(2)}) %copy-start.1) | copy-done | bytes 327704
  2.6 2.6 %pack.1 = (bf16[256,640]{1,0:T(8,128)(2,1)S(1)}, bf16[256,640]{1,0:T(8,128)(2,1)S(1)}, bf16[512,128]{1,0:T(8,128)(2,1)}, bf16[512,128]{1,0:T(8,128)(2,1)}, bf16[...) custom-call(bf16[1,32,5,8,128]{4,3,2,1,0:T(8,128)(2,1)S(1)} %copy-done, ...), custom_call_target="tpu_custom_call" | custom-call | tf_op jit(solution)/shard_map/pack/pallas_call | solution.py:87
  5.2 3.1 %collective-permute-start = (bf16[512,128]{1,0:T(8,128)(2,1)}, bf16[512,128]{1,0:T(8,128)(2,1)S(1)}, u32[]{:S(2)}, u32[]{:S(2)}) collective-permute-start(bf16[512,128]{1,0:T(8,128)(2,1)} %get-tuple-element.32), channel_id=1, source_target_pairs={{0,2},{1,3},{2,0},{3,1},{4,6},{5,7},{6,4},{7,5},{8,10},{9,11},{10,... | collective-permute-start | bytes 393224 | tf_op jit(solution)/shard_map/ppermute | solution.py:371
  8.2 2.5 %collective-permute-start.1 = (bf16[512,128]{1,0:T(8,128)(2,1)}, bf16[512,128]{1,0:T(8,128)(2,1)S(1)}, u32[]{:S(2)}, u32[]{:S(2)}) collective-permute-start(bf16[512,128]{1,0:T(8,128)(2,1)} %get-tuple-element.33), channel_id=1, source_target_pairs={{0,6},{1,7},{2,4},{3,5},{4,2},{5,3},{6,0},{7,1},{8,14},{9,15},{10,... | collective-permute-start | bytes 393224 | tf_op jit(solution)/shard_map/ppermute | solution.py:371
  10.7 1.5 %collective-permute-start.2 = (bf16[32,256]{1,0:T(8,128)(2,1)S(1)}, bf16[32,256]{1,0:T(8,128)(2,1)S(1)}, u32[]{:S(2)}, u32[]{:S(2)}) collective-permute-start(bf16[32,256]{1,0:T(8,128)(2,1)S(1)} %get-tuple-element.34), channel_id=1, source_target_pairs={{0,1},{1,0},{2,3},{3,2},{4,5},{5,4},{6,7},{7,6},{8,9},{9,8},{10,11... | collective-permute-start | bytes 49160 | tf_op jit(solution)/shard_map/ppermute | solution.py:371
  12.2 0.6 %collective-permute-start.3 = (bf16[32,256]{1,0:T(8,128)(2,1)S(1)}, bf16[32,256]{1,0:T(8,128)(2,1)S(1)}, u32[]{:S(2)}, u32[]{:S(2)}) collective-permute-start(bf16[32,256]{1,0:T(8,128)(2,1)S(1)} %get-tuple-element.34), channel_id=1, source_target_pairs={{0,3},{1,2},{2,1},{3,0},{4,7},{5,6},{6,5},{7,4},{8,11},{9,10},{10,... | collective-permute-start | bytes 49160 | tf_op jit(solution)/shard_map/ppermute | solution.py:371
  12.9 1.8 %collective-permute-start.4 = (bf16[32,256]{1,0:T(8,128)(2,1)S(1)}, bf16[32,256]{1,0:T(8,128)(2,1)S(1)}, u32[]{:S(2)}, u32[]{:S(2)}) collective-permute-start(bf16[32,256]{1,0:T(8,128)(2,1)S(1)} %get-tuple-element.34), channel_id=1, source_target_pairs={{0,7},{1,6},{2,5},{3,4},{4,3},{5,2},{6,1},{7,0},{8,15},{9,14},{10,... | collective-permute-start | bytes 49160 | tf_op jit(solution)/shard_map/ppermute | solution.py:371
  14.7 0.9 %copy-done.9 = bf16[32,3,3,3,32]{4,0,3,2,1:T(8,128)(2,1)S(1)} copy-done((bf16[32,3,3,3,32]{4,0,3,2,1:T(8,128)(2,1)S(1)}, bf16[32,3,3,3,32]{4,0,3,2,1:T(8,128)(2,1)}, u32[]{:S(2)}) %copy-start.9) | copy-done | bytes 55320
  15.6 0.9 %copy-done.10 = bf16[32,3,3,3,32]{4,0,3,2,1:T(8,128)(2,1)S(1)} copy-done((bf16[32,3,3,3,32]{4,0,3,2,1:T(8,128)(2,1)S(1)}, bf16[32,3,3,3,32]{4,0,3,2,1:T(8,128)(2,1)}, u32[]{:S(2)}) %copy-start.10) | copy-done | bytes 55320
  16.6 1.9 %bands.1 = (bf16[3,256,768]{2,1,0:T(8,128)(2,1)S(1)}, bf16[3,256,768]{2,1,0:T(8,128)(2,1)S(1)}, bf16[3,256,768]{2,1,0:T(8,128)(2,1)S(1)}) custom-call(bf16[3,3,3,32,32]{4,3,2,1,0:T(8,128)(2,1)S(1)} %bitcast.6, bf16[3,3,3,32,32]{4,3,2,1,0:T(8,128)(2,1)S(1)} %bitcast.7), custom_call_target="tpu_custom_call" | custom-call | flops 1000000000 | bytes 4000000 | tf_op jit(solution)/shard_map/bands/pallas_call | solution.py:140
  18.5 1.0 %copy-done.11 = bf16[3,256,768]{2,1,0:T(8,128)(2,1)} copy-done((bf16[3,256,768]{2,1,0:T(8,128)(2,1)}, bf16[3,256,768]{2,1,0:T(8,128)(2,1)S(1)}, u32[]{:S(2)}) %copy-start.11) | copy-done | bytes 1179672
  20.3 0.7 %copy-done.3 = bf16[32,256]{1,0:T(8,128)(2,1)S(1)} copy-done((bf16[32,256]{1,0:T(8,128)(2,1)S(1)}, bf16[32,256]{1,0:T(8,128)(2,1)}, u32[]{:S(2)}) %copy-start.3) | copy-done | bytes 16408
  21.0 5.5 %main.1 = (bf16[256,640]{1,0:T(8,128)(2,1)S(1)}, bf16[768,896]{1,0:T(8,128)(2,1)S(1)}, f32[32,896]{1,0:T(8,128)S(1)}, f32[32,896]{1,0:T(8,128)}) custom-call(bf16[3,256,768]{2,1,0:T(8,128)(2,1)S(1)} %get-tuple-element.28.t1_ref, bf16[3,256,768]{2,1,0:T(8,128)(2,1)S(1)} %get-tuple-element.29.tv_ref, bf16[256,640]{1,0:T(8,128)(2,1)S(1)} %get-tuple-element.30.f_ref, ...), custom_call_target="tpu_custom_call" | custom-call | tf_op jit(solution)/shard_map/main/pallas_call | solution.py:285
  26.5 1.1 %copy-done.5 = bf16[768,896]{1,0:T(8,128)(2,1)} copy-done((bf16[768,896]{1,0:T(8,128)(2,1)}, bf16[768,896]{1,0:T(8,128)(2,1)S(1)}, u32[]{:S(2)}) %copy-start.5) | copy-done | bytes 1376280
  27.6 0.7 %copy-done.7 = bf16[256,640]{1,0:T(8,128)(2,1)} copy-done((bf16[256,640]{1,0:T(8,128)(2,1)}, bf16[256,640]{1,0:T(8,128)(2,1)S(1)}, u32[]{:S(2)}) %copy-start.7) | copy-done | bytes 327704
  28.3 2.9 %collective-permute-start.10 = (bf16[256,128]{1,0:T(8,128)(2,1)}, bf16[256,128]{1,0:T(8,128)(2,1)S(1)}, u32[]{:S(2)}, u32[]{:S(2)}) collective-permute-start(bf16[256,128]{1,0:T(8,128)(2,1)} %get-tuple-element.41), channel_id=1, source_target_pairs={{0,6},{1,7},{2,4},{3,5},{4,2},{5,3},{6,0},{7,1},{8,14},{9,15},{10,... | collective-permute-start | bytes 196616 | tf_op jit(solution)/shard_map/ppermute | solution.py:371
  31.5 1.5 %collective-permute-start.6 = (bf16[32,896]{1,0:T(8,128)(2,1)S(1)}, bf16[32,896]{1,0:T(8,128)(2,1)S(1)}, u32[]{:S(2)}, u32[]{:S(2)}) collective-permute-start(bf16[32,896]{1,0:T(8,128)(2,1)S(1)} %add.3.refs_0_), channel_id=1, source_target_pairs={{0,16},{1,17},{2,18},{3,19},{4,20},{5,21},{6,22},{7,23},{8,24},{9,... | collective-permute-start | bytes 172040 | tf_op jit(solution)/shard_map/ppermute | solution.py:371
  33.6 1.4 %collective-permute-start.8 = (bf16[32,896]{1,0:T(8,128)(2,1)S(1)}, bf16[32,896]{1,0:T(8,128)(2,1)S(1)}, u32[]{:S(2)}, u32[]{:S(2)}) collective-permute-start(bf16[32,896]{1,0:T(8,128)(2,1)S(1)} %add.3.refs_0_), channel_id=1, source_target_pairs={{0,17},{1,16},{2,19},{3,18},{4,21},{5,20},{6,23},{7,22},{8,25},{9,... | collective-permute-start | bytes 172040 | tf_op jit(solution)/shard_map/ppermute | solution.py:371
  35.2 1.0 %collective-permute-done.9.far_one_ref = bf16[256,128]{1,0:T(8,128)(2,1)S(1)} collective-permute-done((bf16[256,128]{1,0:T(8,128)(2,1)}, bf16[256,128]{1,0:T(8,128)(2,1)S(1)}, u32[]{:S(2)}, u32[]{:S(2)}) %collective-permute-start.9) | collective-permute-done | bytes 65568 | tf_op jit(solution)/shard_map/ppermute | solution.py:371
  36.2 0.7 %copy-done.4 = bf16[32,256]{1,0:T(8,128)(2,1)S(1)} copy-done((bf16[32,256]{1,0:T(8,128)(2,1)S(1)}, bf16[32,256]{1,0:T(8,128)(2,1)}, u32[]{:S(2)}) %copy-start.4) | copy-done | bytes 16408
  36.9 1.3 %copy-done.6 = bf16[768,896]{1,0:T(8,128)(2,1)S(1)} copy-done((bf16[768,896]{1,0:T(8,128)(2,1)S(1)}, bf16[768,896]{1,0:T(8,128)(2,1)}, u32[]{:S(2)}) %copy-start.6) | copy-done | bytes 1376280
  38.3 1.0 %copy-done.8 = bf16[256,640]{1,0:T(8,128)(2,1)S(1)} copy-done((bf16[256,640]{1,0:T(8,128)(2,1)S(1)}, bf16[256,640]{1,0:T(8,128)(2,1)}, u32[]{:S(2)}) %copy-start.8) | copy-done | bytes 327704
  39.2 1.3 %copy-done.12 = bf16[3,256,768]{2,1,0:T(8,128)(2,1)S(1)} copy-done((bf16[3,256,768]{2,1,0:T(8,128)(2,1)S(1)}, bf16[3,256,768]{2,1,0:T(8,128)(2,1)}, u32[]{:S(2)}) %copy-start.12) | copy-done | bytes 1179672
  40.5 3.5 %residual.1 = bf16[1,32,5,8,128]{4,3,2,1,0:T(8,128)(2,1)} custom-call(bf16[3,256,768]{2,1,0:T(8,128)(2,1)S(1)} %get-tuple-element.28.t1_ref, bf16[3,256,768]{2,1,0:T(8,128)(2,1)S(1)} %copy-done.12, bf16[256,640]{1,0:T(8,128)(2,1)S(1)} %copy-done.8, bf16[768,896]{1,0:T(8,128)(2,1)S(1)} %copy-done.6, bf16[256,640]{1,0:T(8,128)(2,1)S(1)} %get-tuple-element.30.f_ref, ...), custom_call_target="tpu_custom_call" | custom-call | flops 3000000000 | bytes 3000000 | tf_op jit(solution)/shard_map/residual/pallas_call | solution.py:353
  44.2 1.1 %collective-permute-start.11 = (bf16[32,896]{1,0:T(8,128)(2,1)S(1)}, bf16[32,896]{1,0:T(8,128)(2,1)S(1)}, u32[]{:S(2)}, u32[]{:S(2)}) collective-permute-start(bf16[32,896]{1,0:T(8,128)(2,1)S(1)} %add.4.refs_0_), channel_id=1, source_target_pairs={{0,2},{1,3},{2,0},{3,1},{4,6},{5,7},{6,4},{7,5},{8,10},{9,11},{10,... | collective-permute-start | bytes 172040 | tf_op jit(solution)/shard_map/ppermute | solution.py:371
  45.3 1.3 %collective-permute-start.12 = (bf16[32,896]{1,0:T(8,128)(2,1)S(1)}, bf16[32,896]{1,0:T(8,128)(2,1)S(1)}, u32[]{:S(2)}, u32[]{:S(2)}) collective-permute-start(bf16[32,896]{1,0:T(8,128)(2,1)S(1)} %add.4.refs_0_), channel_id=1, source_target_pairs={{0,4},{1,5},{2,6},{3,7},{4,0},{5,1},{6,2},{7,3},{8,12},{9,13},{10,... | collective-permute-start | bytes 172040 | tf_op jit(solution)/shard_map/ppermute | solution.py:371
  46.7 1.9 %collective-permute-start.13 = (bf16[32,896]{1,0:T(8,128)(2,1)S(1)}, bf16[32,896]{1,0:T(8,128)(2,1)S(1)}, u32[]{:S(2)}, u32[]{:S(2)}) collective-permute-start(bf16[32,896]{1,0:T(8,128)(2,1)S(1)} %add.4.refs_0_), channel_id=1, source_target_pairs={{0,6},{1,7},{2,4},{3,5},{4,2},{5,3},{6,0},{7,1},{8,14},{9,15},{10,... | collective-permute-start | bytes 172040 | tf_op jit(solution)/shard_map/ppermute | solution.py:371
  48.9 3.0 %collective-permute-done.12.refs_2_ = bf16[32,896]{1,0:T(8,128)(2,1)S(1)} collective-permute-done((bf16[32,896]{1,0:T(8,128)(2,1)S(1)}, bf16[32,896]{1,0:T(8,128)(2,1)S(1)}, u32[]{:S(2)}, u32[]{:S(2)}) %collective-permute-start.12) | collective-permute-done | bytes 57376 | tf_op jit(solution)/shard_map/ppermute | solution.py:371
  51.9 0.8 %collective-permute-done.13.refs_3_ = bf16[32,896]{1,0:T(8,128)(2,1)S(1)} collective-permute-done((bf16[32,896]{1,0:T(8,128)(2,1)S(1)}, bf16[32,896]{1,0:T(8,128)(2,1)S(1)}, u32[]{:S(2)}, u32[]{:S(2)}) %collective-permute-start.13) | collective-permute-done | bytes 57376 | tf_op jit(solution)/shard_map/ppermute | solution.py:371
  52.9 1.3 %collective-permute-done.14.other_ref = f32[32,896]{1,0:T(8,128)S(1)} collective-permute-done((f32[32,896]{1,0:T(8,128)S(1)}, f32[32,896]{1,0:T(8,128)S(1)}, u32[]{:S(2)}, u32[]{:S(2)}) %collective-permute-start.14) | collective-permute-done | bytes 114720 | tf_op jit(solution)/shard_map/ppermute | solution.py:371
  54.2 1.2 %spread.1 = (f32[3,3,3,32,32]{4,3,2,1,0:T(8,128)}, f32[1,32]{1,0:T(1,128)}, f32[3,3,3,32,32]{4,3,2,1,0:T(8,128)}, f32[1,32]{1,0:T(1,128)}) custom-call(f32[32,896]{1,0:T(8,128)S(1)} %add.5.mine_ref, f32[32,896]{1,0:T(8,128)S(1)} %collective-permute-done.14.other_ref), custom_call_target="tpu_custom_call" | custom-call | tf_op jit(solution)/shard_map/spread/pallas_call | solution.py:450
  (40 shorter events, 2.4 us)
Async XLA Ops:
  0.6 1.0 %copy-start = (bf16[1,32,5,8,128]{4,3,2,1,0:T(8,128)(2,1)S(1)}, bf16[1,32,5,8,128]{4,3,2,1,0:T(8,128)(2,1)}, u32[]{:S(2)}) copy-start(bf16[1,32,5,8,128]{4,3,2,1,0:T(8,128)(2,1)} %f_any.1) | copy-start | bytes 983044
  1.6 1.0 %copy-start.1 = (bf16[1,32,5,8,128]{4,3,2,1,0:T(8,128)(2,1)S(1)}, bf16[1,32,5,8,128]{4,3,2,1,0:T(8,128)(2,1)}, u32[]{:S(2)}) copy-start(bf16[1,32,5,8,128]{4,3,2,1,0:T(8,128)(2,1)} %g_any.1) | copy-start | bytes 983044
  5.2 15.1 %collective-permute-start = (bf16[512,128]{1,0:T(8,128)(2,1)}, bf16[512,128]{1,0:T(8,128)(2,1)S(1)}, u32[]{:S(2)}, u32[]{:S(2)}) collective-permute-start(bf16[512,128]{1,0:T(8,128)(2,1)} %get-tuple-element.32), channel_id=1, source_target_pairs={{0,2},{1,3},{2,0},{3,1},{4,6},{5,7},{6,4},{7,5},{8,10},{9,11},{10,... | collective-permute-start | bytes 393224 | tf_op jit(solution)/shard_map/ppermute | solution.py:371
  8.2 12.0 %collective-permute-start.1 = (bf16[512,128]{1,0:T(8,128)(2,1)}, bf16[512,128]{1,0:T(8,128)(2,1)S(1)}, u32[]{:S(2)}, u32[]{:S(2)}) collective-permute-start(bf16[512,128]{1,0:T(8,128)(2,1)} %get-tuple-element.33), channel_id=1, source_target_pairs={{0,6},{1,7},{2,4},{3,5},{4,2},{5,3},{6,0},{7,1},{8,14},{9,15},{10,... | collective-permute-start | bytes 393224 | tf_op jit(solution)/shard_map/ppermute | solution.py:371
  10.7 8.9 %collective-permute-start.2 = (bf16[32,256]{1,0:T(8,128)(2,1)S(1)}, bf16[32,256]{1,0:T(8,128)(2,1)S(1)}, u32[]{:S(2)}, u32[]{:S(2)}) collective-permute-start(bf16[32,256]{1,0:T(8,128)(2,1)S(1)} %get-tuple-element.34), channel_id=1, source_target_pairs={{0,1},{1,0},{2,3},{3,2},{4,5},{5,4},{6,7},{7,6},{8,9},{9,8},{10,11... | collective-permute-start | bytes 49160 | tf_op jit(solution)/shard_map/ppermute | solution.py:371
  12.2 7.4 %collective-permute-start.3 = (bf16[32,256]{1,0:T(8,128)(2,1)S(1)}, bf16[32,256]{1,0:T(8,128)(2,1)S(1)}, u32[]{:S(2)}, u32[]{:S(2)}) collective-permute-start(bf16[32,256]{1,0:T(8,128)(2,1)S(1)} %get-tuple-element.34), channel_id=1, source_target_pairs={{0,3},{1,2},{2,1},{3,0},{4,7},{5,6},{6,5},{7,4},{8,11},{9,10},{10,... | collective-permute-start | bytes 49160 | tf_op jit(solution)/shard_map/ppermute | solution.py:371
  12.9 6.8 %collective-permute-start.4 = (bf16[32,256]{1,0:T(8,128)(2,1)S(1)}, bf16[32,256]{1,0:T(8,128)(2,1)S(1)}, u32[]{:S(2)}, u32[]{:S(2)}) collective-permute-start(bf16[32,256]{1,0:T(8,128)(2,1)S(1)} %get-tuple-element.34), channel_id=1, source_target_pairs={{0,7},{1,6},{2,5},{3,4},{4,3},{5,2},{6,1},{7,0},{8,15},{9,14},{10,... | collective-permute-start | bytes 49160 | tf_op jit(solution)/shard_map/ppermute | solution.py:371
  14.7 0.9 %copy-start.9 = (bf16[32,3,3,3,32]{4,0,3,2,1:T(8,128)(2,1)S(1)}, bf16[32,3,3,3,32]{4,0,3,2,1:T(8,128)(2,1)}, u32[]{:S(2)}) copy-start(bf16[32,3,3,3,32]{4,0,3,2,1:T(8,128)(2,1)} %param.7) | copy-start | bytes 165892
  15.6 0.9 %copy-start.10 = (bf16[32,3,3,3,32]{4,0,3,2,1:T(8,128)(2,1)S(1)}, bf16[32,3,3,3,32]{4,0,3,2,1:T(8,128)(2,1)}, u32[]{:S(2)}) copy-start(bf16[32,3,3,3,32]{4,0,3,2,1:T(8,128)(2,1)} %param.9) | copy-start | bytes 165892
  16.6 2.9 %copy-start.13 = (f32[32]{0:T(128)S(1)}, f32[32]{0:T(128)}, u32[]{:S(2)}) copy-start(f32[32]{0:T(128)} %param.8) | copy-start | bytes 388
  18.5 1.0 %copy-start.11 = (bf16[3,256,768]{2,1,0:T(8,128)(2,1)}, bf16[3,256,768]{2,1,0:T(8,128)(2,1)S(1)}, u32[]{:S(2)}) copy-start(bf16[3,256,768]{2,1,0:T(8,128)(2,1)S(1)} %get-tuple-element.37.t2_ref) | copy-start | bytes 3538948
  19.7 0.6 %copy-start.2 = (bf16[32,256]{1,0:T(8,128)(2,1)}, bf16[32,256]{1,0:T(8,128)(2,1)S(1)}, u32[]{:S(2)}) copy-start(bf16[32,256]{1,0:T(8,128)(2,1)S(1)} %collective-permute-done.4.edge_two_ref) | copy-start | bytes 49156
  20.3 0.7 %copy-start.3 = (bf16[32,256]{1,0:T(8,128)(2,1)S(1)}, bf16[32,256]{1,0:T(8,128)(2,1)}, u32[]{:S(2)}) copy-start(bf16[32,256]{1,0:T(8,128)(2,1)} %copy-done.2) | copy-start | bytes 49156
  21.0 10.2 %copy-start.14 = (f32[32]{0:T(128)S(1)}, f32[32]{0:T(128)}, u32[]{:S(2)}) copy-start(f32[32]{0:T(128)} %param.10) | copy-start | bytes 388
  26.5 1.1 %copy-start.5 = (bf16[768,896]{1,0:T(8,128)(2,1)}, bf16[768,896]{1,0:T(8,128)(2,1)S(1)}, u32[]{:S(2)}) copy-start(bf16[768,896]{1,0:T(8,128)(2,1)S(1)} %get-tuple-element.39.fs_ref) | copy-start | bytes 4128772
  27.6 0.7 %copy-start.7 = (bf16[256,640]{1,0:T(8,128)(2,1)}, bf16[256,640]{1,0:T(8,128)(2,1)S(1)}, u32[]{:S(2)}) copy-start(bf16[256,640]{1,0:T(8,128)(2,1)S(1)} %get-tuple-element.38.h_ref) | copy-start | bytes 983044
  28.3 3.1 %collective-permute-start.5 = (f32[32,896]{1,0:T(8,128)}, f32[32,896]{1,0:T(8,128)S(1)}, u32[]{:S(2)}, u32[]{:S(2)}) collective-permute-start(f32[32,896]{1,0:T(8,128)} %get-tuple-element.36), channel_id=1, source_target_pairs={{0,8},{1,9},{2,10},{3,11},{4,12},{5,13},{6,14},{7,15},{8,0},{9,1},... | collective-permute-start | bytes 344072 | tf_op jit(solution)/shard_map/ppermute | solution.py:371
  28.3 6.9 %collective-permute-start.10 = (bf16[256,128]{1,0:T(8,128)(2,1)}, bf16[256,128]{1,0:T(8,128)(2,1)S(1)}, u32[]{:S(2)}, u32[]{:S(2)}) collective-permute-start(bf16[256,128]{1,0:T(8,128)(2,1)} %get-tuple-element.41), channel_id=1, source_target_pairs={{0,6},{1,7},{2,4},{3,5},{4,2},{5,3},{6,0},{7,1},{8,14},{9,15},{10,... | collective-permute-start | bytes 196616 | tf_op jit(solution)/shard_map/ppermute | solution.py:371
  31.2 5.0 %collective-permute-start.9 = (bf16[256,128]{1,0:T(8,128)(2,1)}, bf16[256,128]{1,0:T(8,128)(2,1)S(1)}, u32[]{:S(2)}, u32[]{:S(2)}) collective-permute-start(bf16[256,128]{1,0:T(8,128)(2,1)} %get-tuple-element.40), channel_id=1, source_target_pairs={{0,2},{1,3},{2,0},{3,1},{4,6},{5,7},{6,4},{7,5},{8,10},{9,11},{10,... | collective-permute-start | bytes 196616 | tf_op jit(solution)/shard_map/ppermute | solution.py:371
  31.5 12.5 %collective-permute-start.6 = (bf16[32,896]{1,0:T(8,128)(2,1)S(1)}, bf16[32,896]{1,0:T(8,128)(2,1)S(1)}, u32[]{:S(2)}, u32[]{:S(2)}) collective-permute-start(bf16[32,896]{1,0:T(8,128)(2,1)S(1)} %add.3.refs_0_), channel_id=1, source_target_pairs={{0,16},{1,17},{2,18},{3,19},{4,20},{5,21},{6,22},{7,23},{8,24},{9,... | collective-permute-start | bytes 172040 | tf_op jit(solution)/shard_map/ppermute | solution.py:371
  33.0 11.0 %collective-permute-start.7 = (bf16[32,896]{1,0:T(8,128)(2,1)S(1)}, bf16[32,896]{1,0:T(8,128)(2,1)S(1)}, u32[]{:S(2)}, u32[]{:S(2)}) collective-permute-start(bf16[32,896]{1,0:T(8,128)(2,1)S(1)} %add.3.refs_0_), channel_id=1, source_target_pairs={{0,1},{1,0},{2,3},{3,2},{4,5},{5,4},{6,7},{7,6},{8,9},{9,8},{10,11... | collective-permute-start | bytes 172040 | tf_op jit(solution)/shard_map/ppermute | solution.py:371
  33.6 10.4 %collective-permute-start.8 = (bf16[32,896]{1,0:T(8,128)(2,1)S(1)}, bf16[32,896]{1,0:T(8,128)(2,1)S(1)}, u32[]{:S(2)}, u32[]{:S(2)}) collective-permute-start(bf16[32,896]{1,0:T(8,128)(2,1)S(1)} %add.3.refs_0_), channel_id=1, source_target_pairs={{0,17},{1,16},{2,19},{3,18},{4,21},{5,20},{6,23},{7,22},{8,25},{9,... | collective-permute-start | bytes 172040 | tf_op jit(solution)/shard_map/ppermute | solution.py:371
  36.2 0.7 %copy-start.4 = (bf16[32,256]{1,0:T(8,128)(2,1)S(1)}, bf16[32,256]{1,0:T(8,128)(2,1)}, u32[]{:S(2)}) copy-start(bf16[32,256]{1,0:T(8,128)(2,1)} %copy-done.2) | copy-start | bytes 49156
  36.9 1.3 %copy-start.6 = (bf16[768,896]{1,0:T(8,128)(2,1)S(1)}, bf16[768,896]{1,0:T(8,128)(2,1)}, u32[]{:S(2)}) copy-start(bf16[768,896]{1,0:T(8,128)(2,1)} %copy-done.5) | copy-start | bytes 4128772
  38.3 1.0 %copy-start.8 = (bf16[256,640]{1,0:T(8,128)(2,1)S(1)}, bf16[256,640]{1,0:T(8,128)(2,1)}, u32[]{:S(2)}) copy-start(bf16[256,640]{1,0:T(8,128)(2,1)} %copy-done.7) | copy-start | bytes 983044
  39.2 1.3 %copy-start.12 = (bf16[3,256,768]{2,1,0:T(8,128)(2,1)S(1)}, bf16[3,256,768]{2,1,0:T(8,128)(2,1)}, u32[]{:S(2)}) copy-start(bf16[3,256,768]{2,1,0:T(8,128)(2,1)} %copy-done.11) | copy-start | bytes 3538948
  44.2 4.7 %collective-permute-start.11 = (bf16[32,896]{1,0:T(8,128)(2,1)S(1)}, bf16[32,896]{1,0:T(8,128)(2,1)S(1)}, u32[]{:S(2)}, u32[]{:S(2)}) collective-permute-start(bf16[32,896]{1,0:T(8,128)(2,1)S(1)} %add.4.refs_0_), channel_id=1, source_target_pairs={{0,2},{1,3},{2,0},{3,1},{4,6},{5,7},{6,4},{7,5},{8,10},{9,11},{10,... | collective-permute-start | bytes 172040 | tf_op jit(solution)/shard_map/ppermute | solution.py:371
  45.3 6.6 %collective-permute-start.12 = (bf16[32,896]{1,0:T(8,128)(2,1)S(1)}, bf16[32,896]{1,0:T(8,128)(2,1)S(1)}, u32[]{:S(2)}, u32[]{:S(2)}) collective-permute-start(bf16[32,896]{1,0:T(8,128)(2,1)S(1)} %add.4.refs_0_), channel_id=1, source_target_pairs={{0,4},{1,5},{2,6},{3,7},{4,0},{5,1},{6,2},{7,3},{8,12},{9,13},{10,... | collective-permute-start | bytes 172040 | tf_op jit(solution)/shard_map/ppermute | solution.py:371
  46.7 6.1 %collective-permute-start.13 = (bf16[32,896]{1,0:T(8,128)(2,1)S(1)}, bf16[32,896]{1,0:T(8,128)(2,1)S(1)}, u32[]{:S(2)}, u32[]{:S(2)}) collective-permute-start(bf16[32,896]{1,0:T(8,128)(2,1)S(1)} %add.4.refs_0_), channel_id=1, source_target_pairs={{0,6},{1,7},{2,4},{3,5},{4,2},{5,3},{6,0},{7,1},{8,14},{9,15},{10,... | collective-permute-start | bytes 172040 | tf_op jit(solution)/shard_map/ppermute | solution.py:371
  52.8 1.3 %collective-permute-start.14 = (f32[32,896]{1,0:T(8,128)S(1)}, f32[32,896]{1,0:T(8,128)S(1)}, u32[]{:S(2)}, u32[]{:S(2)}) collective-permute-start(f32[32,896]{1,0:T(8,128)S(1)} %add.5.mine_ref), channel_id=1, source_target_pairs={{0,8},{1,9},{2,10},{3,11},{4,12},{5,13},{6,14},{7,15},{8,0},{9,1},... | collective-permute-start | bytes 344072 | tf_op jit(solution)/shard_map/ppermute | solution.py:371

commit v3 on v2

--- a/solution.py
+++ b/solution.py
@@ -30,8 +30,16 @@
     return jnp.where(hit, 1.0, 0.0).astype(BF)
 
 
-def params():
-    return pltpu.CompilerParams(vmem_limit_bytes=20 * 2**20)
+def params(mib=8):
+    return pltpu.CompilerParams(vmem_limit_bytes=mib * 2**20)
+
+
+def in_vmem(*arrays):
+    return [pltpu.with_memory_space_constraint(array, pltpu.VMEM) for array in arrays]
+
+
+def in_hbm(*arrays):
+    return [pltpu.with_memory_space_constraint(array, pltpu.HBM) for array in arrays]
 
 
 def is_even(axis):
@@ -82,7 +90,7 @@
     _, ch, nx, ny, _ = features.shape
     rows = ch * ny
     edge_rows = -(-6 * nx // 32) * 32
-    sds = jax.ShapeDtypeStruct
+    sds = pltpu.VMEM
     anywhere = pl.BlockSpec(memory_space=pl.ANY)
     return pl.pallas_call(
         functools.partial(pack_kernel, nx, ch, ny),
@@ -101,12 +109,18 @@
             pltpu.VMEM((rows, nx * LANES), BF),
             pltpu.SemaphoreType.DMA((8,)),
         ],
-        compiler_params=params(),
+        compiler_params=params(4),
         name="pack",
-    )(features, cotangent)
-
-
-def bands_kernel(ny, w1_ref, w2_ref, t1_ref, tv_ref, t2_ref):
+    )(*in_hbm(features, cotangent))
+
+
+def bands_kernel(ny, w1_any, w2_any, t1_ref, tv_ref, t2_ref, held, sems):
+    copies = [pltpu.make_async_copy(src, held.at[i], sems.at[i]) for i, src in enumerate((w1_any, w2_any))]
+    for copy in copies:
+        copy.start()
+    for copy in copies:
+        copy.wait()
+    w1_ref, w2_ref = held.at[0], held.at[1]
     ch = w1_ref.shape[-1]
     rows = ny * ch
     lane = iota((ch, rows), 1)
@@ -139,11 +153,13 @@
     laid = lambda weight: jnp.transpose(weight, (1, 2, 3, 0, 4))
     return pl.pallas_call(
         functools.partial(bands_kernel, ny),
-        out_shape=(jax.ShapeDtypeStruct((3, rows, 3 * rows), BF),) * 3,
-        compiler_params=params(),
+        in_specs=[pl.BlockSpec(memory_space=pl.ANY)] * 2,
+        scratch_shapes=[pltpu.VMEM((2, 3, 3, 3, ch, ch), BF), pltpu.SemaphoreType.DMA((2,))],
+        out_shape=(pltpu.VMEM((3, rows, 3 * rows), BF),) * 3,
+        compiler_params=params(3),
         cost_estimate=pl.CostEstimate(flops=1_000_000_000, bytes_accessed=4_000_000, transcendentals=0),
         name="bands",
-    )(laid(first_weight), laid(second_weight))
+    )(*in_hbm(laid(first_weight), laid(second_weight)))
 
 
 def shifted_rows(out, row, block, before, after, rows):
@@ -201,6 +217,13 @@
     return (preact / (1.0 + jnp.exp(-preact))).astype(BF)
 
 
+def bias_column(ref, ny):
+    ch = ref.shape[1]
+    r, k = iota((ch, ch), 0), iota((ch, ch), 1)
+    column = jnp.sum(jnp.where(r == k, ref[...], 0.0), axis=1, keepdims=True)
+    return jnp.concatenate([column] * ny, axis=0)
+
+
 def sides(even, one, two):
     return jnp.where(even, two, one), jnp.where(even, one, two)
 
@@ -242,7 +265,7 @@
     acc = mm(t1_ref[0], fs[:, 0:n5])
     for a in range(1, 3):
         acc = acc + mm(t1_ref[a], fs[:, a * LANES : a * LANES + n5])
-    preact = acc + bias_ref[...]
+    preact = acc + bias_column(bias_ref, ny)
     pre[...] = preact
     hid_ref[...] = silu(preact)
     hidden = hid_ref[...]
@@ -281,7 +304,7 @@
 def main(t1, tv, field, cot, one, two, near, edge_one, edge_two, bias, ch, ny, scale):
     rows = ch * ny
     nx = field.shape[1] // LANES
-    sds = jax.ShapeDtypeStruct
+    sds = pltpu.VMEM
     return pl.pallas_call(
         functools.partial(main_kernel, nx, ch, ny, scale),
         out_shape=(
@@ -294,9 +317,9 @@
             pltpu.VMEM((3 * rows, (nx + 2) * LANES), BF),
             pltpu.VMEM((rows, nx * LANES), F32),
         ],
-        compiler_params=params(),
+        compiler_params=params(8),
         name="main",
-    )(t1, tv, field, cot, one, two, near, edge_one, edge_two, bias)
+    )(*in_vmem(t1, tv, field, cot, one, two, near, edge_one, edge_two, bias))
 
 
 def residual_kernel(
@@ -325,7 +348,7 @@
         columns = [lane_to(edges, 16 * c + a, 0).astype(BF) for c in range(3)]
         term = mm(t1_ref[a], jnp.concatenate([*pairs[a], jnp.concatenate(columns, axis=0)], axis=1))
         acc = term if acc is None else acc + term
-    hidden = silu(acc + bias1_ref[...])
+    hidden = silu(acc + bias_column(bias1_ref, ny))
     outer = hidden[:, 2 * LANES :].astype(F32)
     for x in range(nx + 2):
         if x == 0:
@@ -339,7 +362,7 @@
     acc = mm(t2_ref[0], hs[:, 0:n5])
     for a in range(1, 3):
         acc = acc + mm(t2_ref[a], hs[:, a * LANES : a * LANES + n5])
-    total = (f_ref[...].astype(F32) + (acc + bias2_ref[...])).astype(BF)
+    total = (f_ref[...].astype(F32) + (acc + bias_column(bias2_ref, ny))).astype(BF)
     r, k = iota((rows, rows), 0), iota((rows, rows), 1)
     back = one_hot(k == (r % ny) * ch + r // ny)
     ordered = mm(back, total)
@@ -354,10 +377,10 @@
         functools.partial(residual_kernel, nx, ch, ny),
         out_shape=jax.ShapeDtypeStruct((1, ch, nx, ny, LANES), BF),
         scratch_shapes=[pltpu.VMEM((3 * rows, 2 * LANES), BF), pltpu.VMEM((3 * rows, (nx + 2) * LANES), BF)],
-        compiler_params=params(),
+        compiler_params=params(8),
         cost_estimate=pl.CostEstimate(flops=3_000_000_000, bytes_accessed=3_000_000, transcendentals=0),
         name="residual",
-    )(t1, t2, hidden, fs, field, far_one, far_two, near, edge_one, edge_two, bias1, bias2)
+    )(*in_vmem(t1, t2, hidden, fs, field, far_one, far_two, near, edge_one, edge_two, bias1, bias2))
 
 
 def moved(array, sizes, step):
@@ -401,10 +424,10 @@
 def add(terms, dtype):
     return pl.pallas_call(
         functools.partial(add_kernel, len(terms)),
-        out_shape=jax.ShapeDtypeStruct(terms[0].shape, dtype),
-        compiler_params=params(),
+        out_shape=pltpu.VMEM(terms[0].shape, dtype),
+        compiler_params=params(1),
         name="add",
-    )(*terms)
+    )(*in_vmem(*terms))
 
 
 def exchange(sent, sizes, pair):
@@ -450,9 +473,9 @@
     first, first_bias, second, second_bias = pl.pallas_call(
         functools.partial(spread_kernel, ch),
         out_shape=(taps, bias, taps, bias),
-        compiler_params=params(),
+        compiler_params=params(4),
         name="spread",
-    )(mine, other)
+    )(*in_vmem(mine, other))
     laid = lambda grad: jnp.transpose(grad, (3, 0, 1, 2, 4))
     return laid(first), first_bias.reshape(ch), laid(second), second_bias.reshape(ch)
 
@@ -469,8 +492,7 @@
     edge_one, edge_two = paired(edge, sizes, 0, 1), paired(edge, sizes, 1, 1)
     far_one, far_two = paired(far_one, sizes, 0, 0), paired(far_two, sizes, 1, 0)
     t1, tv, t2 = bands(first_weight, second_weight, ny)
-    column = lambda bias: jnp.tile(bias, ny)[:, None]
-    bias1, bias2 = column(first_bias), column(second_bias)
+    bias1, bias2 = first_bias.reshape(1, ch), second_bias.reshape(1, ch)
     hidden, fs, keep, give = main(t1, tv, field, cot, one, two, near, edge_one, edge_two, bias1, ch, ny, scale)
     output = residual(t1, t2, hidden, fs, field, far_one, far_two, near, edge_one, edge_two, bias1, bias2, ch, ny)
     mine, other, output = sum_all(keep, give, sizes, output)

time: 55.8 us -> 42.8 us (0.77)
  local copies, waits for them, and re-layouts: 12.5 us -> 0.01 us
    unnamed x30 -> x4, local copies, waits for them, and re-layouts: 12.3 us -> 0.01 us
    pallas_call x4, Pallas kernels: 2.32 us -> 3.43 us  [the longest x1 3.01 us: bands(): pl.pallas_call(functools.partial(bands_kernel, ny), in_specs=[pl.BlockSpe...]
  transfers between devices with their start and end apart: 15 -> 15, of which waited for: 6 -> 6; matrix products, arithmetic and copies ran while one was open for 0% -> 0% of each run, Pallas kernels for 10% -> 16%
where the time goes in v3:
time: 42.8 us; the launch traced here: 42.6 us
  starting transfers between devices  20.3 us (47%)
  Pallas kernels  15.2 us (36%)
  waiting for transfers between devices  6.45 us (15%)
  between operations  0.7 us (2%)
    ppermute x15, starting transfers between devices, moved(): return lax.ppermute(array, AXES, pairs)  20.3 us
    ppermute x15, waiting for transfers between devices, moved(): return lax.ppermute(array, AXES, pairs)  6.45 us
    pallas_call x1, Pallas kernels, main(): pl.pallas_call(functools.partial(main_kernel, nx, ch, ny, scale), out_sha...  4.94 us
    pallas_call x1, Pallas kernels, residual(): pl.pallas_call(functools.partial(residual_kernel, nx, ch, ny), out_shape=...  3.46 us
    pallas_call x1, Pallas kernels, bands(): pl.pallas_call(functools.partial(bands_kernel, ny), in_specs=[pl.BlockSpe...  3.01 us
    pallas_call x1, Pallas kernels, pack(): pl.pallas_call(functools.partial(pack_kernel, nx, ch, ny), out_shape=(sds...  2.14 us
    pallas_call x1, Pallas kernels, spread(): pl.pallas_call(functools.partial(spread_kernel, ch), out_shape=(taps, bia...  1.2 us
  transfers between devices with their start and end apart: 15, of which 6 were waited for; matrix products, arithmetic and copies ran while one was open for 0% of the time, Pallas kernels for 16%

profile of v3, /device:TPU:0, one launch (start us, length us, event | category | flops | bytes accessed | tf_op | source)
XLA Modules:
  0.0 42.6 jit_solution(17740551554867779123)
XLA Ops:
  0.6 2.1 %pack.1 = (bf16[256,640]{1,0:T(8,128)(2,1)S(1)}, bf16[256,640]{1,0:T(8,128)(2,1)S(1)}, bf16[512,128]{1,0:T(8,128)(2,1)S(1)}, bf16[512,128]{1,0:T(8,128)(2,1)S(1)...) custom-call(bf16[1,32,5,8,128]{4,3,2,1,0:T(8,128)(2,1)} %f_any.1, ...), custom_call_target="tpu_custom_call" | custom-call | tf_op jit(solution)/shard_map/pack/pallas_call | solution.py:95
  2.8 3.1 %collective-permute-start = (bf16[512,128]{1,0:T(8,128)(2,1)S(1)}, bf16[512,128]{1,0:T(8,128)(2,1)S(1)}, u32[]{:S(2)}, u32[]{:S(2)}) collective-permute-start(bf16[512,128]{1,0:T(8,128)(2,1)S(1)} %get-tuple-element.32), channel_id=1, source_target_pairs={{0,2},{1,3},{2,0},{3,1},{4,6},{5,7},{6,4},{7,5},{8,10},{9,11},{10,... | collective-permute-start | bytes 393224 | tf_op jit(solution)/shard_map/ppermute | solution.py:394
  5.9 2.5 %collective-permute-start.1 = (bf16[512,128]{1,0:T(8,128)(2,1)S(1)}, bf16[512,128]{1,0:T(8,128)(2,1)S(1)}, u32[]{:S(2)}, u32[]{:S(2)}) collective-permute-start(bf16[512,128]{1,0:T(8,128)(2,1)S(1)} %get-tuple-element.33), channel_id=1, source_target_pairs={{0,6},{1,7},{2,4},{3,5},{4,2},{5,3},{6,0},{7,1},{8,14},{9,15},{10,... | collective-permute-start | bytes 393224 | tf_op jit(solution)/shard_map/ppermute | solution.py:394
  8.3 2.3 %collective-permute-start.4 = (bf16[32,256]{1,0:T(8,128)(2,1)S(1)}, bf16[32,256]{1,0:T(8,128)(2,1)S(1)}, u32[]{:S(2)}, u32[]{:S(2)}) collective-permute-start(bf16[32,256]{1,0:T(8,128)(2,1)S(1)} %get-tuple-element.34), channel_id=1, source_target_pairs={{0,7},{1,6},{2,5},{3,4},{4,3},{5,2},{6,1},{7,0},{8,15},{9,14},{10,... | collective-permute-start | bytes 49160 | tf_op jit(solution)/shard_map/ppermute | solution.py:394
  10.6 0.8 %collective-permute-start.2 = (bf16[32,256]{1,0:T(8,128)(2,1)S(1)}, bf16[32,256]{1,0:T(8,128)(2,1)S(1)}, u32[]{:S(2)}, u32[]{:S(2)}) collective-permute-start(bf16[32,256]{1,0:T(8,128)(2,1)S(1)} %get-tuple-element.34), channel_id=1, source_target_pairs={{0,1},{1,0},{2,3},{3,2},{4,5},{5,4},{6,7},{7,6},{8,9},{9,8},{10,11... | collective-permute-start | bytes 49160 | tf_op jit(solution)/shard_map/ppermute | solution.py:394
  11.4 3.0 %bands.1 = (bf16[3,256,768]{2,1,0:T(8,128)(2,1)S(1)}, bf16[3,256,768]{2,1,0:T(8,128)(2,1)S(1)}, bf16[3,256,768]{2,1,0:T(8,128)(2,1)S(1)}) custom-call(bf16[3,3,3,32,32]{4,3,2,1,0:T(8,128)(2,1)} %bitcast.13, bf16[3,3,3,32,32]{4,3,2,1,0:T(8,128)(2,1)} %bitcast.14), custom_call_target="tpu_custom_call" | custom-call | flops 1000000000 | bytes 4000000 | tf_op jit(solution)/shard_map/bands/pallas_call | solution.py:154
  14.4 1.5 %collective-permute-done.4.edge_two_ref = bf16[32,256]{1,0:T(8,128)(2,1)S(1)} collective-permute-done((bf16[32,256]{1,0:T(8,128)(2,1)S(1)}, bf16[32,256]{1,0:T(8,128)(2,1)S(1)}, u32[]{:S(2)}, u32[]{:S(2)}) %collective-permute-start.4) | collective-permute-done | bytes 16416 | tf_op jit(solution)/shard_map/ppermute | solution.py:394
  15.9 0.1 collective-permute-done.3.edge_one_ref
  16.0 0.0 collective-permute-done.2.near_ref
  16.0 0.0 copy-start.1
  16.1 4.9 %main.1 = (bf16[256,640]{1,0:T(8,128)(2,1)S(1)}, bf16[768,896]{1,0:T(8,128)(2,1)S(1)}, f32[32,896]{1,0:T(8,128)S(1)}, f32[32,896]{1,0:T(8,128)S(1)}) custom-call(bf16[3,256,768]{2,1,0:T(8,128)(2,1)S(1)} %get-tuple-element.28.t1_ref, bf16[3,256,768]{2,1,0:T(8,128)(2,1)S(1)} %get-tuple-element.29.tv_ref, bf16[256,640]{1,0:T(8,128)(2,1)S(1)} %get-tuple-element.30.f_ref, ...), custom_call_target="tpu_custom_call" | custom-call | tf_op jit(solution)/shard_map/main/pallas_call | solution.py:308
  21.0 0.1 collective-permute-start.5
  21.1 1.2 %collective-permute-start.9 = (bf16[256,128]{1,0:T(8,128)(2,1)S(1)}, bf16[256,128]{1,0:T(8,128)(2,1)S(1)}, u32[]{:S(2)}, u32[]{:S(2)}) collective-permute-start(bf16[256,128]{1,0:T(8,128)(2,1)S(1)} %get-tuple-element.40), channel_id=1, source_target_pairs={{0,2},{1,3},{2,0},{3,1},{4,6},{5,7},{6,4},{7,5},{8,10},{9,11},{10,... | collective-permute-start | bytes 196616 | tf_op jit(solution)/shard_map/ppermute | solution.py:394
  22.3 2.5 %collective-permute-start.10 = (bf16[256,128]{1,0:T(8,128)(2,1)S(1)}, bf16[256,128]{1,0:T(8,128)(2,1)S(1)}, u32[]{:S(2)}, u32[]{:S(2)}) collective-permute-start(bf16[256,128]{1,0:T(8,128)(2,1)S(1)} %get-tuple-element.41), channel_id=1, source_target_pairs={{0,6},{1,7},{2,4},{3,5},{4,2},{5,3},{6,0},{7,1},{8,14},{9,15},{10,... | collective-permute-start | bytes 196616 | tf_op jit(solution)/shard_map/ppermute | solution.py:394
  24.8 0.1 add.3.refs_0_
  24.9 1.6 %collective-permute-start.8 = (bf16[32,896]{1,0:T(8,128)(2,1)S(1)}, bf16[32,896]{1,0:T(8,128)(2,1)S(1)}, u32[]{:S(2)}, u32[]{:S(2)}) collective-permute-start(bf16[32,896]{1,0:T(8,128)(2,1)S(1)} %add.3.refs_0_), channel_id=1, source_target_pairs={{0,17},{1,16},{2,19},{3,18},{4,21},{5,20},{6,23},{7,22},{8,25},{9,... | collective-permute-start | bytes 172040 | tf_op jit(solution)/shard_map/ppermute | solution.py:394
  26.5 1.4 %collective-permute-start.7 = (bf16[32,896]{1,0:T(8,128)(2,1)S(1)}, bf16[32,896]{1,0:T(8,128)(2,1)S(1)}, u32[]{:S(2)}, u32[]{:S(2)}) collective-permute-start(bf16[32,896]{1,0:T(8,128)(2,1)S(1)} %add.3.refs_0_), channel_id=1, source_target_pairs={{0,1},{1,0},{2,3},{3,2},{4,5},{5,4},{6,7},{7,6},{8,9},{9,8},{10,11... | collective-permute-start | bytes 172040 | tf_op jit(solution)/shard_map/ppermute | solution.py:394
  27.9 0.5 %collective-permute-start.6 = (bf16[32,896]{1,0:T(8,128)(2,1)S(1)}, bf16[32,896]{1,0:T(8,128)(2,1)S(1)}, u32[]{:S(2)}, u32[]{:S(2)}) collective-permute-start(bf16[32,896]{1,0:T(8,128)(2,1)S(1)} %add.3.refs_0_), channel_id=1, source_target_pairs={{0,16},{1,17},{2,18},{3,19},{4,20},{5,21},{6,22},{7,23},{8,24},{9,... | collective-permute-start | bytes 172040 | tf_op jit(solution)/shard_map/ppermute | solution.py:394
  28.4 0.2 collective-permute-done.10.far_two_ref
  28.6 3.5 %residual.1 = bf16[1,32,5,8,128]{4,3,2,1,0:T(8,128)(2,1)} custom-call(bf16[3,256,768]{2,1,0:T(8,128)(2,1)S(1)} %get-tuple-element.28.t1_ref, bf16[3,256,768]{2,1,0:T(8,128)(2,1)S(1)} %get-tuple-element.37.t2_ref, bf16[256,640]{1,0:T(8,128)(2,1)S(1)} %get-tuple-element.38.h_ref, bf16[768,896]{1,0:T(8,128)(2,1)S(1)} %get-tuple-element.39.fs_ref, ...), custom_call_target="tpu_custom_call" | custom-call | flops 3000000000 | bytes 3000000 | tf_op jit(solution)/shard_map/residual/pallas_call | solution.py:376
  32.1 0.0 collective-permute-done.8.refs_3_
  32.1 0.0 collective-permute-done.6.refs_1_
  32.1 0.2 add.4.refs_0_
  32.3 2.2 %collective-permute-start.13 = (bf16[32,896]{1,0:T(8,128)(2,1)S(1)}, bf16[32,896]{1,0:T(8,128)(2,1)S(1)}, u32[]{:S(2)}, u32[]{:S(2)}) collective-permute-start(bf16[32,896]{1,0:T(8,128)(2,1)S(1)} %add.4.refs_0_), channel_id=1, source_target_pairs={{0,6},{1,7},{2,4},{3,5},{4,2},{5,3},{6,0},{7,1},{8,14},{9,15},{10,... | collective-permute-start | bytes 172040 | tf_op jit(solution)/shard_map/ppermute | solution.py:394
  34.5 0.0 collective-permute-start.12
  34.5 2.2 %collective-permute-start.11 = (bf16[32,896]{1,0:T(8,128)(2,1)S(1)}, bf16[32,896]{1,0:T(8,128)(2,1)S(1)}, u32[]{:S(2)}, u32[]{:S(2)}) collective-permute-start(bf16[32,896]{1,0:T(8,128)(2,1)S(1)} %add.4.refs_0_), channel_id=1, source_target_pairs={{0,2},{1,3},{2,0},{3,1},{4,6},{5,7},{6,4},{7,5},{8,10},{9,11},{10,... | collective-permute-start | bytes 172040 | tf_op jit(solution)/shard_map/ppermute | solution.py:394
  36.6 2.0 %collective-permute-done.13.refs_3_ = bf16[32,896]{1,0:T(8,128)(2,1)S(1)} collective-permute-done((bf16[32,896]{1,0:T(8,128)(2,1)S(1)}, bf16[32,896]{1,0:T(8,128)(2,1)S(1)}, u32[]{:S(2)}, u32[]{:S(2)}) %collective-permute-start.13) | collective-permute-done | bytes 57376 | tf_op jit(solution)/shard_map/ppermute | solution.py:394
  38.6 1.4 %collective-permute-done.12.refs_2_ = bf16[32,896]{1,0:T(8,128)(2,1)S(1)} collective-permute-done((bf16[32,896]{1,0:T(8,128)(2,1)S(1)}, bf16[32,896]{1,0:T(8,128)(2,1)S(1)}, u32[]{:S(2)}, u32[]{:S(2)}) %collective-permute-start.12) | collective-permute-done | bytes 57376 | tf_op jit(solution)/shard_map/ppermute | solution.py:394
  40.0 0.1 add.5.mine_ref
  40.1 0.0 collective-permute-start.14
  40.1 1.3 %collective-permute-done.14.other_ref = f32[32,896]{1,0:T(8,128)S(1)} collective-permute-done((f32[32,896]{1,0:T(8,128)S(1)}, f32[32,896]{1,0:T(8,128)S(1)}, u32[]{:S(2)}, u32[]{:S(2)}) %collective-permute-start.14) | collective-permute-done | bytes 114720 | tf_op jit(solution)/shard_map/ppermute | solution.py:394
  41.4 1.2 %spread.1 = (f32[3,3,3,32,32]{4,3,2,1,0:T(8,128)}, f32[1,32]{1,0:T(1,128)}, f32[3,3,3,32,32]{4,3,2,1,0:T(8,128)}, f32[1,32]{1,0:T(1,128)}) custom-call(f32[32,896]{1,0:T(8,128)S(1)} %add.5.mine_ref, f32[32,896]{1,0:T(8,128)S(1)} %collective-permute-done.14.other_ref), custom_call_target="tpu_custom_call" | custom-call | tf_op jit(solution)/shard_map/spread/pallas_call | solution.py:473
  (10 shorter events, 0.0 us)
Async XLA Ops:
  2.8 13.2 %collective-permute-start = (bf16[512,128]{1,0:T(8,128)(2,1)S(1)}, bf16[512,128]{1,0:T(8,128)(2,1)S(1)}, u32[]{:S(2)}, u32[]{:S(2)}) collective-permute-start(bf16[512,128]{1,0:T(8,128)(2,1)S(1)} %get-tuple-element.32), channel_id=1, source_target_pairs={{0,2},{1,3},{2,0},{3,1},{4,6},{5,7},{6,4},{7,5},{8,10},{9,11},{10,... | collective-permute-start | bytes 393224 | tf_op jit(solution)/shard_map/ppermute | solution.py:394
  5.9 10.2 %collective-permute-start.1 = (bf16[512,128]{1,0:T(8,128)(2,1)S(1)}, bf16[512,128]{1,0:T(8,128)(2,1)S(1)}, u32[]{:S(2)}, u32[]{:S(2)}) collective-permute-start(bf16[512,128]{1,0:T(8,128)(2,1)S(1)} %get-tuple-element.33), channel_id=1, source_target_pairs={{0,6},{1,7},{2,4},{3,5},{4,2},{5,3},{6,0},{7,1},{8,14},{9,15},{10,... | collective-permute-start | bytes 393224 | tf_op jit(solution)/shard_map/ppermute | solution.py:394
  8.3 7.6 %collective-permute-start.4 = (bf16[32,256]{1,0:T(8,128)(2,1)S(1)}, bf16[32,256]{1,0:T(8,128)(2,1)S(1)}, u32[]{:S(2)}, u32[]{:S(2)}) collective-permute-start(bf16[32,256]{1,0:T(8,128)(2,1)S(1)} %get-tuple-element.34), channel_id=1, source_target_pairs={{0,7},{1,6},{2,5},{3,4},{4,3},{5,2},{6,1},{7,0},{8,15},{9,14},{10,... | collective-permute-start | bytes 49160 | tf_op jit(solution)/shard_map/ppermute | solution.py:394
  10.6 5.4 %collective-permute-start.3 = (bf16[32,256]{1,0:T(8,128)(2,1)S(1)}, bf16[32,256]{1,0:T(8,128)(2,1)S(1)}, u32[]{:S(2)}, u32[]{:S(2)}) collective-permute-start(bf16[32,256]{1,0:T(8,128)(2,1)S(1)} %get-tuple-element.34), channel_id=1, source_target_pairs={{0,3},{1,2},{2,1},{3,0},{4,7},{5,6},{6,5},{7,4},{8,11},{9,10},{10,... | collective-permute-start | bytes 49160 | tf_op jit(solution)/shard_map/ppermute | solution.py:394
  10.6 5.4 %collective-permute-start.2 = (bf16[32,256]{1,0:T(8,128)(2,1)S(1)}, bf16[32,256]{1,0:T(8,128)(2,1)S(1)}, u32[]{:S(2)}, u32[]{:S(2)}) collective-permute-start(bf16[32,256]{1,0:T(8,128)(2,1)S(1)} %get-tuple-element.34), channel_id=1, source_target_pairs={{0,1},{1,0},{2,3},{3,2},{4,5},{5,4},{6,7},{7,6},{8,9},{9,8},{10,11... | collective-permute-start | bytes 49160 | tf_op jit(solution)/shard_map/ppermute | solution.py:394
  11.4 4.6 %copy-start = (f32[32]{0:T(128)S(1)}, f32[32]{0:T(128)}, u32[]{:S(2)}) copy-start(f32[32]{0:T(128)} %param.8) | copy-start | bytes 388
  16.0 12.5 %copy-start.1 = (f32[32]{0:T(128)S(1)}, f32[32]{0:T(128)}, u32[]{:S(2)}) copy-start(f32[32]{0:T(128)} %param.10) | copy-start | bytes 388
  21.0 3.8 %collective-permute-start.5 = (f32[32,896]{1,0:T(8,128)S(1)}, f32[32,896]{1,0:T(8,128)S(1)}, u32[]{:S(2)}, u32[]{:S(2)}) collective-permute-start(f32[32,896]{1,0:T(8,128)S(1)} %get-tuple-element.36), channel_id=1, source_target_pairs={{0,8},{1,9},{2,10},{3,11},{4,12},{5,13},{6,14},{7,15},{8,0},{9,1},... | collective-permute-start | bytes 344072 | tf_op jit(solution)/shard_map/ppermute | solution.py:394
  21.1 7.3 %collective-permute-start.9 = (bf16[256,128]{1,0:T(8,128)(2,1)S(1)}, bf16[256,128]{1,0:T(8,128)(2,1)S(1)}, u32[]{:S(2)}, u32[]{:S(2)}) collective-permute-start(bf16[256,128]{1,0:T(8,128)(2,1)S(1)} %get-tuple-element.40), channel_id=1, source_target_pairs={{0,2},{1,3},{2,0},{3,1},{4,6},{5,7},{6,4},{7,5},{8,10},{9,11},{10,... | collective-permute-start | bytes 196616 | tf_op jit(solution)/shard_map/ppermute | solution.py:394
  22.3 6.3 %collective-permute-start.10 = (bf16[256,128]{1,0:T(8,128)(2,1)S(1)}, bf16[256,128]{1,0:T(8,128)(2,1)S(1)}, u32[]{:S(2)}, u32[]{:S(2)}) collective-permute-start(bf16[256,128]{1,0:T(8,128)(2,1)S(1)} %get-tuple-element.41), channel_id=1, source_target_pairs={{0,6},{1,7},{2,4},{3,5},{4,2},{5,3},{6,0},{7,1},{8,14},{9,15},{10,... | collective-permute-start | bytes 196616 | tf_op jit(solution)/shard_map/ppermute | solution.py:394
  24.9 7.1 %collective-permute-start.8 = (bf16[32,896]{1,0:T(8,128)(2,1)S(1)}, bf16[32,896]{1,0:T(8,128)(2,1)S(1)}, u32[]{:S(2)}, u32[]{:S(2)}) collective-permute-start(bf16[32,896]{1,0:T(8,128)(2,1)S(1)} %add.3.refs_0_), channel_id=1, source_target_pairs={{0,17},{1,16},{2,19},{3,18},{4,21},{5,20},{6,23},{7,22},{8,25},{9,... | collective-permute-start | bytes 172040 | tf_op jit(solution)/shard_map/ppermute | solution.py:394
  26.5 5.5 %collective-permute-start.7 = (bf16[32,896]{1,0:T(8,128)(2,1)S(1)}, bf16[32,896]{1,0:T(8,128)(2,1)S(1)}, u32[]{:S(2)}, u32[]{:S(2)}) collective-permute-start(bf16[32,896]{1,0:T(8,128)(2,1)S(1)} %add.3.refs_0_), channel_id=1, source_target_pairs={{0,1},{1,0},{2,3},{3,2},{4,5},{5,4},{6,7},{7,6},{8,9},{9,8},{10,11... | collective-permute-start | bytes 172040 | tf_op jit(solution)/shard_map/ppermute | solution.py:394
  27.9 4.2 %collective-permute-start.6 = (bf16[32,896]{1,0:T(8,128)(2,1)S(1)}, bf16[32,896]{1,0:T(8,128)(2,1)S(1)}, u32[]{:S(2)}, u32[]{:S(2)}) collective-permute-start(bf16[32,896]{1,0:T(8,128)(2,1)S(1)} %add.3.refs_0_), channel_id=1, source_target_pairs={{0,16},{1,17},{2,18},{3,19},{4,20},{5,21},{6,22},{7,23},{8,24},{9,... | collective-permute-start | bytes 172040 | tf_op jit(solution)/shard_map/ppermute | solution.py:394
  32.3 6.4 %collective-permute-start.13 = (bf16[32,896]{1,0:T(8,128)(2,1)S(1)}, bf16[32,896]{1,0:T(8,128)(2,1)S(1)}, u32[]{:S(2)}, u32[]{:S(2)}) collective-permute-start(bf16[32,896]{1,0:T(8,128)(2,1)S(1)} %add.4.refs_0_), channel_id=1, source_target_pairs={{0,6},{1,7},{2,4},{3,5},{4,2},{5,3},{6,0},{7,1},{8,14},{9,15},{10,... | collective-permute-start | bytes 172040 | tf_op jit(solution)/shard_map/ppermute | solution.py:394
  34.5 5.5 %collective-permute-start.12 = (bf16[32,896]{1,0:T(8,128)(2,1)S(1)}, bf16[32,896]{1,0:T(8,128)(2,1)S(1)}, u32[]{:S(2)}, u32[]{:S(2)}) collective-permute-start(bf16[32,896]{1,0:T(8,128)(2,1)S(1)} %add.4.refs_0_), channel_id=1, source_target_pairs={{0,4},{1,5},{2,6},{3,7},{4,0},{5,1},{6,2},{7,3},{8,12},{9,13},{10,... | collective-permute-start | bytes 172040 | tf_op jit(solution)/shard_map/ppermute | solution.py:394
  34.5 5.5 %collective-permute-start.11 = (bf16[32,896]{1,0:T(8,128)(2,1)S(1)}, bf16[32,896]{1,0:T(8,128)(2,1)S(1)}, u32[]{:S(2)}, u32[]{:S(2)}) collective-permute-start(bf16[32,896]{1,0:T(8,128)(2,1)S(1)} %add.4.refs_0_), channel_id=1, source_target_pairs={{0,2},{1,3},{2,0},{3,1},{4,6},{5,7},{6,4},{7,5},{8,10},{9,11},{10,... | collective-permute-start | bytes 172040 | tf_op jit(solution)/shard_map/ppermute | solution.py:394
  40.1 1.3 %collective-permute-start.14 = (f32[32,896]{1,0:T(8,128)S(1)}, f32[32,896]{1,0:T(8,128)S(1)}, u32[]{:S(2)}, u32[]{:S(2)}) collective-permute-start(f32[32,896]{1,0:T(8,128)S(1)} %add.5.mine_ref), channel_id=1, source_target_pairs={{0,8},{1,9},{2,10},{3,11},{4,12},{5,13},{6,14},{7,15},{8,0},{9,1},... | collective-permute-start | bytes 344072 | tf_op jit(solution)/shard_map/ppermute | solution.py:394

commit v4 on v3

v4 whole, which is shorter than its diff:
```python
import functools

import jax
import jax.numpy as jnp
from jax import lax
from jax.experimental import pallas as pl
from jax.experimental.pallas import tpu as pltpu
from jax.sharding import PartitionSpec as P

AXES = ("smp", "gx", "gz")
BF = jnp.bfloat16
F32 = jnp.float32
LANES = 128
TERMS = 896


def mm(a, b):
    return lax.dot_general(a, b, (((1,), (0,)), ((), ())), preferred_element_type=F32)


def mm_nt(a, b):
    return lax.dot_general(a, b, (((1,), (1,)), ((), ())), preferred_element_type=F32)


def iota(shape, dim):
    return lax.broadcasted_iota(jnp.int32, shape, dim)


def one_hot(hit):
    return jnp.where(hit, 1.0, 0.0).astype(BF)


def params(mib=8):
    return pltpu.CompilerParams(vmem_limit_bytes=mib * 2**20)


def in_vmem(*arrays):
    return [pltpu.with_memory_space_constraint(array, pltpu.VMEM) for array in arrays]


def in_hbm(*arrays):
    return [pltpu.with_memory_space_constraint(array, pltpu.HBM) for array in arrays]


def is_even(axis):
    return lax.axis_index(axis) % 2 == 0


def ordered(ch, ny):
    r, k = iota((ch * ny, ch * ny), 0), iota((ch * ny, ch * ny), 1)
    return one_hot(k == (r % ch) * ny + r // ch)


def faces_kernel(nx, ch, ny, f_any, g_any, w1_any, w2_any, up_ref, dn_ref, held, w1_ref, w2_ref, raw, sems):
    rows = ch * ny
    wanted = ((0, nx - 2), (0, nx - 1), (1, nx - 1), (0, 1), (0, 0), (1, 0))
    others = [(i, x) for x in range(nx) for i in range(2) if (i, x) not in wanted]
    copies = {
        (i, x): pltpu.make_async_copy((f_any, g_any)[i].at[0, :, x], held.at[i, x], sems.at[i * nx + x])
        for i, x in (*wanted, *others)
    }
    weights = [pltpu.make_async_copy(src, dst, sems.at[2 * nx + i]) for i, (src, dst) in enumerate(((w1_any, w1_ref), (w2_any, w2_ref)))]
    for copy in (*copies.values(), *weights):
        copy.start()
    for j, (i, x) in enumerate(wanted):
        copies[i, x].wait()
        raw[:, j * LANES : (j + 1) * LANES] = held[i, x].astype(F32).reshape(rows, LANES).astype(BF)
    out = mm(ordered(ch, ny), raw[...]).astype(BF)
    for j in range(3):
        at = slice(j * rows, (j + 1) * rows)
        up_ref[at] = out[:, j * LANES : (j + 1) * LANES]
        dn_ref[at] = out[:, (j + 3) * LANES : (j + 4) * LANES]
    for key in others:
        copies[key].wait()
    for copy in weights:
        copy.wait()


def faces(features, cotangent, first_weight, second_weight):
    _, ch, nx, ny, _ = features.shape
    rows = ch * ny
    sds = pltpu.VMEM
    laid = lambda weight: jnp.transpose(weight, (1, 2, 3, 0, 4))
    return pl.pallas_call(
        functools.partial(faces_kernel, nx, ch, ny),
        out_shape=(
            sds((3 * rows, LANES), BF),
            sds((3 * rows, LANES), BF),
            sds((2, nx, ch, ny, LANES), BF),
            sds((3, 3, 3, ch, ch), BF),
            sds((3, 3, 3, ch, ch), BF),
        ),
        in_specs=[pl.BlockSpec(memory_space=pl.ANY)] * 4,
        scratch_shapes=[pltpu.VMEM((rows, 6 * LANES), BF), pltpu.SemaphoreType.DMA((2 * nx + 2,))],
        compiler_params=params(4),
        name="faces",
    )(*in_hbm(features, cotangent, laid(first_weight), laid(second_weight)))


def pack_kernel(nx, ch, ny, held, fo_ref, go_ref, edge_ref, raw):
    rows = ch * ny
    perm = ordered(ch, ny)
    for i, dst in enumerate((fo_ref, go_ref)):
        for x in range(nx):
            raw[:, x * LANES : (x + 1) * LANES] = held[i, x].astype(F32).reshape(rows, LANES).astype(BF)
        dst[...] = mm(perm, raw[...]).astype(BF)
    n = edge_ref.shape[0]
    j, m = iota((n, nx * LANES), 0), iota((n, nx * LANES), 1)
    c, x = j // nx, j % nx
    zf = jnp.where(c < 2, c, LANES - 4 + c)
    pick_f = one_hot((c < 4) & (m == x * LANES + zf))
    zg = jnp.where(c == 4, 0, LANES - 1)
    pick_g = one_hot((c >= 4) & (c < 6) & (m == x * LANES + zg))
    edge_ref[...] = (mm_nt(pick_f, fo_ref[...]) + mm_nt(pick_g, go_ref[...])).astype(BF)


def pack(held):
    _, nx, ch, ny, _ = held.shape
    rows = ch * ny
    edge_rows = -(-6 * nx // 32) * 32
    sds = pltpu.VMEM
    return pl.pallas_call(
        functools.partial(pack_kernel, nx, ch, ny),
        out_shape=(sds((rows, nx * LANES), BF), sds((rows, nx * LANES), BF), sds((edge_rows, rows), BF)),
        scratch_shapes=[pltpu.VMEM((rows, nx * LANES), BF)],
        compiler_params=params(4),
        cost_estimate=pl.CostEstimate(flops=500_000_000, bytes_accessed=1_000_000, transcendentals=0),
        name="pack",
    )(*in_vmem(held))


def bands_kernel(ny, w1_ref, w2_ref, t1_ref, tv_ref, t2_ref):
    ch = w1_ref.shape[-1]
    rows = ny * ch
    lane = iota((ch, rows), 1)
    r, k = iota((ch, LANES), 0), iota((ch, LANES), 1)
    places = [one_hot(k == r + b * ch) for b in range(3)]

    def direct(ref):
        wide = None
        for b in range(3):
            part = mm(ref[:, b].reshape(9 * ch, ch), places[b])
            wide = part if wide is None else wide + part
        return [wide[i * ch : (i + 1) * ch] for i in range(9)]

    def flipped(ref):
        none = jnp.zeros((ch, ch), BF)
        stack = [ref[2 - a, 2 - b, 2 - c] if b < 3 else none for a in range(3) for c in range(3) for b in range(4)]
        wide = mm_nt(one_hot(r == k)[:, :ch], jnp.concatenate(stack, axis=0))
        return [wide[:, i * LANES : (i + 1) * LANES] for i in range(9)]

    rest = jnp.zeros((ch, rows - LANES), F32)
    for taps, out in ((direct(w1_ref), t1_ref), (flipped(w2_ref), tv_ref), (direct(w2_ref), t2_ref)):
        for i, tap in enumerate(taps):
            a, c = i // 3, i % 3
            wide = jnp.concatenate([tap, rest], axis=1)
            for y in range(ny):
                block = wide if y == 1 else pltpu.roll(wide, (ch * (y - 1)) % rows, 1)
                if y == 0:
                    block = jnp.where(lane >= rows - ch, 0.0, block)
                if y == ny - 1:
                    block = jnp.where(lane < ch, 0.0, block)
                out[a, y * ch : (y + 1) * ch, c * rows : (c + 1) * rows] = block.astype(BF)


def bands(first_weight, second_weight, ny):
    ch = first_weight.shape[-1]
    rows = ch * ny
    return pl.pallas_call(
        functools.partial(bands_kernel, ny),
        out_shape=(pltpu.VMEM((3, rows, 3 * rows), BF),) * 3,
        compiler_params=params(3),
        cost_estimate=pl.CostEstimate(flops=1_000_000_000, bytes_accessed=4_000_000, transcendentals=0),
        name="bands",
    )(*in_vmem(first_weight, second_weight))


def shifted_rows(out, row, block, before, after, rows):
    lane = iota(block.shape, 1)
    at = slice(row * LANES, (row + 1) * LANES)
    wide = block.astype(F32)
    out[0:rows, at] = jnp.where(lane == 0, before, pltpu.roll(wide, 1, 1)).astype(BF)
    out[rows : 2 * rows, at] = block
    out[2 * rows :, at] = jnp.where(lane == LANES - 1, after, pltpu.roll(wide, LANES - 1, 1)).astype(BF)


def lane_to(edges, source, target):
    shift = (target - source) % LANES
    return edges if shift == 0 else pltpu.roll(edges, shift, 1)


def fold_taps(product, ch, ny):
    rows = ch * ny
    lane = iota((ch, rows), 1)
    total = None
    for y in range(ny):
        block = product[y * ch : (y + 1) * ch]
        if y == 0:
            block = jnp.where(lane >= rows - ch, 0.0, block)
        if y == ny - 1:
            block = jnp.where(lane < ch, 0.0, block)
        if y != 1:
            block = pltpu.roll(block, (ch * (1 - y)) % rows, 1)
        total = block if total is None else total + block
    return total[:, :LANES]


def place_taps(columns, folded, a, c, ch):
    lane = iota(folded.shape, 1)
    for b in range(3):
        target = ch * ((a * 3 + b) * 3 + c)
        col, offset = target // LANES, target % LANES
        moved = lane_to(folded, b * ch, offset)
        columns[col] = jnp.where((lane >= offset) & (lane < offset + ch), moved, columns[col])


def bias_terms(field, ch, ny):
    nx = field.shape[1] // LANES
    wide = field.astype(F32)
    total = wide[:, 0:LANES]
    for x in range(1, nx):
        total = total + wide[:, x * LANES : (x + 1) * LANES]
    folded = total[0:ch]
    for y in range(1, ny):
        folded = folded + total[y * ch : (y + 1) * ch]
    return jnp.sum(folded, axis=1, keepdims=True)


def silu(preact):
    return (preact / (1.0 + jnp.exp(-preact))).astype(BF)


def bias_column(ref, ny):
    ch = ref.shape[1]
    r, k = iota((ch, ch), 0), iota((ch, ch), 1)
    column = jnp.sum(jnp.where(r == k, ref[...], 0.0), axis=1, keepdims=True)
    return jnp.concatenate([column] * ny, axis=0)


def edge_columns(nx, sources):
    n = sources[0][3].shape[0]
    j, k = iota((LANES, n), 0), iota((LANES, n), 1)
    s, xx = j // 16, j % 16
    column = jnp.where(s == 0, 2, jnp.where(s == 1, 3, jnp.where(s == 5, 0, jnp.where(s == 6, 1, jnp.where(s == 3, 5, jnp.where(s == 7, 4, -1))))))
    out = None
    for low, high, start, message in sources:
        hit = (column >= 0) & (xx >= low) & (xx < high) & (k == column * nx + xx - low + start)
        part = mm(one_hot(hit), message)
        out = part if out is None else out + part
    return out


def conv_inside(t_ref, field, out, nx):
    n, m = nx * LANES, (nx - 1) * LANES
    out[...] = mm(t_ref[1], field[:, 0:n])
    out[:, LANES:] = out[:, LANES:] + mm(t_ref[0], field[:, 0:m])
    out[:, 0:m] = out[:, 0:m] + mm(t_ref[2], field[:, LANES:n])


def gate(hidden_grad, preact):
    logistic = 1.0 / (1.0 + jnp.exp(-preact))
    return (hidden_grad * logistic * (1.0 + preact * (1.0 - logistic))).astype(BF)


def tap_terms(upstream, taps, ch, ny):
    columns = [jnp.zeros((ch, LANES), F32) for _ in range(TERMS // LANES)]
    for a in range(3):
        for c in range(3):
            product = mm_nt(*((taps(2 - a, 2 - c), upstream) if upstream is not None else taps(a, c)))
            place_taps(columns, fold_taps(product, ch, ny), a, c, ch)
    return columns


def with_bias(columns, field, ch, ny):
    lane = iota((ch, LANES), 1)
    return columns[:-1] + [jnp.where(lane == 27 * ch % LANES, bias_terms(field, ch, ny), columns[-1])]


def inner_kernel(
    nx, ch, ny,
    t1_ref, tv_ref, f_ref, g_ref, near_ref, bias_ref,
    fs, gs, pre, grad, hid_ref, second_ref, first_ref,
):
    rows = ch * ny
    edges = edge_columns(nx, ((2, nx + 2, 0, near_ref[...]),)).T
    for src, dst, left, right in ((f_ref, fs, 16, 80), (g_ref, gs, 48, 112)):
        for x in range(nx):
            block = src[:, x * LANES : (x + 1) * LANES]
            shifted_rows(dst, x, block, lane_to(edges, left + x + 2, 0), lane_to(edges, right + x + 2, LANES - 1), rows)
    conv_inside(t1_ref, fs, pre, nx)
    pre[...] = pre[...] + bias_column(bias_ref, ny)
    conv_inside(tv_ref, gs, grad, nx)
    n = (nx - 2) * LANES
    inside = slice(LANES, LANES + n)
    preact = pre[:, inside]
    hid_ref[...] = silu(preact)
    preact_grad = gate(grad[:, inside], preact)
    window = lambda ref, a, c: ref[c * rows : (c + 1) * rows, a * LANES : a * LANES + n]
    second = tap_terms(hid_ref[...], lambda a, c: window(gs, a, c), ch, ny)
    first = tap_terms(None, lambda a, c: (preact_grad, window(fs, a, c)), ch, ny)
    second = with_bias(second, g_ref[...], ch, ny)
    first = with_bias(first, preact_grad, ch, ny)
    for i in range(TERMS // LANES):
        at = slice(i * LANES, (i + 1) * LANES)
        second_ref[:, at] = second[i]
        first_ref[:, at] = first[i]


def inner(t1, tv, field, cot, near, bias, ch, ny):
    rows = ch * ny
    nx = field.shape[1] // LANES
    sds = pltpu.VMEM
    return pl.pallas_call(
        functools.partial(inner_kernel, nx, ch, ny),
        out_shape=(
            sds((3 * rows, nx * LANES), BF),
            sds((3 * rows, nx * LANES), BF),
            sds((rows, nx * LANES), F32),
            sds((rows, nx * LANES), F32),
            sds((rows, (nx - 2) * LANES), BF),
            sds((ch, TERMS), F32),
            sds((ch, TERMS), F32),
        ),
        compiler_params=params(6),
        cost_estimate=pl.CostEstimate(flops=2_000_000_000, bytes_accessed=4_000_000, transcendentals=0),
        name="inner",
    )(*in_vmem(t1, tv, field, cot, near, bias))


def outer_kernel(
    nx, ch, ny, scale,
    t1_ref, tv_ref, fs, gs, pre, grad, part_second_ref, part_first_ref, above_ref, below_ref, before_ref, after_ref,
    hid_ref, fe, keep_ref, give_ref,
    ge,
):
    rows = ch * ny
    edges = edge_columns(nx, ((0, 2, nx - 2, before_ref[...]), (nx + 2, nx + 4, 0, after_ref[...]))).T
    for i, (dst, left, right) in enumerate(((fe, 16, 80), (ge, 48, 112))):
        for j, (src, xx) in enumerate(((above_ref, 1), (below_ref, nx + 2))):
            block = src[(i + 1) * rows : (i + 2) * rows]
            shifted_rows(dst, j, block, lane_to(edges, left + xx, 0), lane_to(edges, right + xx, LANES - 1), rows)

    last = (nx - 1) * LANES
    ends = lambda ref: jnp.concatenate([ref[:, 0:LANES], ref[:, last:]], axis=1)
    both = lambda t, e: jnp.concatenate([mm(t[0], e[:, 0:LANES]), mm(t[2], e[:, LANES:])], axis=1)
    preact = ends(pre) + both(t1_ref, fe)
    hid_ref[...] = silu(preact)
    preact_grad = gate(ends(grad) + both(tv_ref, ge), preact)

    def window(own, end, a, c):
        at = slice(c * rows, (c + 1) * rows)
        head = end[at, 0:LANES] if a == 0 else own[at, (a - 1) * LANES : a * LANES]
        tail = end[at, LANES:] if a == 2 else own[at, last + (a - 1) * LANES : last + a * LANES]
        return jnp.concatenate([head, tail], axis=1)

    second = tap_terms(hid_ref[...], lambda a, c: window(gs, ge, a, c), ch, ny)
    first = tap_terms(None, lambda a, c: (preact_grad, window(fs, fe, a, c)), ch, ny)
    first = with_bias(first, preact_grad, ch, ny)
    mine = is_even("smp")
    for i in range(TERMS // LANES):
        at = slice(i * LANES, (i + 1) * LANES)
        part_second = (second[i] + part_second_ref[:, at]) * scale
        part_first = (first[i] + part_first_ref[:, at]) * scale
        keep_ref[:, at] = jnp.where(mine, part_second, part_first)
        give_ref[:, at] = jnp.where(mine, part_first, part_second)


def outer(t1, tv, fs, gs, pre, grad, second, first, above, below, before, after, ch, ny, scale):
    rows = ch * ny
    nx = fs.shape[1] // LANES
    sds = pltpu.VMEM
    return pl.pallas_call(
        functools.partial(outer_kernel, nx, ch, ny, scale),
        out_shape=(
            sds((rows, 2 * LANES), BF),
            sds((3 * rows, 2 * LANES), BF),
            sds((ch, TERMS), F32),
            sds((ch, TERMS), F32),
        ),
        scratch_shapes=[pltpu.VMEM((3 * rows, 2 * LANES), BF)],
        compiler_params=params(6),
        name="outer",
    )(*in_vmem(t1, tv, fs, gs, pre, grad, second, first, above, below, before, after))


def residual_kernel(
    nx, ch, ny,
    t1_ref, t2_ref, h_ref, h_end_ref, fs_ref, fe_ref, f_ref, above_ref, below_ref, near_ref, before_ref, after_ref, bias1_ref, bias2_ref,
    o_ref,
    ends, hs,
):
    rows = ch * ny
    above, below = above_ref[0:rows], below_ref[0:rows]
    sources = ((2, nx + 2, 0, near_ref[...]), (0, 2, nx - 2, before_ref[...]), (nx + 2, nx + 4, 0, after_ref[...]))
    edges_t = edge_columns(nx, sources)
    end = fe_ref[rows : 2 * rows]
    unshifted = [above, end[:, 0:LANES], *(f_ref[:, x * LANES : (x + 1) * LANES] for x in range(nx)), end[:, LANES:], below]
    j, k = iota((LANES, LANES), 0), iota((LANES, LANES), 1)
    own_end = jnp.where(j // 16 == 2, 0, jnp.where(j // 16 == 4, LANES - 1, -1))
    for x in range(nx + 4):
        edges_t = edges_t + mm_nt(one_hot((j % 16 == x) & (k == own_end)), unshifted[x])
    edges = edges_t.T
    shifted_rows(ends, 0, above, lane_to(edges, 16, 0), lane_to(edges, 80, LANES - 1), rows)
    shifted_rows(ends, 1, below, lane_to(edges, 16 + nx + 3, 0), lane_to(edges, 80 + nx + 3, LANES - 1), rows)
    acc = None
    row = lambda x: fs_ref[:, x * LANES : (x + 1) * LANES]
    pairs = ((ends[:, 0:LANES], row(nx - 1)), (fe_ref[:, 0:LANES], fe_ref[:, LANES:]), (row(0), ends[:, LANES:]))
    for a in range(3):
        columns = [lane_to(edges, 16 * c + a, 0).astype(BF) for c in range(3)]
        term = mm(t1_ref[a], jnp.concatenate([*pairs[a], jnp.concatenate(columns, axis=0)], axis=1))
        acc = term if acc is None else acc + term
    hidden = silu(acc + bias_column(bias1_ref, ny))
    outer = hidden[:, 2 * LANES :].astype(F32)
    for x in range(nx + 2):
        if x == 0:
            block = hidden[:, 0:LANES]
        elif x == nx + 1:
            block = hidden[:, LANES : 2 * LANES]
        elif x == 1:
            block = h_end_ref[:, 0:LANES]
        elif x == nx:
            block = h_end_ref[:, LANES:]
        else:
            block = h_ref[:, (x - 2) * LANES : (x - 1) * LANES]
        shifted_rows(hs, x, block, lane_to(outer, x, 0), lane_to(outer, 64 + x, LANES - 1), rows)
    n5 = nx * LANES
    acc = mm(t2_ref[0], hs[:, 0:n5])
    for a in range(1, 3):
        acc = acc + mm(t2_ref[a], hs[:, a * LANES : a * LANES + n5])
    total = (f_ref[...].astype(F32) + (acc + bias_column(bias2_ref, ny))).astype(BF)
    r, k = iota((rows, rows), 0), iota((rows, rows), 1)
    back = one_hot(k == (r % ny) * ch + r // ny)
    ordered = mm(back, total)
    for x in range(nx):
        o_ref[0, :, x] = ordered[:, x * LANES : (x + 1) * LANES].reshape(ch, ny, LANES).astype(BF)


def residual(t1, t2, hidden, hidden_end, fs, fe, field, above, below, near, before, after, bias1, bias2, ch, ny):
    rows = ch * ny
    nx = field.shape[1] // LANES
    return pl.pallas_call(
        functools.partial(residual_kernel, nx, ch, ny),
        out_shape=jax.ShapeDtypeStruct((1, ch, nx, ny, LANES), BF),
        scratch_shapes=[pltpu.VMEM((3 * rows, 2 * LANES), BF), pltpu.VMEM((3 * rows, (nx + 2) * LANES), BF)],
        compiler_params=params(8),
        cost_estimate=pl.CostEstimate(flops=3_000_000_000, bytes_accessed=3_000_000, transcendentals=0),
        name="residual",
    )(*in_vmem(t1, t2, hidden, hidden_end, fs, fe, field, above, below, near, before, after, bias1, bias2))


def moved(array, sizes, step):
    ns, nx, nz = sizes
    pairs = []
    for s in range(ns):
        for x in range(nx):
            for z in range(nz):
                t, u, v = step(s, x, z)
                pairs.append(((s * nx + x) * nz + z, (t * nx + u) * nz + v))
    return lax.ppermute(array, AXES, pairs)


def along(array, sizes, dx):
    ns, nx, nz = sizes
    return moved(array, sizes, lambda s, x, z: (s, (x + dx) % nx, z))


def swapped(array, sizes, bits):
    return moved(array, sizes, lambda s, x, z: (s ^ bits[0], x ^ bits[1], z ^ bits[2]))


def add_kernel(n_in, *refs):
    terms = [ref[...].astype(F32) for ref in refs[:n_in]]
    out = refs[n_in]
    while len(terms) > 1:
        terms = [terms[i] + terms[i + 1] for i in range(0, len(terms), 2)]
    total = terms[0]
    n = total.shape[1] - LANES
    out[:, :n] = total[:, :n].astype(out.dtype)
    tail = total[:, n:]
    lane = iota(tail.shape, 1)
    spare = 864 % LANES
    joined = tail + pltpu.roll(tail, LANES - 1, 1)
    if out.dtype == BF:
        low = joined - joined.astype(BF).astype(F32)
        tail = jnp.where(lane == spare + 1, pltpu.roll(low, 1, 1), tail)
    out[:, n:] = jnp.where(lane == spare, joined, tail).astype(out.dtype)


def add(terms, dtype):
    return pl.pallas_call(
        functools.partial(add_kernel, len(terms)),
        out_shape=pltpu.VMEM(terms[0].shape, dtype),
        compiler_params=params(1),
        name="add",
    )(*in_vmem(*terms))


def exchange(sent, sizes, pair):
    steps = [(0, 0, 0)]
    for bits in pair:
        steps = steps + [tuple(p ^ q for p, q in zip(bits, step)) for step in steps]
    return [sent] + [swapped(sent, sizes, step) for step in steps[1:]]


def sum_all(keep, give, sizes, output):
    near = (1, 0, 0)
    bits = [(0, 1 << i, 0) for i in range(sizes[1].bit_length() - 1)]
    bits += [(0, 0, 1 << i) for i in range(sizes[2].bit_length() - 1)]
    bits += [(1 << i, 0, 0) for i in range(1, sizes[0].bit_length() - 1)]
    terms = [keep, swapped(give, sizes, near)]
    for i in range(0, len(bits), 2):
        terms = exchange(add(terms, BF), sizes, bits[i : i + 2])
        if i == 0:
            *terms, output = lax.optimization_barrier((*terms, output))
    mine = add(terms, F32)
    return mine, swapped(mine, sizes, near), output


def spread_kernel(ch, mine_ref, other_ref, first_ref, first_bias_ref, second_ref, second_bias_ref):
    even = is_even("smp")
    mine, other = mine_ref[...], other_ref[...]
    r, k = iota((ch, LANES), 0), iota((ch, LANES), 1)
    for terms, out, bias in (
        (jnp.where(even, other, mine), first_ref, first_bias_ref),
        (jnp.where(even, mine, other), second_ref, second_bias_ref),
    ):
        for tap in range(27):
            at = tap * ch
            block = terms[:, at // LANES * LANES : (at // LANES + 1) * LANES]
            out[tap // 9, tap // 3 % 3, tap % 3] = lane_to(block, at % LANES, 0)[:, :ch]
        tail = lane_to(terms[:, TERMS - LANES :], 27 * ch % LANES, 0)[:, 0:1]
        bias[...] = jnp.sum(jnp.where(r == k, tail, 0.0), axis=0, keepdims=True)[:, :ch]


def spread(mine, other, ch):
    sds = jax.ShapeDtypeStruct
    taps, bias = sds((3, 3, 3, ch, ch), F32), sds((1, ch), F32)
    first, first_bias, second, second_bias = pl.pallas_call(
        functools.partial(spread_kernel, ch),
        out_shape=(taps, bias, taps, bias),
        compiler_params=params(4),
        name="spread",
    )(*in_vmem(mine, other))
    laid = lambda grad: jnp.transpose(grad, (3, 0, 1, 2, 4))
    return laid(first), first_bias.reshape(ch), laid(second), second_bias.reshape(ch)


def shards(sizes, features, first_weight, first_bias, second_weight, second_bias, cotangent):
    ns, ngx, ngz = sizes
    _, ch, nx, ny, nz = features.shape
    assert features.shape[0] == 1 and nz == LANES and ngz == 2
    assert not any(n & (n - 1) for n in sizes) and ns > 1
    scale = float((ns * nx * ngx * ny * nz * ngz) ** -0.5)
    up, down, held, weight1, weight2 = faces(features, cotangent, first_weight, second_weight)
    above, below = along(up, sizes, 1), along(down, sizes, -1)
    field, cot, edge = pack(held)
    near = swapped(edge, sizes, (0, 0, 1))
    before, after = along(near, sizes, 1), along(near, sizes, -1)
    t1, tv, t2 = bands(weight1, weight2, ny)
    bias1, bias2 = first_bias.reshape(1, ch), second_bias.reshape(1, ch)
    fs, gs, pre, grad, hidden, second, first = inner(t1, tv, field, cot, near, bias1, ch, ny)
    hidden_end, fe, keep, give = outer(
        t1, tv, fs, gs, pre, grad, second, first, above, below, before, after, ch, ny, scale
    )
    output = residual(t1, t2, hidden, hidden_end, fs, fe, field, above, below, near, before, after, bias1, bias2, ch, ny)
    mine, other, output = sum_all(keep, give, sizes, output)
    return output, *spread(mine, other, ch)


def solution(mesh):
    sizes = tuple(mesh.shape[axis] for axis in AXES)
    split = P("smp", None, "gx", None, "gz")
    return jax.shard_map(
        functools.partial(shards, sizes),
        mesh=mesh,
        in_specs=(split, P(), P(), P(), P(), split),
        out_specs=(split, P(), P(), P(), P()),
        check_vma=False,
    )
```

time: 42.8 us -> 41.4 us (0.967)
  starting transfers between devices: 20.3 us -> 16.8 us
  waiting for transfers between devices: 6.45 us -> 9.78 us
  Pallas kernels: 15.2 us -> 13.9 us
    ppermute x15 -> x13, starting transfers between devices: 20.3 us -> 16.8 us  [moved(): return lax.ppermute(array, AXES, pairs)]
    ppermute x15 -> x13, waiting for transfers between devices: 6.45 us -> 9.78 us  [moved(): return lax.ppermute(array, AXES, pairs)]
    pallas_call x1, Pallas kernels: 2.14 us -> 0.82 us  [pack(): pl.pallas_call(functools.partial(pack_kernel, nx, ch, ny), out_shape=(sds...]
    pallas_call x2 -> x4, Pallas kernels: 7.95 us -> 8.04 us  [the longest x1 3.89 us: inner(): pl.pallas_call(functools.partial(inner_kernel, nx, ch, ny), out_shape=(sd...]
  transfers between devices with their start and end apart: 15 -> 13, of which waited for: 6 -> 8; matrix products, arithmetic and copies ran while one was open for 0% -> 0% of each run, Pallas kernels for 16% -> 21%
where the time goes in v4:
time: 41.4 us; the launch traced here: 41.2 us
  starting transfers between devices  16.8 us (41%)
  Pallas kernels  13.9 us (34%)
  waiting for transfers between devices  9.78 us (24%)
  between operations  0.71 us (2%)
    ppermute x13, starting transfers between devices, moved(): return lax.ppermute(array, AXES, pairs)  16.8 us
    ppermute x13, waiting for transfers between devices, moved(): return lax.ppermute(array, AXES, pairs)  9.78 us
    pallas_call x1, Pallas kernels, inner(): pl.pallas_call(functools.partial(inner_kernel, nx, ch, ny), out_shape=(sd...  3.89 us
    pallas_call x1, Pallas kernels, residual(): pl.pallas_call(functools.partial(residual_kernel, nx, ch, ny), out_shape=...  3.42 us
    pallas_call x1, Pallas kernels, outer(): pl.pallas_call(functools.partial(outer_kernel, nx, ch, ny, scale), out_sh...  2.16 us
    pallas_call x1, Pallas kernels, faces(): pl.pallas_call(functools.partial(faces_kernel, nx, ch, ny), out_shape=(sd...  1.44 us
    pallas_call x1, Pallas kernels, spread(): pl.pallas_call(functools.partial(spread_kernel, ch), out_shape=(taps, bia...  1.2 us
  transfers between devices with their start and end apart: 13, of which 8 were waited for; matrix products, arithmetic and copies ran while one was open for 0% of the time, Pallas kernels for 21%

profile of v4, /device:TPU:0, one launch (start us, length us, event | category | flops | bytes accessed | tf_op | source)
XLA Modules:
  0.0 41.2 jit_solution(12892624779614954566)
XLA Ops:
  0.6 1.4 %faces.1 = (bf16[768,128]{1,0:T(8,128)(2,1)S(1)}, bf16[768,128]{1,0:T(8,128)(2,1)S(1)}, bf16[2,5,32,8,128]{4,3,2,1,0:T(8,128)(2,1)S(1)}, bf16[3,3,3,32,32]{4,3,2...) custom-call(bf16[1,32,5,8,128]{4,3,2,1,0:T(8,128)(2,1)} %f_any.1, bf16[1,32,5,8,128]{4,3,2,1,0:T(8,128)(2,1)} %g_any.1, ...), custom_call_target="tpu_custom_call" | custom-call | tf_op jit(solution)/shard_map/faces/pallas_call | solution.py:84
  2.1 3.1 %collective-permute-start.1 = (bf16[768,128]{1,0:T(8,128)(2,1)S(1)}, bf16[768,128]{1,0:T(8,128)(2,1)S(1)}, u32[]{:S(2)}, u32[]{:S(2)}) collective-permute-start(bf16[768,128]{1,0:T(8,128)(2,1)S(1)} %get-tuple-element.50), channel_id=1, source_target_pairs={{0,2},{1,3},{2,4},{3,5},{4,6},{5,7},{6,0},{7,1},{8,10},{9,11},{10,... | collective-permute-start | bytes 589832 | tf_op jit(solution)/shard_map/ppermute | solution.py:459
  5.2 2.1 %collective-permute-start.2 = (bf16[768,128]{1,0:T(8,128)(2,1)S(1)}, bf16[768,128]{1,0:T(8,128)(2,1)S(1)}, u32[]{:S(2)}, u32[]{:S(2)}) collective-permute-start(bf16[768,128]{1,0:T(8,128)(2,1)S(1)} %get-tuple-element.51), channel_id=1, source_target_pairs={{0,6},{1,7},{2,0},{3,1},{4,2},{5,3},{6,4},{7,5},{8,14},{9,15},{10,... | collective-permute-start | bytes 589832 | tf_op jit(solution)/shard_map/ppermute | solution.py:459
  7.2 0.8 %pack.1 = (bf16[256,640]{1,0:T(8,128)(2,1)S(1)}, bf16[256,640]{1,0:T(8,128)(2,1)S(1)}, bf16[32,256]{1,0:T(8,128)(2,1)S(1)}) custom-call(bf16[2,5,32,8,128]{4,3,2,1,0:T(8,128)(2,1)S(1)} %get-tuple-element.40.held), custom_call_target="tpu_custom_call" | custom-call | flops 500000000 | bytes 1000000 | tf_op jit(solution)/shard_map/pack/pallas_call | solution.py:122
  8.1 1.7 %collective-permute-start = (bf16[32,256]{1,0:T(8,128)(2,1)S(1)}, bf16[32,256]{1,0:T(8,128)(2,1)S(1)}, u32[]{:S(2)}, u32[]{:S(2)}) collective-permute-start(bf16[32,256]{1,0:T(8,128)(2,1)S(1)} %get-tuple-element.43), channel_id=1, source_target_pairs={{0,1},{1,0},{2,3},{3,2},{4,5},{5,4},{6,7},{7,6},{8,9},{9,8},{10,11... | collective-permute-start | bytes 49160 | tf_op jit(solution)/shard_map/ppermute | solution.py:459
  9.7 0.6 %bands.1 = (bf16[3,256,768]{2,1,0:T(8,128)(2,1)S(1)}, bf16[3,256,768]{2,1,0:T(8,128)(2,1)S(1)}, bf16[3,256,768]{2,1,0:T(8,128)(2,1)S(1)}) custom-call(bf16[3,3,3,32,32]{4,3,2,1,0:T(8,128)(2,1)S(1)} %get-tuple-element.36.w1_ref, bf16[3,3,3,32,32]{4,3,2,1,0:T(8,128)(2,1)S(1)} %get-tuple-element.37.w2_ref), custom_call_target="tpu_custom_call" | custom-call | flops 1000000000 | bytes 4000000 | tf_op jit(solution)/shard_map/bands/pallas_call | solution.py:169
  10.3 1.5 %collective-permute-done.near_ref = bf16[32,256]{1,0:T(8,128)(2,1)S(1)} collective-permute-done((bf16[32,256]{1,0:T(8,128)(2,1)S(1)}, bf16[32,256]{1,0:T(8,128)(2,1)S(1)}, u32[]{:S(2)}, u32[]{:S(2)}) %collective-permute-start) | collective-permute-done | bytes 16416 | tf_op jit(solution)/shard_map/ppermute | solution.py:459
  11.8 2.0 %collective-permute-start.4 = (bf16[32,256]{1,0:T(8,128)(2,1)S(1)}, bf16[32,256]{1,0:T(8,128)(2,1)S(1)}, u32[]{:S(2)}, u32[]{:S(2)}) collective-permute-start(bf16[32,256]{1,0:T(8,128)(2,1)S(1)} %collective-permute-done.near_ref), channel_id=1, source_target_pairs={{0,6},{1,7},{2,0},{3,1},{4,2},{5,3},{6,4},{7,5},{8,14},{9,15},{10,... | collective-permute-start | bytes 49160 | tf_op jit(solution)/shard_map/ppermute | solution.py:459
  13.8 0.1 collective-permute-start.3
  13.9 3.9 %inner.1 = (bf16[768,640]{1,0:T(8,128)(2,1)S(1)}, bf16[768,640]{1,0:T(8,128)(2,1)S(1)}, f32[256,640]{1,0:T(8,128)S(1)}, f32[256,640]{1,0:T(8,128)S(1)}, bf16[256...) custom-call(bf16[3,256,768]{2,1,0:T(8,128)(2,1)S(1)} %get-tuple-element.38.t1_ref, ...), custom_call_target="tpu_custom_call" | custom-call | flops 2000000000 | bytes 4000000 | tf_op jit(solution)/shard_map/inner/pallas_call | solution.py:313
  17.8 0.0 collective-permute-done.4.after_ref
  17.8 1.6 %collective-permute-done.3.before_ref = bf16[32,256]{1,0:T(8,128)(2,1)S(1)} collective-permute-done((bf16[32,256]{1,0:T(8,128)(2,1)S(1)}, bf16[32,256]{1,0:T(8,128)(2,1)S(1)}, u32[]{:S(2)}, u32[]{:S(2)}) %collective-permute-start.3) | collective-permute-done | bytes 16416 | tf_op jit(solution)/shard_map/ppermute | solution.py:459
  19.3 0.0 collective-permute-done.1.above_ref
  19.3 2.2 %outer.1 = (bf16[256,256]{1,0:T(8,128)(2,1)S(1)}, bf16[768,256]{1,0:T(8,128)(2,1)S(1)}, f32[32,896]{1,0:T(8,128)S(1)}, f32[32,896]{1,0:T(8,128)S(1)}) custom-call(bf16[3,256,768]{2,1,0:T(8,128)(2,1)S(1)} %get-tuple-element.38.t1_ref, bf16[3,256,768]{2,1,0:T(8,128)(2,1)S(1)} %get-tuple-element.39.tv_ref, bf16[768,640]{1,0:T(8,128)(2,1)S(1)} %get-tuple-element.44.fs.fs_ref, ...), custom_call_target="tpu_custom_call" | custom-call | tf_op jit(solution)/shard_map/outer/pallas_call | solution.py:372
  21.5 0.1 collective-permute-start.5
  21.6 1.3 %collective-permute-done.5.refs_1_ = f32[32,896]{1,0:T(8,128)S(1)} collective-permute-done((f32[32,896]{1,0:T(8,128)S(1)}, f32[32,896]{1,0:T(8,128)S(1)}, u32[]{:S(2)}, u32[]{:S(2)}) %collective-permute-start.5) | collective-permute-done | bytes 114720 | tf_op jit(solution)/shard_map/ppermute | solution.py:459
  22.9 0.1 add.3.refs_0_
  23.0 2.2 %collective-permute-start.8 = (bf16[32,896]{1,0:T(8,128)(2,1)S(1)}, bf16[32,896]{1,0:T(8,128)(2,1)S(1)}, u32[]{:S(2)}, u32[]{:S(2)}) collective-permute-start(bf16[32,896]{1,0:T(8,128)(2,1)S(1)} %add.3.refs_0_), channel_id=1, source_target_pairs={{0,6},{1,7},{2,4},{3,5},{4,2},{5,3},{6,0},{7,1},{8,14},{9,15},{10,... | collective-permute-start | bytes 172040 | tf_op jit(solution)/shard_map/ppermute | solution.py:459
  25.3 2.2 %collective-permute-start.6 = (bf16[32,896]{1,0:T(8,128)(2,1)S(1)}, bf16[32,896]{1,0:T(8,128)(2,1)S(1)}, u32[]{:S(2)}, u32[]{:S(2)}) collective-permute-start(bf16[32,896]{1,0:T(8,128)(2,1)S(1)} %add.3.refs_0_), channel_id=1, source_target_pairs={{0,2},{1,3},{2,0},{3,1},{4,6},{5,7},{6,4},{7,5},{8,10},{9,11},{10,... | collective-permute-start | bytes 172040 | tf_op jit(solution)/shard_map/ppermute | solution.py:459
  27.4 3.4 %residual.1 = bf16[1,32,5,8,128]{4,3,2,1,0:T(8,128)(2,1)} custom-call(bf16[3,256,768]{2,1,0:T(8,128)(2,1)S(1)} %get-tuple-element.38.t1_ref, bf16[3,256,768]{2,1,0:T(8,128)(2,1)S(1)} %get-tuple-element.54.t2_ref, bf16[256,384]{1,0:T(8,128)(2,1)S(1)} %get-tuple-element.55.h_ref, bf16[256,256]{1,0:T(8,128)(2,1)S(1)} %get-tuple-element.56.h_end_ref, ...), custom_call_target="tpu_custom_call" | custom-call | flops 3000000000 | bytes 3000000 | tf_op jit(solution)/shard_map/residual/pallas_call | solution.py:441
  30.9 0.4 %collective-permute-done.7.refs_2_ = bf16[32,896]{1,0:T(8,128)(2,1)S(1)} collective-permute-done((bf16[32,896]{1,0:T(8,128)(2,1)S(1)}, bf16[32,896]{1,0:T(8,128)(2,1)S(1)}, u32[]{:S(2)}, u32[]{:S(2)}) %collective-permute-start.7) | collective-permute-done | bytes 57376 | tf_op jit(solution)/shard_map/ppermute | solution.py:459
  31.3 0.2 add.4.refs_0_
  31.5 2.5 %collective-permute-start.11 = (bf16[32,896]{1,0:T(8,128)(2,1)S(1)}, bf16[32,896]{1,0:T(8,128)(2,1)S(1)}, u32[]{:S(2)}, u32[]{:S(2)}) collective-permute-start(bf16[32,896]{1,0:T(8,128)(2,1)S(1)} %add.4.refs_0_), channel_id=1, source_target_pairs={{0,17},{1,16},{2,19},{3,18},{4,21},{5,20},{6,23},{7,22},{8,25},{9,... | collective-permute-start | bytes 172040 | tf_op jit(solution)/shard_map/ppermute | solution.py:459
  33.9 0.5 %collective-permute-start.10 = (bf16[32,896]{1,0:T(8,128)(2,1)S(1)}, bf16[32,896]{1,0:T(8,128)(2,1)S(1)}, u32[]{:S(2)}, u32[]{:S(2)}) collective-permute-start(bf16[32,896]{1,0:T(8,128)(2,1)S(1)} %add.4.refs_0_), channel_id=1, source_target_pairs={{0,16},{1,17},{2,18},{3,19},{4,20},{5,21},{6,22},{7,23},{8,24},{9,... | collective-permute-start | bytes 172040 | tf_op jit(solution)/shard_map/ppermute | solution.py:459
  34.4 0.5 %collective-permute-start.9 = (bf16[32,896]{1,0:T(8,128)(2,1)S(1)}, bf16[32,896]{1,0:T(8,128)(2,1)S(1)}, u32[]{:S(2)}, u32[]{:S(2)}) collective-permute-start(bf16[32,896]{1,0:T(8,128)(2,1)S(1)} %add.4.refs_0_), channel_id=1, source_target_pairs={{0,1},{1,0},{2,3},{3,2},{4,5},{5,4},{6,7},{7,6},{8,9},{9,8},{10,11... | collective-permute-start | bytes 172040 | tf_op jit(solution)/shard_map/ppermute | solution.py:459
  34.9 1.6 %collective-permute-done.11.refs_3_ = bf16[32,896]{1,0:T(8,128)(2,1)S(1)} collective-permute-done((bf16[32,896]{1,0:T(8,128)(2,1)S(1)}, bf16[32,896]{1,0:T(8,128)(2,1)S(1)}, u32[]{:S(2)}, u32[]{:S(2)}) %collective-permute-start.11) | collective-permute-done | bytes 57376 | tf_op jit(solution)/shard_map/ppermute | solution.py:459
  36.6 1.5 %collective-permute-done.10.refs_2_ = bf16[32,896]{1,0:T(8,128)(2,1)S(1)} collective-permute-done((bf16[32,896]{1,0:T(8,128)(2,1)S(1)}, bf16[32,896]{1,0:T(8,128)(2,1)S(1)}, u32[]{:S(2)}, u32[]{:S(2)}) %collective-permute-start.10) | collective-permute-done | bytes 57376 | tf_op jit(solution)/shard_map/ppermute | solution.py:459
  38.1 0.5 %collective-permute-done.9.refs_1_ = bf16[32,896]{1,0:T(8,128)(2,1)S(1)} collective-permute-done((bf16[32,896]{1,0:T(8,128)(2,1)S(1)}, bf16[32,896]{1,0:T(8,128)(2,1)S(1)}, u32[]{:S(2)}, u32[]{:S(2)}) %collective-permute-start.9) | collective-permute-done | bytes 57376 | tf_op jit(solution)/shard_map/ppermute | solution.py:459
  38.6 0.1 add.5.mine_ref
  38.7 0.0 collective-permute-start.12
  38.7 1.3 %collective-permute-done.12.other_ref = f32[32,896]{1,0:T(8,128)S(1)} collective-permute-done((f32[32,896]{1,0:T(8,128)S(1)}, f32[32,896]{1,0:T(8,128)S(1)}, u32[]{:S(2)}, u32[]{:S(2)}) %collective-permute-start.12) | collective-permute-done | bytes 114720 | tf_op jit(solution)/shard_map/ppermute | solution.py:459
  40.0 1.2 %spread.1 = (f32[3,3,3,32,32]{4,3,2,1,0:T(8,128)}, f32[1,32]{1,0:T(1,128)}, f32[3,3,3,32,32]{4,3,2,1,0:T(8,128)}, f32[1,32]{1,0:T(1,128)}) custom-call(f32[32,896]{1,0:T(8,128)S(1)} %add.5.mine_ref, f32[32,896]{1,0:T(8,128)S(1)} %collective-permute-done.12.other_ref), custom_call_target="tpu_custom_call" | custom-call | tf_op jit(solution)/shard_map/spread/pallas_call | solution.py:538
  (8 shorter events, 0.0 us)
Async XLA Ops:
  2.1 17.3 %collective-permute-start.1 = (bf16[768,128]{1,0:T(8,128)(2,1)S(1)}, bf16[768,128]{1,0:T(8,128)(2,1)S(1)}, u32[]{:S(2)}, u32[]{:S(2)}) collective-permute-start(bf16[768,128]{1,0:T(8,128)(2,1)S(1)} %get-tuple-element.50), channel_id=1, source_target_pairs={{0,2},{1,3},{2,4},{3,5},{4,6},{5,7},{6,0},{7,1},{8,10},{9,11},{10,... | collective-permute-start | bytes 589832 | tf_op jit(solution)/shard_map/ppermute | solution.py:459
  5.2 14.2 %collective-permute-start.2 = (bf16[768,128]{1,0:T(8,128)(2,1)S(1)}, bf16[768,128]{1,0:T(8,128)(2,1)S(1)}, u32[]{:S(2)}, u32[]{:S(2)}) collective-permute-start(bf16[768,128]{1,0:T(8,128)(2,1)S(1)} %get-tuple-element.51), channel_id=1, source_target_pairs={{0,6},{1,7},{2,0},{3,1},{4,2},{5,3},{6,4},{7,5},{8,14},{9,15},{10,... | collective-permute-start | bytes 589832 | tf_op jit(solution)/shard_map/ppermute | solution.py:459
  8.1 3.8 %collective-permute-start = (bf16[32,256]{1,0:T(8,128)(2,1)S(1)}, bf16[32,256]{1,0:T(8,128)(2,1)S(1)}, u32[]{:S(2)}, u32[]{:S(2)}) collective-permute-start(bf16[32,256]{1,0:T(8,128)(2,1)S(1)} %get-tuple-element.43), channel_id=1, source_target_pairs={{0,1},{1,0},{2,3},{3,2},{4,5},{5,4},{6,7},{7,6},{8,9},{9,8},{10,11... | collective-permute-start | bytes 49160 | tf_op jit(solution)/shard_map/ppermute | solution.py:459
  9.7 4.1 %copy-start = (f32[32]{0:T(128)S(1)}, f32[32]{0:T(128)}, u32[]{:S(2)}) copy-start(f32[32]{0:T(128)} %param.8) | copy-start | bytes 388
  11.8 5.9 %collective-permute-start.4 = (bf16[32,256]{1,0:T(8,128)(2,1)S(1)}, bf16[32,256]{1,0:T(8,128)(2,1)S(1)}, u32[]{:S(2)}, u32[]{:S(2)}) collective-permute-start(bf16[32,256]{1,0:T(8,128)(2,1)S(1)} %collective-permute-done.near_ref), channel_id=1, source_target_pairs={{0,6},{1,7},{2,0},{3,1},{4,2},{5,3},{6,4},{7,5},{8,14},{9,15},{10,... | collective-permute-start | bytes 49160 | tf_op jit(solution)/shard_map/ppermute | solution.py:459
  13.8 5.5 %collective-permute-start.3 = (bf16[32,256]{1,0:T(8,128)(2,1)S(1)}, bf16[32,256]{1,0:T(8,128)(2,1)S(1)}, u32[]{:S(2)}, u32[]{:S(2)}) collective-permute-start(bf16[32,256]{1,0:T(8,128)(2,1)S(1)} %collective-permute-done.near_ref), channel_id=1, source_target_pairs={{0,2},{1,3},{2,4},{3,5},{4,6},{5,7},{6,0},{7,1},{8,10},{9,11},{10,... | collective-permute-start | bytes 49160 | tf_op jit(solution)/shard_map/ppermute | solution.py:459
  19.3 8.1 %copy-start.1 = (f32[32]{0:T(128)S(1)}, f32[32]{0:T(128)}, u32[]{:S(2)}) copy-start(f32[32]{0:T(128)} %param.10) | copy-start | bytes 388
  21.5 1.4 %collective-permute-start.5 = (f32[32,896]{1,0:T(8,128)S(1)}, f32[32,896]{1,0:T(8,128)S(1)}, u32[]{:S(2)}, u32[]{:S(2)}) collective-permute-start(f32[32,896]{1,0:T(8,128)S(1)} %get-tuple-element.53), channel_id=1, source_target_pairs={{0,8},{1,9},{2,10},{3,11},{4,12},{5,13},{6,14},{7,15},{8,0},{9,1},... | collective-permute-start | bytes 344072 | tf_op jit(solution)/shard_map/ppermute | solution.py:459
  23.0 7.8 %collective-permute-start.8 = (bf16[32,896]{1,0:T(8,128)(2,1)S(1)}, bf16[32,896]{1,0:T(8,128)(2,1)S(1)}, u32[]{:S(2)}, u32[]{:S(2)}) collective-permute-start(bf16[32,896]{1,0:T(8,128)(2,1)S(1)} %add.3.refs_0_), channel_id=1, source_target_pairs={{0,6},{1,7},{2,4},{3,5},{4,2},{5,3},{6,0},{7,1},{8,14},{9,15},{10,... | collective-permute-start | bytes 172040 | tf_op jit(solution)/shard_map/ppermute | solution.py:459
  25.3 6.0 %collective-permute-start.7 = (bf16[32,896]{1,0:T(8,128)(2,1)S(1)}, bf16[32,896]{1,0:T(8,128)(2,1)S(1)}, u32[]{:S(2)}, u32[]{:S(2)}) collective-permute-start(bf16[32,896]{1,0:T(8,128)(2,1)S(1)} %add.3.refs_0_), channel_id=1, source_target_pairs={{0,4},{1,5},{2,6},{3,7},{4,0},{5,1},{6,2},{7,3},{8,12},{9,13},{10,... | collective-permute-start | bytes 172040 | tf_op jit(solution)/shard_map/ppermute | solution.py:459
  25.3 6.0 %collective-permute-start.6 = (bf16[32,896]{1,0:T(8,128)(2,1)S(1)}, bf16[32,896]{1,0:T(8,128)(2,1)S(1)}, u32[]{:S(2)}, u32[]{:S(2)}) collective-permute-start(bf16[32,896]{1,0:T(8,128)(2,1)S(1)} %add.3.refs_0_), channel_id=1, source_target_pairs={{0,2},{1,3},{2,0},{3,1},{4,6},{5,7},{6,4},{7,5},{8,10},{9,11},{10,... | collective-permute-start | bytes 172040 | tf_op jit(solution)/shard_map/ppermute | solution.py:459
  31.5 5.1 %collective-permute-start.11 = (bf16[32,896]{1,0:T(8,128)(2,1)S(1)}, bf16[32,896]{1,0:T(8,128)(2,1)S(1)}, u32[]{:S(2)}, u32[]{:S(2)}) collective-permute-start(bf16[32,896]{1,0:T(8,128)(2,1)S(1)} %add.4.refs_0_), channel_id=1, source_target_pairs={{0,17},{1,16},{2,19},{3,18},{4,21},{5,20},{6,23},{7,22},{8,25},{9,... | collective-permute-start | bytes 172040 | tf_op jit(solution)/shard_map/ppermute | solution.py:459
  33.9 4.2 %collective-permute-start.10 = (bf16[32,896]{1,0:T(8,128)(2,1)S(1)}, bf16[32,896]{1,0:T(8,128)(2,1)S(1)}, u32[]{:S(2)}, u32[]{:S(2)}) collective-permute-start(bf16[32,896]{1,0:T(8,128)(2,1)S(1)} %add.4.refs_0_), channel_id=1, source_target_pairs={{0,16},{1,17},{2,18},{3,19},{4,20},{5,21},{6,22},{7,23},{8,24},{9,... | collective-permute-start | bytes 172040 | tf_op jit(solution)/shard_map/ppermute | solution.py:459
  34.4 4.2 %collective-permute-start.9 = (bf16[32,896]{1,0:T(8,128)(2,1)S(1)}, bf16[32,896]{1,0:T(8,128)(2,1)S(1)}, u32[]{:S(2)}, u32[]{:S(2)}) collective-permute-start(bf16[32,896]{1,0:T(8,128)(2,1)S(1)} %add.4.refs_0_), channel_id=1, source_target_pairs={{0,1},{1,0},{2,3},{3,2},{4,5},{5,4},{6,7},{7,6},{8,9},{9,8},{10,11... | collective-permute-start | bytes 172040 | tf_op jit(solution)/shard_map/ppermute | solution.py:459
  38.7 1.3 %collective-permute-start.12 = (f32[32,896]{1,0:T(8,128)S(1)}, f32[32,896]{1,0:T(8,128)S(1)}, u32[]{:S(2)}, u32[]{:S(2)}) collective-permute-start(f32[32,896]{1,0:T(8,128)S(1)} %add.5.mine_ref), channel_id=1, source_target_pairs={{0,8},{1,9},{2,10},{3,11},{4,12},{5,13},{6,14},{7,15},{8,0},{9,1},... | collective-permute-start | bytes 344072 | tf_op jit(solution)/shard_map/ppermute | solution.py:459

commit v5 on v4

--- a/solution.py
+++ b/solution.py
@@ -129,7 +129,8 @@
     )(*in_vmem(held))
 
 
-def bands_kernel(ny, w1_ref, w2_ref, t1_ref, tv_ref, t2_ref):
+def bands_kernel(ny, w1_ref, w2_ref, edge_ref, t1_ref, tv_ref, t2_ref, copy_ref):
+    copy_ref[...] = edge_ref[...]
     ch = w1_ref.shape[-1]
     rows = ny * ch
     lane = iota((ch, rows), 1)
@@ -163,25 +164,25 @@
                 out[a, y * ch : (y + 1) * ch, c * rows : (c + 1) * rows] = block.astype(BF)
 
 
-def bands(first_weight, second_weight, ny):
+def bands(first_weight, second_weight, edge, ny):
     ch = first_weight.shape[-1]
     rows = ch * ny
     return pl.pallas_call(
         functools.partial(bands_kernel, ny),
-        out_shape=(pltpu.VMEM((3, rows, 3 * rows), BF),) * 3,
+        out_shape=(pltpu.VMEM((3, rows, 3 * rows), BF),) * 3 + (pltpu.VMEM(edge.shape, BF),),
         compiler_params=params(3),
         cost_estimate=pl.CostEstimate(flops=1_000_000_000, bytes_accessed=4_000_000, transcendentals=0),
         name="bands",
-    )(*in_vmem(first_weight, second_weight))
-
-
-def shifted_rows(out, row, block, before, after, rows):
+    )(*in_vmem(first_weight, second_weight, edge))
+
+
+def shifted_rows(out, row, block, ends, rows):
     lane = iota(block.shape, 1)
     at = slice(row * LANES, (row + 1) * LANES)
     wide = block.astype(F32)
-    out[0:rows, at] = jnp.where(lane == 0, before, pltpu.roll(wide, 1, 1)).astype(BF)
+    out[0:rows, at] = jnp.where(lane == 0, ends, pltpu.roll(wide, 1, 1)).astype(BF)
     out[rows : 2 * rows, at] = block
-    out[2 * rows :, at] = jnp.where(lane == LANES - 1, after, pltpu.roll(wide, LANES - 1, 1)).astype(BF)
+    out[2 * rows :, at] = jnp.where(lane == LANES - 1, ends, pltpu.roll(wide, LANES - 1, 1)).astype(BF)
 
 
 def lane_to(edges, source, target):
@@ -191,18 +192,24 @@
 
 def fold_taps(product, ch, ny):
     rows = ch * ny
-    lane = iota((ch, rows), 1)
+    lane = iota((ch, LANES), 1)
     total = None
     for y in range(ny):
-        block = product[y * ch : (y + 1) * ch]
+        low = max(ch * (y - 1), 0)
+        high = min(ch * (y + 2), rows)
+        band = product[y * ch : (y + 1) * ch]
+        col = low // LANES
+        turn = ch * (y - 1) % LANES
+        part = lane_to(band[:, col * LANES : (col + 1) * LANES], turn, 0)
+        if (high - 1) // LANES > col:
+            rest = lane_to(band[:, (col + 1) * LANES : (col + 2) * LANES], turn, 0)
+            part = jnp.where(lane < LANES - turn, part, rest)
         if y == 0:
-            block = jnp.where(lane >= rows - ch, 0.0, block)
+            part = jnp.where(lane < ch, 0.0, part)
         if y == ny - 1:
-            block = jnp.where(lane < ch, 0.0, block)
-        if y != 1:
-            block = pltpu.roll(block, (ch * (1 - y)) % rows, 1)
-        total = block if total is None else total + block
-    return total[:, :LANES]
+            part = jnp.where(lane < 2 * ch, part, 0.0)
+        total = part if total is None else total + part
+    return total
 
 
 def place_taps(columns, folded, a, c, ch):
@@ -226,8 +233,8 @@
     return jnp.sum(folded, axis=1, keepdims=True)
 
 
-def silu(preact):
-    return (preact / (1.0 + jnp.exp(-preact))).astype(BF)
+def logistic(preact):
+    return 1.0 / (1.0 + jnp.exp(-preact))
 
 
 def bias_column(ref, ny):
@@ -235,6 +242,19 @@
     r, k = iota((ch, ch), 0), iota((ch, ch), 1)
     column = jnp.sum(jnp.where(r == k, ref[...], 0.0), axis=1, keepdims=True)
     return jnp.concatenate([column] * ny, axis=0)
+
+
+def end_columns(nx, sources):
+    n = sources[0][3].shape[0]
+    j, k = iota((LANES, n), 0), iota((LANES, n), 1)
+    row, side = j % 64 // 2, j % 2
+    column = jnp.where(j < 64, jnp.where(side == 0, 0, 3), jnp.where(side == 0, 4, 5))
+    out = None
+    for x, start, count, message in sources:
+        hit = (row >= x) & (row < x + count) & (k == column * nx + row - x + start)
+        part = mm(one_hot(hit), message)
+        out = part if out is None else out + part
+    return out
 
 
 def edge_columns(nx, sources):
@@ -257,9 +277,8 @@
     out[:, 0:m] = out[:, 0:m] + mm(t_ref[2], field[:, LANES:n])
 
 
-def gate(hidden_grad, preact):
-    logistic = 1.0 / (1.0 + jnp.exp(-preact))
-    return (hidden_grad * logistic * (1.0 + preact * (1.0 - logistic))).astype(BF)
+def gate(hidden_grad, preact, q):
+    return (hidden_grad * q * (1.0 + preact * (1.0 - q))).astype(BF)
 
 
 def tap_terms(upstream, taps, ch, ny):
@@ -282,19 +301,20 @@
     fs, gs, pre, grad, hid_ref, second_ref, first_ref,
 ):
     rows = ch * ny
-    edges = edge_columns(nx, ((2, nx + 2, 0, near_ref[...]),)).T
-    for src, dst, left, right in ((f_ref, fs, 16, 80), (g_ref, gs, 48, 112)):
+    ends = end_columns(nx, ((0, 0, nx, near_ref[...]),)).T
+    for src, dst, first in ((f_ref, fs, 0), (g_ref, gs, 64)):
         for x in range(nx):
             block = src[:, x * LANES : (x + 1) * LANES]
-            shifted_rows(dst, x, block, lane_to(edges, left + x + 2, 0), lane_to(edges, right + x + 2, LANES - 1), rows)
+            shifted_rows(dst, x, block, lane_to(ends, first + 2 * x + 1, 0), rows)
     conv_inside(t1_ref, fs, pre, nx)
     pre[...] = pre[...] + bias_column(bias_ref, ny)
     conv_inside(tv_ref, gs, grad, nx)
     n = (nx - 2) * LANES
     inside = slice(LANES, LANES + n)
     preact = pre[:, inside]
-    hid_ref[...] = silu(preact)
-    preact_grad = gate(grad[:, inside], preact)
+    q = logistic(preact)
+    hid_ref[...] = (preact * q).astype(BF)
+    preact_grad = gate(grad[:, inside], preact, q)
     window = lambda ref, a, c: ref[c * rows : (c + 1) * rows, a * LANES : a * LANES + n]
     second = tap_terms(hid_ref[...], lambda a, c: window(gs, a, c), ch, ny)
     first = tap_terms(None, lambda a, c: (preact_grad, window(fs, a, c)), ch, ny)
@@ -334,18 +354,19 @@
     ge,
 ):
     rows = ch * ny
-    edges = edge_columns(nx, ((0, 2, nx - 2, before_ref[...]), (nx + 2, nx + 4, 0, after_ref[...]))).T
-    for i, (dst, left, right) in enumerate(((fe, 16, 80), (ge, 48, 112))):
-        for j, (src, xx) in enumerate(((above_ref, 1), (below_ref, nx + 2))):
+    columns = end_columns(nx, ((0, nx - 1, 1, before_ref[...]), (1, 0, 1, after_ref[...]))).T
+    for i, dst in enumerate((fe, ge)):
+        for j, src in enumerate((above_ref, below_ref)):
             block = src[(i + 1) * rows : (i + 2) * rows]
-            shifted_rows(dst, j, block, lane_to(edges, left + xx, 0), lane_to(edges, right + xx, LANES - 1), rows)
+            shifted_rows(dst, j, block, lane_to(columns, 64 * i + 2 * j + 1, 0), rows)
 
     last = (nx - 1) * LANES
     ends = lambda ref: jnp.concatenate([ref[:, 0:LANES], ref[:, last:]], axis=1)
     both = lambda t, e: jnp.concatenate([mm(t[0], e[:, 0:LANES]), mm(t[2], e[:, LANES:])], axis=1)
     preact = ends(pre) + both(t1_ref, fe)
-    hid_ref[...] = silu(preact)
-    preact_grad = gate(ends(grad) + both(tv_ref, ge), preact)
+    q = logistic(preact)
+    hid_ref[...] = (preact * q).astype(BF)
+    preact_grad = gate(ends(grad) + both(tv_ref, ge), preact, q)
 
     def window(own, end, a, c):
         at = slice(c * rows, (c + 1) * rows)
@@ -383,11 +404,11 @@
     )(*in_vmem(t1, tv, fs, gs, pre, grad, second, first, above, below, before, after))
 
 
-def residual_kernel(
+def rim_kernel(
     nx, ch, ny,
-    t1_ref, t2_ref, h_ref, h_end_ref, fs_ref, fe_ref, f_ref, above_ref, below_ref, near_ref, before_ref, after_ref, bias1_ref, bias2_ref,
-    o_ref,
-    ends, hs,
+    t1_ref, h_ref, h_end_ref, fs_ref, fe_ref, f_ref, above_ref, below_ref, near_ref, before_ref, after_ref, bias_ref,
+    hs,
+    ends,
 ):
     rows = ch * ny
     above, below = above_ref[0:rows], below_ref[0:rows]
@@ -400,8 +421,10 @@
     for x in range(nx + 4):
         edges_t = edges_t + mm_nt(one_hot((j % 16 == x) & (k == own_end)), unshifted[x])
     edges = edges_t.T
-    shifted_rows(ends, 0, above, lane_to(edges, 16, 0), lane_to(edges, 80, LANES - 1), rows)
-    shifted_rows(ends, 1, below, lane_to(edges, 16 + nx + 3, 0), lane_to(edges, 80 + nx + 3, LANES - 1), rows)
+    lane = iota((rows, LANES), 1)
+    both = lambda left, right: jnp.where(lane == 0, lane_to(edges, left, 0), lane_to(edges, right, LANES - 1))
+    shifted_rows(ends, 0, above, both(16, 80), rows)
+    shifted_rows(ends, 1, below, both(16 + nx + 3, 80 + nx + 3), rows)
     acc = None
     row = lambda x: fs_ref[:, x * LANES : (x + 1) * LANES]
     pairs = ((ends[:, 0:LANES], row(nx - 1)), (fe_ref[:, 0:LANES], fe_ref[:, LANES:]), (row(0), ends[:, LANES:]))
@@ -409,7 +432,8 @@
         columns = [lane_to(edges, 16 * c + a, 0).astype(BF) for c in range(3)]
         term = mm(t1_ref[a], jnp.concatenate([*pairs[a], jnp.concatenate(columns, axis=0)], axis=1))
         acc = term if acc is None else acc + term
-    hidden = silu(acc + bias_column(bias1_ref, ny))
+    preact = acc + bias_column(bias_ref, ny)
+    hidden = (preact * logistic(preact)).astype(BF)
     outer = hidden[:, 2 * LANES :].astype(F32)
     for x in range(nx + 2):
         if x == 0:
@@ -422,12 +446,29 @@
             block = h_end_ref[:, LANES:]
         else:
             block = h_ref[:, (x - 2) * LANES : (x - 1) * LANES]
-        shifted_rows(hs, x, block, lane_to(outer, x, 0), lane_to(outer, 64 + x, LANES - 1), rows)
-    n5 = nx * LANES
-    acc = mm(t2_ref[0], hs[:, 0:n5])
+        shifted_rows(hs, x, block, jnp.where(lane == 0, lane_to(outer, x, 0), lane_to(outer, 64 + x, LANES - 1)), rows)
+
+
+def rim(t1, hidden, hidden_end, fs, fe, field, above, below, near, before, after, bias, ch, ny):
+    rows = ch * ny
+    nx = field.shape[1] // LANES
+    return pl.pallas_call(
+        functools.partial(rim_kernel, nx, ch, ny),
+        out_shape=pltpu.VMEM((3 * rows, (nx + 2) * LANES), BF),
+        scratch_shapes=[pltpu.VMEM((3 * rows, 2 * LANES), BF)],
+        compiler_params=params(6),
+        cost_estimate=pl.CostEstimate(flops=1_000_000_000, bytes_accessed=3_000_000, transcendentals=0),
+        name="rim",
+    )(*in_vmem(t1, hidden, hidden_end, fs, fe, field, above, below, near, before, after, bias))
+
+
+def residual_kernel(nx, ch, ny, t2_ref, hs, f_ref, bias_ref, o_ref):
+    rows = ch * ny
+    n = nx * LANES
+    acc = mm(t2_ref[0], hs[:, 0:n])
     for a in range(1, 3):
-        acc = acc + mm(t2_ref[a], hs[:, a * LANES : a * LANES + n5])
-    total = (f_ref[...].astype(F32) + (acc + bias_column(bias2_ref, ny))).astype(BF)
+        acc = acc + mm(t2_ref[a], hs[:, a * LANES : a * LANES + n])
+    total = (f_ref[...].astype(F32) + (acc + bias_column(bias_ref, ny))).astype(BF)
     r, k = iota((rows, rows), 0), iota((rows, rows), 1)
     back = one_hot(k == (r % ny) * ch + r // ny)
     ordered = mm(back, total)
@@ -435,17 +476,15 @@
         o_ref[0, :, x] = ordered[:, x * LANES : (x + 1) * LANES].reshape(ch, ny, LANES).astype(BF)
 
 
-def residual(t1, t2, hidden, hidden_end, fs, fe, field, above, below, near, before, after, bias1, bias2, ch, ny):
-    rows = ch * ny
+def residual(t2, hs, field, bias, ch, ny):
     nx = field.shape[1] // LANES
     return pl.pallas_call(
         functools.partial(residual_kernel, nx, ch, ny),
         out_shape=jax.ShapeDtypeStruct((1, ch, nx, ny, LANES), BF),
-        scratch_shapes=[pltpu.VMEM((3 * rows, 2 * LANES), BF), pltpu.VMEM((3 * rows, (nx + 2) * LANES), BF)],
-        compiler_params=params(8),
+        compiler_params=params(6),
         cost_estimate=pl.CostEstimate(flops=3_000_000_000, bytes_accessed=3_000_000, transcendentals=0),
         name="residual",
-    )(*in_vmem(t1, t2, hidden, hidden_end, fs, fe, field, above, below, near, before, after, bias1, bias2))
+    )(*in_vmem(t2, hs, field, bias))
 
 
 def moved(array, sizes, step):
@@ -459,9 +498,9 @@
     return lax.ppermute(array, AXES, pairs)
 
 
-def along(array, sizes, dx):
+def along(array, sizes, dx, dz=0):
     ns, nx, nz = sizes
-    return moved(array, sizes, lambda s, x, z: (s, (x + dx) % nx, z))
+    return moved(array, sizes, lambda s, x, z: (s, (x + dx) % nx, (z + dz) % nz))
 
 
 def swapped(array, sizes, bits):
@@ -502,15 +541,20 @@
     return [sent] + [swapped(sent, sizes, step) for step in steps[1:]]
 
 
-def sum_all(keep, give, sizes, output):
+def sum_all(keep, give, sizes, hs, finish):
     near = (1, 0, 0)
     bits = [(0, 1 << i, 0) for i in range(sizes[1].bit_length() - 1)]
-    bits += [(0, 0, 1 << i) for i in range(sizes[2].bit_length() - 1)]
-    bits += [(1 << i, 0, 0) for i in range(1, sizes[0].bit_length() - 1)]
+    flat = [(0, 0, 1 << i) for i in range(sizes[2].bit_length() - 1)]
+    flat += [(1 << i, 0, 0) for i in range(1, sizes[0].bit_length() - 1)]
+    groups = [flat[i : i + 2] for i in range(0, len(flat), 2)] + [bits[i : i + 2] for i in range(0, len(bits), 2)]
     terms = [keep, swapped(give, sizes, near)]
-    for i in range(0, len(bits), 2):
-        terms = exchange(add(terms, BF), sizes, bits[i : i + 2])
+    output = None
+    for i, group in enumerate(groups):
+        terms = exchange(add(terms, BF), sizes, group)
         if i == 0:
+            *terms, hs = lax.optimization_barrier((*terms, hs))
+            output = finish(hs)
+        elif i == 1:
             *terms, output = lax.optimization_barrier((*terms, output))
     mine = add(terms, F32)
     return mine, swapped(mine, sizes, near), output
@@ -555,15 +599,15 @@
     above, below = along(up, sizes, 1), along(down, sizes, -1)
     field, cot, edge = pack(held)
     near = swapped(edge, sizes, (0, 0, 1))
-    before, after = along(near, sizes, 1), along(near, sizes, -1)
-    t1, tv, t2 = bands(weight1, weight2, ny)
+    t1, tv, t2, edge = bands(weight1, weight2, edge, ny)
+    before, after = along(edge, sizes, 1, 1), along(edge, sizes, -1, 1)
     bias1, bias2 = first_bias.reshape(1, ch), second_bias.reshape(1, ch)
     fs, gs, pre, grad, hidden, second, first = inner(t1, tv, field, cot, near, bias1, ch, ny)
     hidden_end, fe, keep, give = outer(
         t1, tv, fs, gs, pre, grad, second, first, above, below, before, after, ch, ny, scale
     )
-    output = residual(t1, t2, hidden, hidden_end, fs, fe, field, above, below, near, before, after, bias1, bias2, ch, ny)
-    mine, other, output = sum_all(keep, give, sizes, output)
+    hs = rim(t1, hidden, hidden_end, fs, fe, field, above, below, near, before, after, bias1, ch, ny)
+    mine, other, output = sum_all(keep, give, sizes, hs, lambda hs: residual(t2, hs, field, bias2, ch, ny))
     return output, *spread(mine, other, ch)
 
 

time: 41.4 us -> 39.3 us (0.949)
  waiting for transfers between devices: 9.78 us -> 6.96 us
  starting transfers between devices: 16.8 us -> 17.8 us
    ppermute x13, waiting for transfers between devices: 9.78 us -> 6.96 us  [moved(): return lax.ppermute(array, AXES, pairs)]
    pallas_call x0 -> x1, Pallas kernels: none -> 1.79 us  [rim(): pl.pallas_call(functools.partial(rim_kernel, nx, ch, ny), out_shape=pltpu...]
    pallas_call x1, Pallas kernels: 3.42 us -> 2.06 us  [residual(): pl.pallas_call(functools.partial(residual_kernel, nx, ch, ny), out_shape=...]
    ppermute x13, starting transfers between devices: 16.8 us -> 17.8 us  [moved(): return lax.ppermute(array, AXES, pairs)]
  transfers between devices with their start and end apart: 13 -> 13, of which waited for: 8 -> 8; matrix products, arithmetic and copies ran while one was open for 0% -> 0% of each run, Pallas kernels for 21% -> 22%
where the time goes in v5:
time: 39.3 us; the launch traced here: 39.2 us
  starting transfers between devices  17.8 us (45%)
  Pallas kernels  13.7 us (35%)
  waiting for transfers between devices  6.96 us (18%)
  between operations  0.7 us (2%)
    ppermute x13, starting transfers between devices, moved(): return lax.ppermute(array, AXES, pairs)  17.8 us
    ppermute x13, waiting for transfers between devices, moved(): return lax.ppermute(array, AXES, pairs)  6.96 us
    pallas_call x1, Pallas kernels, inner(): pl.pallas_call(functools.partial(inner_kernel, nx, ch, ny), out_shape=(sd...  3.59 us
    pallas_call x1, Pallas kernels, residual(): pl.pallas_call(functools.partial(residual_kernel, nx, ch, ny), out_shape=...  2.06 us
    pallas_call x1, Pallas kernels, outer(): pl.pallas_call(functools.partial(outer_kernel, nx, ch, ny, scale), out_sh...  1.84 us
    pallas_call x1, Pallas kernels, rim(): pl.pallas_call(functools.partial(rim_kernel, nx, ch, ny), out_shape=pltpu...  1.79 us
    pallas_call x1, Pallas kernels, faces(): pl.pallas_call(functools.partial(faces_kernel, nx, ch, ny), out_shape=(sd...  1.44 us
    pallas_call x1, Pallas kernels, spread(): pl.pallas_call(functools.partial(spread_kernel, ch), out_shape=(taps, bia...  1.2 us
  transfers between devices with their start and end apart: 13, of which 8 were waited for; matrix products, arithmetic and copies ran while one was open for 0% of the time, Pallas kernels for 22%

profile of v5, /device:TPU:0, one launch (start us, length us, event | category | flops | bytes accessed | tf_op | source)
XLA Modules:
  0.0 39.2 jit_solution(3153768302952144903)
XLA Ops:
  0.6 1.4 %faces.1 = (bf16[768,128]{1,0:T(8,128)(2,1)S(1)}, bf16[768,128]{1,0:T(8,128)(2,1)S(1)}, bf16[2,5,32,8,128]{4,3,2,1,0:T(8,128)(2,1)S(1)}, bf16[3,3,3,32,32]{4,3,2...) custom-call(bf16[1,32,5,8,128]{4,3,2,1,0:T(8,128)(2,1)} %f_any.1, bf16[1,32,5,8,128]{4,3,2,1,0:T(8,128)(2,1)} %g_any.1, ...), custom_call_target="tpu_custom_call" | custom-call | tf_op jit(solution)/shard_map/faces/pallas_call | solution.py:84
  2.1 3.1 %collective-permute-start.1 = (bf16[768,128]{1,0:T(8,128)(2,1)S(1)}, bf16[768,128]{1,0:T(8,128)(2,1)S(1)}, u32[]{:S(2)}, u32[]{:S(2)}) collective-permute-start(bf16[768,128]{1,0:T(8,128)(2,1)S(1)} %get-tuple-element.56), channel_id=1, source_target_pairs={{0,2},{1,3},{2,4},{3,5},{4,6},{5,7},{6,0},{7,1},{8,10},{9,11},{10,... | collective-permute-start | bytes 589832 | tf_op jit(solution)/shard_map/ppermute | solution.py:498
  5.2 2.1 %collective-permute-start.2 = (bf16[768,128]{1,0:T(8,128)(2,1)S(1)}, bf16[768,128]{1,0:T(8,128)(2,1)S(1)}, u32[]{:S(2)}, u32[]{:S(2)}) collective-permute-start(bf16[768,128]{1,0:T(8,128)(2,1)S(1)} %get-tuple-element.57), channel_id=1, source_target_pairs={{0,6},{1,7},{2,0},{3,1},{4,2},{5,3},{6,4},{7,5},{8,14},{9,15},{10,... | collective-permute-start | bytes 589832 | tf_op jit(solution)/shard_map/ppermute | solution.py:498
  7.2 0.8 %pack.1 = (bf16[256,640]{1,0:T(8,128)(2,1)S(1)}, bf16[256,640]{1,0:T(8,128)(2,1)S(1)}, bf16[32,256]{1,0:T(8,128)(2,1)S(1)}) custom-call(bf16[2,5,32,8,128]{4,3,2,1,0:T(8,128)(2,1)S(1)} %get-tuple-element.44.held), custom_call_target="tpu_custom_call" | custom-call | flops 500000000 | bytes 1000000 | tf_op jit(solution)/shard_map/pack/pallas_call | solution.py:122
  8.1 1.7 %collective-permute-start = (bf16[32,256]{1,0:T(8,128)(2,1)S(1)}, bf16[32,256]{1,0:T(8,128)(2,1)S(1)}, u32[]{:S(2)}, u32[]{:S(2)}) collective-permute-start(bf16[32,256]{1,0:T(8,128)(2,1)S(1)} %get-tuple-element.45.edge_ref), channel_id=1, source_target_pairs={{0,1},{1,0},{2,3},{3,2},{4,5},{5,4},{6,7},{7,6},{8,9},{9,8},{10,11... | collective-permute-start | bytes 49160 | tf_op jit(solution)/shard_map/ppermute | solution.py:498
  9.7 0.6 %bands.1 = (bf16[3,256,768]{2,1,0:T(8,128)(2,1)S(1)}, bf16[3,256,768]{2,1,0:T(8,128)(2,1)S(1)}, bf16[3,256,768]{2,1,0:T(8,128)(2,1)S(1)}, bf16[32,256]{1,0:T(8,128)(2,1)S(1)}) custom-call(bf16[3,3,3,32,32]{4,3,2,1,0:T(8,128)(2,1)S(1)} %get-tuple-element.42.w1_ref, bf16[3,3,3,32,32]{4,3,2,1,0:T(8,128)(2,1)S(1)} %get-tuple-element.43.w2_ref, ...), custom_call_target="tpu_custom_call" | custom-call | flops 1000000000 | bytes 4000000 | tf_op jit(solution)/shard_map/bands/pallas_call | solution.py:170
  10.3 1.8 %collective-permute-start.4 = (bf16[32,256]{1,0:T(8,128)(2,1)S(1)}, bf16[32,256]{1,0:T(8,128)(2,1)S(1)}, u32[]{:S(2)}, u32[]{:S(2)}) collective-permute-start(bf16[32,256]{1,0:T(8,128)(2,1)S(1)} %get-tuple-element.58), channel_id=1, source_target_pairs={{0,7},{1,6},{2,1},{3,0},{4,3},{5,2},{6,5},{7,4},{8,15},{9,14},{10,... | collective-permute-start | bytes 49160 | tf_op jit(solution)/shard_map/ppermute | solution.py:498
  12.1 1.2 %collective-permute-start.3 = (bf16[32,256]{1,0:T(8,128)(2,1)S(1)}, bf16[32,256]{1,0:T(8,128)(2,1)S(1)}, u32[]{:S(2)}, u32[]{:S(2)}) collective-permute-start(bf16[32,256]{1,0:T(8,128)(2,1)S(1)} %get-tuple-element.58), channel_id=1, source_target_pairs={{0,3},{1,2},{2,5},{3,4},{4,7},{5,6},{6,1},{7,0},{8,11},{9,10},{10,... | collective-permute-start | bytes 49160 | tf_op jit(solution)/shard_map/ppermute | solution.py:498
  13.3 3.6 %inner.1 = (bf16[768,640]{1,0:T(8,128)(2,1)S(1)}, bf16[768,640]{1,0:T(8,128)(2,1)S(1)}, f32[256,640]{1,0:T(8,128)S(1)}, f32[256,640]{1,0:T(8,128)S(1)}, bf16[256...) custom-call(bf16[3,256,768]{2,1,0:T(8,128)(2,1)S(1)} %get-tuple-element.46.t1_ref, ...), custom_call_target="tpu_custom_call" | custom-call | flops 2000000000 | bytes 4000000 | tf_op jit(solution)/shard_map/inner/pallas_call | solution.py:333
  16.9 0.3 collective-permute-done.4.after_ref
  17.2 1.4 %collective-permute-done.3.before_ref = bf16[32,256]{1,0:T(8,128)(2,1)S(1)} collective-permute-done((bf16[32,256]{1,0:T(8,128)(2,1)S(1)}, bf16[32,256]{1,0:T(8,128)(2,1)S(1)}, u32[]{:S(2)}, u32[]{:S(2)}) %collective-permute-start.3) | collective-permute-done | bytes 16416 | tf_op jit(solution)/shard_map/ppermute | solution.py:498
  18.6 0.0 collective-permute-done.2.below_ref
  18.6 1.8 %outer.1 = (bf16[256,256]{1,0:T(8,128)(2,1)S(1)}, bf16[768,256]{1,0:T(8,128)(2,1)S(1)}, f32[32,896]{1,0:T(8,128)S(1)}, f32[32,896]{1,0:T(8,128)S(1)}) custom-call(bf16[3,256,768]{2,1,0:T(8,128)(2,1)S(1)} %get-tuple-element.46.t1_ref, bf16[3,256,768]{2,1,0:T(8,128)(2,1)S(1)} %get-tuple-element.47.tv_ref, bf16[768,640]{1,0:T(8,128)(2,1)S(1)} %get-tuple-element.50.fs.fs_ref, ...), custom_call_target="tpu_custom_call" | custom-call | tf_op jit(solution)/shard_map/outer/pallas_call | solution.py:393
  20.4 0.1 collective-permute-start.5
  20.5 1.3 %collective-permute-done.5.refs_1_ = f32[32,896]{1,0:T(8,128)S(1)} collective-permute-done((f32[32,896]{1,0:T(8,128)S(1)}, f32[32,896]{1,0:T(8,128)S(1)}, u32[]{:S(2)}, u32[]{:S(2)}) %collective-permute-start.5) | collective-permute-done | bytes 114720 | tf_op jit(solution)/shard_map/ppermute | solution.py:498
  21.8 0.1 add.3.refs_0_
  22.0 2.5 %collective-permute-start.8 = (bf16[32,896]{1,0:T(8,128)(2,1)S(1)}, bf16[32,896]{1,0:T(8,128)(2,1)S(1)}, u32[]{:S(2)}, u32[]{:S(2)}) collective-permute-start(bf16[32,896]{1,0:T(8,128)(2,1)S(1)} %add.3.refs_0_), channel_id=1, source_target_pairs={{0,17},{1,16},{2,19},{3,18},{4,21},{5,20},{6,23},{7,22},{8,25},{9,... | collective-permute-start | bytes 172040 | tf_op jit(solution)/shard_map/ppermute | solution.py:498
  24.4 0.5 %collective-permute-start.7 = (bf16[32,896]{1,0:T(8,128)(2,1)S(1)}, bf16[32,896]{1,0:T(8,128)(2,1)S(1)}, u32[]{:S(2)}, u32[]{:S(2)}) collective-permute-start(bf16[32,896]{1,0:T(8,128)(2,1)S(1)} %add.3.refs_0_), channel_id=1, source_target_pairs={{0,16},{1,17},{2,18},{3,19},{4,20},{5,21},{6,22},{7,23},{8,24},{9,... | collective-permute-start | bytes 172040 | tf_op jit(solution)/shard_map/ppermute | solution.py:498
  24.9 0.5 %collective-permute-start.6 = (bf16[32,896]{1,0:T(8,128)(2,1)S(1)}, bf16[32,896]{1,0:T(8,128)(2,1)S(1)}, u32[]{:S(2)}, u32[]{:S(2)}) collective-permute-start(bf16[32,896]{1,0:T(8,128)(2,1)S(1)} %add.3.refs_0_), channel_id=1, source_target_pairs={{0,1},{1,0},{2,3},{3,2},{4,5},{5,4},{6,7},{7,6},{8,9},{9,8},{10,11... | collective-permute-start | bytes 172040 | tf_op jit(solution)/shard_map/ppermute | solution.py:498
  25.4 1.8 %rim.1.hs = bf16[768,896]{1,0:T(8,128)(2,1)S(1)} custom-call(bf16[3,256,768]{2,1,0:T(8,128)(2,1)S(1)} %get-tuple-element.46.t1_ref, bf16[256,384]{1,0:T(8,128)(2,1)S(1)} %get-tuple-element.61.h_ref, bf16[256,256]{1,0:T(8,128)(2,1)S(1)} %get-tuple-element.62.h_end_ref, bf16[768,640]{1,0:T(8,128)(2,1)S(1)} %get-tuple-element.50.fs.fs_ref, ...), custom_call_target="tpu_custom_call" | custom-call | flops 1000000000 | bytes 3000000 | tf_op jit(solution)/shard_map/rim/pallas_call | solution.py:455
  27.3 1.3 %collective-permute-done.7.refs_2_ = bf16[32,896]{1,0:T(8,128)(2,1)S(1)} collective-permute-done((bf16[32,896]{1,0:T(8,128)(2,1)S(1)}, bf16[32,896]{1,0:T(8,128)(2,1)S(1)}, u32[]{:S(2)}, u32[]{:S(2)}) %collective-permute-start.7) | collective-permute-done | bytes 57376 | tf_op jit(solution)/shard_map/ppermute | solution.py:498
  28.6 0.5 %collective-permute-done.6.refs_1_ = bf16[32,896]{1,0:T(8,128)(2,1)S(1)} collective-permute-done((bf16[32,896]{1,0:T(8,128)(2,1)S(1)}, bf16[32,896]{1,0:T(8,128)(2,1)S(1)}, u32[]{:S(2)}, u32[]{:S(2)}) %collective-permute-start.6) | collective-permute-done | bytes 57376 | tf_op jit(solution)/shard_map/ppermute | solution.py:498
  29.1 0.2 add.4.refs_0_
  29.3 1.0 %collective-permute-start.11 = (bf16[32,896]{1,0:T(8,128)(2,1)S(1)}, bf16[32,896]{1,0:T(8,128)(2,1)S(1)}, u32[]{:S(2)}, u32[]{:S(2)}) collective-permute-start(bf16[32,896]{1,0:T(8,128)(2,1)S(1)} %add.4.refs_0_), channel_id=1, source_target_pairs={{0,6},{1,7},{2,4},{3,5},{4,2},{5,3},{6,0},{7,1},{8,14},{9,15},{10,... | collective-permute-start | bytes 172040 | tf_op jit(solution)/shard_map/ppermute | solution.py:498
  30.3 3.4 %collective-permute-start.9 = (bf16[32,896]{1,0:T(8,128)(2,1)S(1)}, bf16[32,896]{1,0:T(8,128)(2,1)S(1)}, u32[]{:S(2)}, u32[]{:S(2)}) collective-permute-start(bf16[32,896]{1,0:T(8,128)(2,1)S(1)} %add.4.refs_0_), channel_id=1, source_target_pairs={{0,2},{1,3},{2,0},{3,1},{4,6},{5,7},{6,4},{7,5},{8,10},{9,11},{10,... | collective-permute-start | bytes 172040 | tf_op jit(solution)/shard_map/ppermute | solution.py:498
  33.7 2.1 %residual.1 = bf16[1,32,5,8,128]{4,3,2,1,0:T(8,128)(2,1)} custom-call(bf16[3,256,768]{2,1,0:T(8,128)(2,1)S(1)} %get-tuple-element.68.t2_ref, bf16[768,896]{1,0:T(8,128)(2,1)S(1)} %rim.1.hs, bf16[256,640]{1,0:T(8,128)(2,1)S(1)} %get-tuple-element.48.f_ref, f32[1,32]{1,0:T(1,128)S(1)} %bitcast.10), custom_call_target="tpu_custom_call" | custom-call | flops 3000000000 | bytes 3000000 | tf_op jit(solution)/shard_map/residual/pallas_call | solution.py:481
  35.7 0.1 collective-permute-done.11.refs_3_
  35.8 0.7 %collective-permute-done.10.refs_2_ = bf16[32,896]{1,0:T(8,128)(2,1)S(1)} collective-permute-done((bf16[32,896]{1,0:T(8,128)(2,1)S(1)}, bf16[32,896]{1,0:T(8,128)(2,1)S(1)}, u32[]{:S(2)}, u32[]{:S(2)}) %collective-permute-start.10) | collective-permute-done | bytes 57376 | tf_op jit(solution)/shard_map/ppermute | solution.py:498
  36.5 0.1 add.5.mine_ref
  36.6 0.0 collective-permute-start.12
  36.6 1.3 %collective-permute-done.12.other_ref = f32[32,896]{1,0:T(8,128)S(1)} collective-permute-done((f32[32,896]{1,0:T(8,128)S(1)}, f32[32,896]{1,0:T(8,128)S(1)}, u32[]{:S(2)}, u32[]{:S(2)}) %collective-permute-start.12) | collective-permute-done | bytes 114720 | tf_op jit(solution)/shard_map/ppermute | solution.py:498
  38.0 1.2 %spread.1 = (f32[3,3,3,32,32]{4,3,2,1,0:T(8,128)}, f32[1,32]{1,0:T(1,128)}, f32[3,3,3,32,32]{4,3,2,1,0:T(8,128)}, f32[1,32]{1,0:T(1,128)}) custom-call(f32[32,896]{1,0:T(8,128)S(1)} %add.5.mine_ref, f32[32,896]{1,0:T(8,128)S(1)} %collective-permute-done.12.other_ref), custom_call_target="tpu_custom_call" | custom-call | tf_op jit(solution)/shard_map/spread/pallas_call | solution.py:582
  (9 shorter events, 0.0 us)
Async XLA Ops:
  2.1 16.5 %collective-permute-start.1 = (bf16[768,128]{1,0:T(8,128)(2,1)S(1)}, bf16[768,128]{1,0:T(8,128)(2,1)S(1)}, u32[]{:S(2)}, u32[]{:S(2)}) collective-permute-start(bf16[768,128]{1,0:T(8,128)(2,1)S(1)} %get-tuple-element.56), channel_id=1, source_target_pairs={{0,2},{1,3},{2,4},{3,5},{4,6},{5,7},{6,0},{7,1},{8,10},{9,11},{10,... | collective-permute-start | bytes 589832 | tf_op jit(solution)/shard_map/ppermute | solution.py:498
  5.2 13.4 %collective-permute-start.2 = (bf16[768,128]{1,0:T(8,128)(2,1)S(1)}, bf16[768,128]{1,0:T(8,128)(2,1)S(1)}, u32[]{:S(2)}, u32[]{:S(2)}) collective-permute-start(bf16[768,128]{1,0:T(8,128)(2,1)S(1)} %get-tuple-element.57), channel_id=1, source_target_pairs={{0,6},{1,7},{2,0},{3,1},{4,2},{5,3},{6,4},{7,5},{8,14},{9,15},{10,... | collective-permute-start | bytes 589832 | tf_op jit(solution)/shard_map/ppermute | solution.py:498
  8.1 5.2 %collective-permute-start = (bf16[32,256]{1,0:T(8,128)(2,1)S(1)}, bf16[32,256]{1,0:T(8,128)(2,1)S(1)}, u32[]{:S(2)}, u32[]{:S(2)}) collective-permute-start(bf16[32,256]{1,0:T(8,128)(2,1)S(1)} %get-tuple-element.45.edge_ref), channel_id=1, source_target_pairs={{0,1},{1,0},{2,3},{3,2},{4,5},{5,4},{6,7},{7,6},{8,9},{9,8},{10,11... | collective-permute-start | bytes 49160 | tf_op jit(solution)/shard_map/ppermute | solution.py:498
  9.7 3.5 %copy-start = (f32[32]{0:T(128)S(1)}, f32[32]{0:T(128)}, u32[]{:S(2)}) copy-start(f32[32]{0:T(128)} %param.8) | copy-start | bytes 388
  10.3 6.9 %collective-permute-start.4 = (bf16[32,256]{1,0:T(8,128)(2,1)S(1)}, bf16[32,256]{1,0:T(8,128)(2,1)S(1)}, u32[]{:S(2)}, u32[]{:S(2)}) collective-permute-start(bf16[32,256]{1,0:T(8,128)(2,1)S(1)} %get-tuple-element.58), channel_id=1, source_target_pairs={{0,7},{1,6},{2,1},{3,0},{4,3},{5,2},{6,5},{7,4},{8,15},{9,14},{10,... | collective-permute-start | bytes 49160 | tf_op jit(solution)/shard_map/ppermute | solution.py:498
  12.1 6.4 %collective-permute-start.3 = (bf16[32,256]{1,0:T(8,128)(2,1)S(1)}, bf16[32,256]{1,0:T(8,128)(2,1)S(1)}, u32[]{:S(2)}, u32[]{:S(2)}) collective-permute-start(bf16[32,256]{1,0:T(8,128)(2,1)S(1)} %get-tuple-element.58), channel_id=1, source_target_pairs={{0,3},{1,2},{2,5},{3,4},{4,7},{5,6},{6,1},{7,0},{8,11},{9,10},{10,... | collective-permute-start | bytes 49160 | tf_op jit(solution)/shard_map/ppermute | solution.py:498
  20.4 1.4 %collective-permute-start.5 = (f32[32,896]{1,0:T(8,128)S(1)}, f32[32,896]{1,0:T(8,128)S(1)}, u32[]{:S(2)}, u32[]{:S(2)}) collective-permute-start(f32[32,896]{1,0:T(8,128)S(1)} %get-tuple-element.60), channel_id=1, source_target_pairs={{0,8},{1,9},{2,10},{3,11},{4,12},{5,13},{6,14},{7,15},{8,0},{9,1},... | collective-permute-start | bytes 344072 | tf_op jit(solution)/shard_map/ppermute | solution.py:498
  22.0 5.3 %collective-permute-start.8 = (bf16[32,896]{1,0:T(8,128)(2,1)S(1)}, bf16[32,896]{1,0:T(8,128)(2,1)S(1)}, u32[]{:S(2)}, u32[]{:S(2)}) collective-permute-start(bf16[32,896]{1,0:T(8,128)(2,1)S(1)} %add.3.refs_0_), channel_id=1, source_target_pairs={{0,17},{1,16},{2,19},{3,18},{4,21},{5,20},{6,23},{7,22},{8,25},{9,... | collective-permute-start | bytes 172040 | tf_op jit(solution)/shard_map/ppermute | solution.py:498
  24.4 4.2 %collective-permute-start.7 = (bf16[32,896]{1,0:T(8,128)(2,1)S(1)}, bf16[32,896]{1,0:T(8,128)(2,1)S(1)}, u32[]{:S(2)}, u32[]{:S(2)}) collective-permute-start(bf16[32,896]{1,0:T(8,128)(2,1)S(1)} %add.3.refs_0_), channel_id=1, source_target_pairs={{0,16},{1,17},{2,18},{3,19},{4,20},{5,21},{6,22},{7,23},{8,24},{9,... | collective-permute-start | bytes 172040 | tf_op jit(solution)/shard_map/ppermute | solution.py:498
  24.9 4.2 %collective-permute-start.6 = (bf16[32,896]{1,0:T(8,128)(2,1)S(1)}, bf16[32,896]{1,0:T(8,128)(2,1)S(1)}, u32[]{:S(2)}, u32[]{:S(2)}) collective-permute-start(bf16[32,896]{1,0:T(8,128)(2,1)S(1)} %add.3.refs_0_), channel_id=1, source_target_pairs={{0,1},{1,0},{2,3},{3,2},{4,5},{5,4},{6,7},{7,6},{8,9},{9,8},{10,11... | collective-permute-start | bytes 172040 | tf_op jit(solution)/shard_map/ppermute | solution.py:498
  25.4 8.2 %copy-start.1 = (f32[32]{0:T(128)S(1)}, f32[32]{0:T(128)}, u32[]{:S(2)}) copy-start(f32[32]{0:T(128)} %param.10) | copy-start | bytes 388
  29.3 6.6 %collective-permute-start.11 = (bf16[32,896]{1,0:T(8,128)(2,1)S(1)}, bf16[32,896]{1,0:T(8,128)(2,1)S(1)}, u32[]{:S(2)}, u32[]{:S(2)}) collective-permute-start(bf16[32,896]{1,0:T(8,128)(2,1)S(1)} %add.4.refs_0_), channel_id=1, source_target_pairs={{0,6},{1,7},{2,4},{3,5},{4,2},{5,3},{6,0},{7,1},{8,14},{9,15},{10,... | collective-permute-start | bytes 172040 | tf_op jit(solution)/shard_map/ppermute | solution.py:498
  30.3 6.3 %collective-permute-start.10 = (bf16[32,896]{1,0:T(8,128)(2,1)S(1)}, bf16[32,896]{1,0:T(8,128)(2,1)S(1)}, u32[]{:S(2)}, u32[]{:S(2)}) collective-permute-start(bf16[32,896]{1,0:T(8,128)(2,1)S(1)} %add.4.refs_0_), channel_id=1, source_target_pairs={{0,4},{1,5},{2,6},{3,7},{4,0},{5,1},{6,2},{7,3},{8,12},{9,13},{10,... | collective-permute-start | bytes 172040 | tf_op jit(solution)/shard_map/ppermute | solution.py:498
  30.3 6.3 %collective-permute-start.9 = (bf16[32,896]{1,0:T(8,128)(2,1)S(1)}, bf16[32,896]{1,0:T(8,128)(2,1)S(1)}, u32[]{:S(2)}, u32[]{:S(2)}) collective-permute-start(bf16[32,896]{1,0:T(8,128)(2,1)S(1)} %add.4.refs_0_), channel_id=1, source_target_pairs={{0,2},{1,3},{2,0},{3,1},{4,6},{5,7},{6,4},{7,5},{8,10},{9,11},{10,... | collective-permute-start | bytes 172040 | tf_op jit(solution)/shard_map/ppermute | solution.py:498
  36.6 1.3 %collective-permute-start.12 = (f32[32,896]{1,0:T(8,128)S(1)}, f32[32,896]{1,0:T(8,128)S(1)}, u32[]{:S(2)}, u32[]{:S(2)}) collective-permute-start(f32[32,896]{1,0:T(8,128)S(1)} %add.5.mine_ref), channel_id=1, source_target_pairs={{0,8},{1,9},{2,10},{3,11},{4,12},{5,13},{6,14},{7,15},{8,0},{9,1},... | collective-permute-start | bytes 344072 | tf_op jit(solution)/shard_map/ppermute | solution.py:498

commit v6 on v5

--- a/solution.py
+++ b/solution.py
@@ -242,6 +242,11 @@
     r, k = iota((ch, ch), 0), iota((ch, ch), 1)
     column = jnp.sum(jnp.where(r == k, ref[...], 0.0), axis=1, keepdims=True)
     return jnp.concatenate([column] * ny, axis=0)
+
+
+def sides(one, two):
+    even = is_even("gx")
+    return jnp.where(even, two, one), jnp.where(even, one, two)
 
 
 def end_columns(nx, sources):
@@ -342,19 +347,33 @@
             sds((ch, TERMS), F32),
         ),
         compiler_params=params(6),
-        cost_estimate=pl.CostEstimate(flops=2_000_000_000, bytes_accessed=4_000_000, transcendentals=0),
+        cost_estimate=pl.CostEstimate(flops=1000, bytes_accessed=1000, transcendentals=0),
         name="inner",
     )(*in_vmem(t1, tv, field, cot, near, bias))
 
 
+def corners_kernel(nx, one_ref, two_ref, columns_ref):
+    before, after = sides(one_ref[...], two_ref[...])
+    columns_ref[...] = end_columns(nx, ((0, nx - 1, 1, before), (1, 0, 1, after))).T
+
+
+def corners(one, two, nx):
+    return pl.pallas_call(
+        functools.partial(corners_kernel, nx),
+        out_shape=pltpu.VMEM((one.shape[1], LANES), F32),
+        compiler_params=params(1),
+        name="corners",
+    )(*in_vmem(one, two))
+
+
 def outer_kernel(
     nx, ch, ny, scale,
-    t1_ref, tv_ref, fs, gs, pre, grad, part_second_ref, part_first_ref, above_ref, below_ref, before_ref, after_ref,
+    t1_ref, tv_ref, fs, gs, pre, grad, part_second_ref, part_first_ref, above_ref, below_ref, columns_ref,
     hid_ref, fe, keep_ref, give_ref,
     ge,
 ):
     rows = ch * ny
-    columns = end_columns(nx, ((0, nx - 1, 1, before_ref[...]), (1, 0, 1, after_ref[...]))).T
+    columns = columns_ref[...]
     for i, dst in enumerate((fe, ge)):
         for j, src in enumerate((above_ref, below_ref)):
             block = src[(i + 1) * rows : (i + 2) * rows]
@@ -386,7 +405,7 @@
         give_ref[:, at] = jnp.where(mine, part_first, part_second)
 
 
-def outer(t1, tv, fs, gs, pre, grad, second, first, above, below, before, after, ch, ny, scale):
+def outer(t1, tv, fs, gs, pre, grad, second, first, above, below, columns, ch, ny, scale):
     rows = ch * ny
     nx = fs.shape[1] // LANES
     sds = pltpu.VMEM
@@ -401,18 +420,19 @@
         scratch_shapes=[pltpu.VMEM((3 * rows, 2 * LANES), BF)],
         compiler_params=params(6),
         name="outer",
-    )(*in_vmem(t1, tv, fs, gs, pre, grad, second, first, above, below, before, after))
+    )(*in_vmem(t1, tv, fs, gs, pre, grad, second, first, above, below, columns))
 
 
 def rim_kernel(
     nx, ch, ny,
-    t1_ref, h_ref, h_end_ref, fs_ref, fe_ref, f_ref, above_ref, below_ref, near_ref, before_ref, after_ref, bias_ref,
+    t1_ref, h_ref, h_end_ref, fs_ref, fe_ref, f_ref, above_ref, below_ref, near_ref, corner_one_ref, corner_two_ref, bias_ref,
     hs,
     ends,
 ):
     rows = ch * ny
     above, below = above_ref[0:rows], below_ref[0:rows]
-    sources = ((2, nx + 2, 0, near_ref[...]), (0, 2, nx - 2, before_ref[...]), (nx + 2, nx + 4, 0, after_ref[...]))
+    before, after = sides(corner_one_ref[...], corner_two_ref[...])
+    sources = ((2, nx + 2, 0, near_ref[...]), (0, 2, nx - 2, before), (nx + 2, nx + 4, 0, after))
     edges_t = edge_columns(nx, sources)
     end = fe_ref[rows : 2 * rows]
     unshifted = [above, end[:, 0:LANES], *(f_ref[:, x * LANES : (x + 1) * LANES] for x in range(nx)), end[:, LANES:], below]
@@ -449,7 +469,7 @@
         shifted_rows(hs, x, block, jnp.where(lane == 0, lane_to(outer, x, 0), lane_to(outer, 64 + x, LANES - 1)), rows)
 
 
-def rim(t1, hidden, hidden_end, fs, fe, field, above, below, near, before, after, bias, ch, ny):
+def rim(t1, hidden, hidden_end, fs, fe, field, above, below, near, corner_one, corner_two, bias, ch, ny):
     rows = ch * ny
     nx = field.shape[1] // LANES
     return pl.pallas_call(
@@ -459,7 +479,7 @@
         compiler_params=params(6),
         cost_estimate=pl.CostEstimate(flops=1_000_000_000, bytes_accessed=3_000_000, transcendentals=0),
         name="rim",
-    )(*in_vmem(t1, hidden, hidden_end, fs, fe, field, above, below, near, before, after, bias))
+    )(*in_vmem(t1, hidden, hidden_end, fs, fe, field, above, below, near, corner_one, corner_two, bias))
 
 
 def residual_kernel(nx, ch, ny, t2_ref, hs, f_ref, bias_ref, o_ref):
@@ -496,6 +516,11 @@
                 t, u, v = step(s, x, z)
                 pairs.append(((s * nx + x) * nz + z, (t * nx + u) * nz + v))
     return lax.ppermute(array, AXES, pairs)
+
+
+def diagonal(array, sizes, turn):
+    ns, nx, nz = sizes
+    return moved(array, sizes, lambda s, x, z: (s, (x + (1 if x % 2 == turn else -1)) % nx, (z + 1) % nz))
 
 
 def along(array, sizes, dx, dz=0):
@@ -592,7 +617,7 @@
 def shards(sizes, features, first_weight, first_bias, second_weight, second_bias, cotangent):
     ns, ngx, ngz = sizes
     _, ch, nx, ny, nz = features.shape
-    assert features.shape[0] == 1 and nz == LANES and ngz == 2
+    assert features.shape[0] == 1 and nz == LANES and ngz == 2 and ngx % 2 == 0
     assert not any(n & (n - 1) for n in sizes) and ns > 1
     scale = float((ns * nx * ngx * ny * nz * ngz) ** -0.5)
     up, down, held, weight1, weight2 = faces(features, cotangent, first_weight, second_weight)
@@ -600,13 +625,14 @@
     field, cot, edge = pack(held)
     near = swapped(edge, sizes, (0, 0, 1))
     t1, tv, t2, edge = bands(weight1, weight2, edge, ny)
-    before, after = along(edge, sizes, 1, 1), along(edge, sizes, -1, 1)
+    corner_two, corner_one = diagonal(edge, sizes, 1), diagonal(edge, sizes, 0)
     bias1, bias2 = first_bias.reshape(1, ch), second_bias.reshape(1, ch)
     fs, gs, pre, grad, hidden, second, first = inner(t1, tv, field, cot, near, bias1, ch, ny)
+    columns = corners(corner_one, corner_two, nx)
     hidden_end, fe, keep, give = outer(
-        t1, tv, fs, gs, pre, grad, second, first, above, below, before, after, ch, ny, scale
+        t1, tv, fs, gs, pre, grad, second, first, above, below, columns, ch, ny, scale
     )
-    hs = rim(t1, hidden, hidden_end, fs, fe, field, above, below, near, before, after, bias1, ch, ny)
+    hs = rim(t1, hidden, hidden_end, fs, fe, field, above, below, near, corner_one, corner_two, bias1, ch, ny)
     mine, other, output = sum_all(keep, give, sizes, hs, lambda hs: residual(t2, hs, field, bias2, ch, ny))
     return output, *spread(mine, other, ch)
 

time: 39.3 us -> 38.6 us (0.982)
  starting transfers between devices: 17.8 us -> 17.1 us
    ppermute x13, starting transfers between devices: 17.8 us -> 17.1 us  [moved(): return lax.ppermute(array, AXES, pairs)]
  transfers between devices with their start and end apart: 13 -> 13, of which waited for: 8 -> 6; matrix products, arithmetic and copies ran while one was open for 0% -> 0% of each run, Pallas kernels for 22% -> 24%
where the time goes in v6:
time: 38.6 us; the launch traced here: 38.5 us
  starting transfers between devices  17.1 us (44%)
  Pallas kernels  13.8 us (36%)
  waiting for transfers between devices  6.85 us (18%)
  between operations  0.73 us (2%)
    ppermute x13, starting transfers between devices, moved(): return lax.ppermute(array, AXES, pairs)  17.1 us
    ppermute x13, waiting for transfers between devices, moved(): return lax.ppermute(array, AXES, pairs)  6.85 us
    pallas_call x1, Pallas kernels, inner(): pl.pallas_call(functools.partial(inner_kernel, nx, ch, ny), out_shape=(sd...  3.59 us
    pallas_call x1, Pallas kernels, residual(): pl.pallas_call(functools.partial(residual_kernel, nx, ch, ny), out_shape=...  2.06 us
    pallas_call x1, Pallas kernels, rim(): pl.pallas_call(functools.partial(rim_kernel, nx, ch, ny), out_shape=pltpu...  1.8 us
    pallas_call x1, Pallas kernels, outer(): pl.pallas_call(functools.partial(outer_kernel, nx, ch, ny, scale), out_sh...  1.64 us
    pallas_call x1, Pallas kernels, faces(): pl.pallas_call(functools.partial(faces_kernel, nx, ch, ny), out_shape=(sd...  1.44 us
    pallas_call x1, Pallas kernels, spread(): pl.pallas_call(functools.partial(spread_kernel, ch), out_shape=(taps, bia...  1.2 us
  transfers between devices with their start and end apart: 13, of which 6 were waited for; matrix products, arithmetic and copies ran while one was open for 0% of the time, Pallas kernels for 24%

profile of v6, /device:TPU:0, one launch (start us, length us, event | category | flops | bytes accessed | tf_op | source)
XLA Modules:
  0.0 38.5 jit_solution(14701809812060217486)
XLA Ops:
  0.6 1.4 %faces.1 = (bf16[768,128]{1,0:T(8,128)(2,1)S(1)}, bf16[768,128]{1,0:T(8,128)(2,1)S(1)}, bf16[2,5,32,8,128]{4,3,2,1,0:T(8,128)(2,1)S(1)}, bf16[3,3,3,32,32]{4,3,2...) custom-call(bf16[1,32,5,8,128]{4,3,2,1,0:T(8,128)(2,1)} %f_any.1, bf16[1,32,5,8,128]{4,3,2,1,0:T(8,128)(2,1)} %g_any.1, ...), custom_call_target="tpu_custom_call" | custom-call | tf_op jit(solution)/shard_map/faces/pallas_call | solution.py:84
  2.1 3.1 %collective-permute-start.1 = (bf16[768,128]{1,0:T(8,128)(2,1)S(1)}, bf16[768,128]{1,0:T(8,128)(2,1)S(1)}, u32[]{:S(2)}, u32[]{:S(2)}) collective-permute-start(bf16[768,128]{1,0:T(8,128)(2,1)S(1)} %get-tuple-element.56), channel_id=1, source_target_pairs={{0,2},{1,3},{2,4},{3,5},{4,6},{5,7},{6,0},{7,1},{8,10},{9,11},{10,... | collective-permute-start | bytes 589832 | tf_op jit(solution)/shard_map/ppermute | solution.py:518
  5.2 2.1 %collective-permute-start.2 = (bf16[768,128]{1,0:T(8,128)(2,1)S(1)}, bf16[768,128]{1,0:T(8,128)(2,1)S(1)}, u32[]{:S(2)}, u32[]{:S(2)}) collective-permute-start(bf16[768,128]{1,0:T(8,128)(2,1)S(1)} %get-tuple-element.57), channel_id=1, source_target_pairs={{0,6},{1,7},{2,0},{3,1},{4,2},{5,3},{6,4},{7,5},{8,14},{9,15},{10,... | collective-permute-start | bytes 589832 | tf_op jit(solution)/shard_map/ppermute | solution.py:518
  7.2 0.8 %pack.1 = (bf16[256,640]{1,0:T(8,128)(2,1)S(1)}, bf16[256,640]{1,0:T(8,128)(2,1)S(1)}, bf16[32,256]{1,0:T(8,128)(2,1)S(1)}) custom-call(bf16[2,5,32,8,128]{4,3,2,1,0:T(8,128)(2,1)S(1)} %get-tuple-element.44.held), custom_call_target="tpu_custom_call" | custom-call | flops 500000000 | bytes 1000000 | tf_op jit(solution)/shard_map/pack/pallas_call | solution.py:122
  8.1 1.7 %collective-permute-start = (bf16[32,256]{1,0:T(8,128)(2,1)S(1)}, bf16[32,256]{1,0:T(8,128)(2,1)S(1)}, u32[]{:S(2)}, u32[]{:S(2)}) collective-permute-start(bf16[32,256]{1,0:T(8,128)(2,1)S(1)} %get-tuple-element.45.edge_ref), channel_id=1, source_target_pairs={{0,1},{1,0},{2,3},{3,2},{4,5},{5,4},{6,7},{7,6},{8,9},{9,8},{10,11... | collective-permute-start | bytes 49160 | tf_op jit(solution)/shard_map/ppermute | solution.py:518
  9.7 0.6 %bands.1 = (bf16[3,256,768]{2,1,0:T(8,128)(2,1)S(1)}, bf16[3,256,768]{2,1,0:T(8,128)(2,1)S(1)}, bf16[3,256,768]{2,1,0:T(8,128)(2,1)S(1)}, bf16[32,256]{1,0:T(8,128)(2,1)S(1)}) custom-call(bf16[3,3,3,32,32]{4,3,2,1,0:T(8,128)(2,1)S(1)} %get-tuple-element.42.w1_ref, bf16[3,3,3,32,32]{4,3,2,1,0:T(8,128)(2,1)S(1)} %get-tuple-element.43.w2_ref, ...), custom_call_target="tpu_custom_call" | custom-call | flops 1000000000 | bytes 4000000 | tf_op jit(solution)/shard_map/bands/pallas_call | solution.py:170
  10.3 1.8 %collective-permute-start.4 = (bf16[32,256]{1,0:T(8,128)(2,1)S(1)}, bf16[32,256]{1,0:T(8,128)(2,1)S(1)}, u32[]{:S(2)}, u32[]{:S(2)}) collective-permute-start(bf16[32,256]{1,0:T(8,128)(2,1)S(1)} %get-tuple-element.58), channel_id=1, source_target_pairs={{0,7},{1,6},{2,5},{3,4},{4,3},{5,2},{6,1},{7,0},{8,15},{9,14},{10,... | collective-permute-start | bytes 49160 | tf_op jit(solution)/shard_map/ppermute | solution.py:518
  12.1 0.5 %collective-permute-start.3 = (bf16[32,256]{1,0:T(8,128)(2,1)S(1)}, bf16[32,256]{1,0:T(8,128)(2,1)S(1)}, u32[]{:S(2)}, u32[]{:S(2)}) collective-permute-start(bf16[32,256]{1,0:T(8,128)(2,1)S(1)} %get-tuple-element.58), channel_id=1, source_target_pairs={{0,3},{1,2},{2,1},{3,0},{4,7},{5,6},{6,5},{7,4},{8,11},{9,10},{10,... | collective-permute-start | bytes 49160 | tf_op jit(solution)/shard_map/ppermute | solution.py:518
  12.6 3.6 %inner.1 = (bf16[768,640]{1,0:T(8,128)(2,1)S(1)}, bf16[768,640]{1,0:T(8,128)(2,1)S(1)}, f32[256,640]{1,0:T(8,128)S(1)}, f32[256,640]{1,0:T(8,128)S(1)}, bf16[256...) custom-call(bf16[3,256,768]{2,1,0:T(8,128)(2,1)S(1)} %get-tuple-element.46.t1_ref, ...), custom_call_target="tpu_custom_call" | custom-call | flops 1000 | bytes 1000 | tf_op jit(solution)/shard_map/inner/pallas_call | solution.py:338
  16.2 1.7 %collective-permute-done.4.two_ref.corner_two_ref = bf16[32,256]{1,0:T(8,128)(2,1)S(1)} collective-permute-done((bf16[32,256]{1,0:T(8,128)(2,1)S(1)}, bf16[32,256]{1,0:T(8,128)(2,1)S(1)}, u32[]{:S(2)}, u32[]{:S(2)}) %collective-permute-start.4) | collective-permute-done | bytes 16416 | tf_op jit(solution)/shard_map/ppermute | solution.py:518
  17.9 0.0 collective-permute-done.3.one_ref.corner_one_ref
  17.9 0.2 corners.1.columns_ref
  18.2 1.6 %outer.1 = (bf16[256,256]{1,0:T(8,128)(2,1)S(1)}, bf16[768,256]{1,0:T(8,128)(2,1)S(1)}, f32[32,896]{1,0:T(8,128)S(1)}, f32[32,896]{1,0:T(8,128)S(1)}) custom-call(bf16[3,256,768]{2,1,0:T(8,128)(2,1)S(1)} %get-tuple-element.46.t1_ref, bf16[3,256,768]{2,1,0:T(8,128)(2,1)S(1)} %get-tuple-element.47.tv_ref, bf16[768,640]{1,0:T(8,128)(2,1)S(1)} %get-tuple-element.50.fs.fs_ref, ...), custom_call_target="tpu_custom_call" | custom-call | tf_op jit(solution)/shard_map/outer/pallas_call | solution.py:412
  19.8 0.1 collective-permute-start.5
  19.9 1.3 %collective-permute-done.5.refs_1_ = f32[32,896]{1,0:T(8,128)S(1)} collective-permute-done((f32[32,896]{1,0:T(8,128)S(1)}, f32[32,896]{1,0:T(8,128)S(1)}, u32[]{:S(2)}, u32[]{:S(2)}) %collective-permute-start.5) | collective-permute-done | bytes 114720 | tf_op jit(solution)/shard_map/ppermute | solution.py:518
  21.2 0.1 add.3.refs_0_
  21.3 1.5 %collective-permute-start.8 = (bf16[32,896]{1,0:T(8,128)(2,1)S(1)}, bf16[32,896]{1,0:T(8,128)(2,1)S(1)}, u32[]{:S(2)}, u32[]{:S(2)}) collective-permute-start(bf16[32,896]{1,0:T(8,128)(2,1)S(1)} %add.3.refs_0_), channel_id=1, source_target_pairs={{0,17},{1,16},{2,19},{3,18},{4,21},{5,20},{6,23},{7,22},{8,25},{9,... | collective-permute-start | bytes 172040 | tf_op jit(solution)/shard_map/ppermute | solution.py:518
  22.9 0.5 %collective-permute-start.7 = (bf16[32,896]{1,0:T(8,128)(2,1)S(1)}, bf16[32,896]{1,0:T(8,128)(2,1)S(1)}, u32[]{:S(2)}, u32[]{:S(2)}) collective-permute-start(bf16[32,896]{1,0:T(8,128)(2,1)S(1)} %add.3.refs_0_), channel_id=1, source_target_pairs={{0,16},{1,17},{2,18},{3,19},{4,20},{5,21},{6,22},{7,23},{8,24},{9,... | collective-permute-start | bytes 172040 | tf_op jit(solution)/shard_map/ppermute | solution.py:518
  23.4 1.5 %collective-permute-start.6 = (bf16[32,896]{1,0:T(8,128)(2,1)S(1)}, bf16[32,896]{1,0:T(8,128)(2,1)S(1)}, u32[]{:S(2)}, u32[]{:S(2)}) collective-permute-start(bf16[32,896]{1,0:T(8,128)(2,1)S(1)} %add.3.refs_0_), channel_id=1, source_target_pairs={{0,1},{1,0},{2,3},{3,2},{4,5},{5,4},{6,7},{7,6},{8,9},{9,8},{10,11... | collective-permute-start | bytes 172040 | tf_op jit(solution)/shard_map/ppermute | solution.py:518
  24.8 1.8 %rim.1.hs = bf16[768,896]{1,0:T(8,128)(2,1)S(1)} custom-call(bf16[3,256,768]{2,1,0:T(8,128)(2,1)S(1)} %get-tuple-element.46.t1_ref, bf16[256,384]{1,0:T(8,128)(2,1)S(1)} %get-tuple-element.61.h_ref, bf16[256,256]{1,0:T(8,128)(2,1)S(1)} %get-tuple-element.62.h_end_ref, bf16[768,640]{1,0:T(8,128)(2,1)S(1)} %get-tuple-element.50.fs.fs_ref, ...), custom_call_target="tpu_custom_call" | custom-call | flops 1000000000 | bytes 3000000 | tf_op jit(solution)/shard_map/rim/pallas_call | solution.py:475
  26.6 0.8 %collective-permute-done.7.refs_2_ = bf16[32,896]{1,0:T(8,128)(2,1)S(1)} collective-permute-done((bf16[32,896]{1,0:T(8,128)(2,1)S(1)}, bf16[32,896]{1,0:T(8,128)(2,1)S(1)}, u32[]{:S(2)}, u32[]{:S(2)}) %collective-permute-start.7) | collective-permute-done | bytes 57376 | tf_op jit(solution)/shard_map/ppermute | solution.py:518
  27.4 0.1 collective-permute-done.6.refs_1_
  27.5 0.2 add.4.refs_0_
  27.7 1.8 %collective-permute-start.11 = (bf16[32,896]{1,0:T(8,128)(2,1)S(1)}, bf16[32,896]{1,0:T(8,128)(2,1)S(1)}, u32[]{:S(2)}, u32[]{:S(2)}) collective-permute-start(bf16[32,896]{1,0:T(8,128)(2,1)S(1)} %add.4.refs_0_), channel_id=1, source_target_pairs={{0,6},{1,7},{2,4},{3,5},{4,2},{5,3},{6,0},{7,1},{8,14},{9,15},{10,... | collective-permute-start | bytes 172040 | tf_op jit(solution)/shard_map/ppermute | solution.py:518
  29.6 0.4 %collective-permute-start.10 = (bf16[32,896]{1,0:T(8,128)(2,1)S(1)}, bf16[32,896]{1,0:T(8,128)(2,1)S(1)}, u32[]{:S(2)}, u32[]{:S(2)}) collective-permute-start(bf16[32,896]{1,0:T(8,128)(2,1)S(1)} %add.4.refs_0_), channel_id=1, source_target_pairs={{0,4},{1,5},{2,6},{3,7},{4,0},{5,1},{6,2},{7,3},{8,12},{9,13},{10,... | collective-permute-start | bytes 172040 | tf_op jit(solution)/shard_map/ppermute | solution.py:518
  30.0 2.1 %collective-permute-start.9 = (bf16[32,896]{1,0:T(8,128)(2,1)S(1)}, bf16[32,896]{1,0:T(8,128)(2,1)S(1)}, u32[]{:S(2)}, u32[]{:S(2)}) collective-permute-start(bf16[32,896]{1,0:T(8,128)(2,1)S(1)} %add.4.refs_0_), channel_id=1, source_target_pairs={{0,2},{1,3},{2,0},{3,1},{4,6},{5,7},{6,4},{7,5},{8,10},{9,11},{10,... | collective-permute-start | bytes 172040 | tf_op jit(solution)/shard_map/ppermute | solution.py:518
  32.1 2.1 %residual.1 = bf16[1,32,5,8,128]{4,3,2,1,0:T(8,128)(2,1)} custom-call(bf16[3,256,768]{2,1,0:T(8,128)(2,1)S(1)} %get-tuple-element.68.t2_ref, bf16[768,896]{1,0:T(8,128)(2,1)S(1)} %rim.1.hs, bf16[256,640]{1,0:T(8,128)(2,1)S(1)} %get-tuple-element.48.f_ref, f32[1,32]{1,0:T(1,128)S(1)} %bitcast.10), custom_call_target="tpu_custom_call" | custom-call | flops 3000000000 | bytes 3000000 | tf_op jit(solution)/shard_map/residual/pallas_call | solution.py:501
  34.2 1.7 %collective-permute-done.10.refs_2_ = bf16[32,896]{1,0:T(8,128)(2,1)S(1)} collective-permute-done((bf16[32,896]{1,0:T(8,128)(2,1)S(1)}, bf16[32,896]{1,0:T(8,128)(2,1)S(1)}, u32[]{:S(2)}, u32[]{:S(2)}) %collective-permute-start.10) | collective-permute-done | bytes 57376 | tf_op jit(solution)/shard_map/ppermute | solution.py:518
  35.8 0.1 add.5.mine_ref
  35.9 0.0 collective-permute-start.12
  35.9 1.3 %collective-permute-done.12.other_ref = f32[32,896]{1,0:T(8,128)S(1)} collective-permute-done((f32[32,896]{1,0:T(8,128)S(1)}, f32[32,896]{1,0:T(8,128)S(1)}, u32[]{:S(2)}, u32[]{:S(2)}) %collective-permute-start.12) | collective-permute-done | bytes 114720 | tf_op jit(solution)/shard_map/ppermute | solution.py:518
  37.3 1.2 %spread.1 = (f32[3,3,3,32,32]{4,3,2,1,0:T(8,128)}, f32[1,32]{1,0:T(1,128)}, f32[3,3,3,32,32]{4,3,2,1,0:T(8,128)}, f32[1,32]{1,0:T(1,128)}) custom-call(f32[32,896]{1,0:T(8,128)S(1)} %add.5.mine_ref, f32[32,896]{1,0:T(8,128)S(1)} %collective-permute-done.12.other_ref), custom_call_target="tpu_custom_call" | custom-call | tf_op jit(solution)/shard_map/spread/pallas_call | solution.py:607
  (10 shorter events, 0.0 us)
Async XLA Ops:
  2.1 16.1 %collective-permute-start.1 = (bf16[768,128]{1,0:T(8,128)(2,1)S(1)}, bf16[768,128]{1,0:T(8,128)(2,1)S(1)}, u32[]{:S(2)}, u32[]{:S(2)}) collective-permute-start(bf16[768,128]{1,0:T(8,128)(2,1)S(1)} %get-tuple-element.56), channel_id=1, source_target_pairs={{0,2},{1,3},{2,4},{3,5},{4,6},{5,7},{6,0},{7,1},{8,10},{9,11},{10,... | collective-permute-start | bytes 589832 | tf_op jit(solution)/shard_map/ppermute | solution.py:518
  5.2 13.0 %collective-permute-start.2 = (bf16[768,128]{1,0:T(8,128)(2,1)S(1)}, bf16[768,128]{1,0:T(8,128)(2,1)S(1)}, u32[]{:S(2)}, u32[]{:S(2)}) collective-permute-start(bf16[768,128]{1,0:T(8,128)(2,1)S(1)} %get-tuple-element.57), channel_id=1, source_target_pairs={{0,6},{1,7},{2,0},{3,1},{4,2},{5,3},{6,4},{7,5},{8,14},{9,15},{10,... | collective-permute-start | bytes 589832 | tf_op jit(solution)/shard_map/ppermute | solution.py:518
  8.1 4.6 %collective-permute-start = (bf16[32,256]{1,0:T(8,128)(2,1)S(1)}, bf16[32,256]{1,0:T(8,128)(2,1)S(1)}, u32[]{:S(2)}, u32[]{:S(2)}) collective-permute-start(bf16[32,256]{1,0:T(8,128)(2,1)S(1)} %get-tuple-element.45.edge_ref), channel_id=1, source_target_pairs={{0,1},{1,0},{2,3},{3,2},{4,5},{5,4},{6,7},{7,6},{8,9},{9,8},{10,11... | collective-permute-start | bytes 49160 | tf_op jit(solution)/shard_map/ppermute | solution.py:518
  9.7 2.9 %copy-start = (f32[32]{0:T(128)S(1)}, f32[32]{0:T(128)}, u32[]{:S(2)}) copy-start(f32[32]{0:T(128)} %param.8) | copy-start | bytes 388
  10.3 7.6 %collective-permute-start.4 = (bf16[32,256]{1,0:T(8,128)(2,1)S(1)}, bf16[32,256]{1,0:T(8,128)(2,1)S(1)}, u32[]{:S(2)}, u32[]{:S(2)}) collective-permute-start(bf16[32,256]{1,0:T(8,128)(2,1)S(1)} %get-tuple-element.58), channel_id=1, source_target_pairs={{0,7},{1,6},{2,5},{3,4},{4,3},{5,2},{6,1},{7,0},{8,15},{9,14},{10,... | collective-permute-start | bytes 49160 | tf_op jit(solution)/shard_map/ppermute | solution.py:518
  12.1 5.8 %collective-permute-start.3 = (bf16[32,256]{1,0:T(8,128)(2,1)S(1)}, bf16[32,256]{1,0:T(8,128)(2,1)S(1)}, u32[]{:S(2)}, u32[]{:S(2)}) collective-permute-start(bf16[32,256]{1,0:T(8,128)(2,1)S(1)} %get-tuple-element.58), channel_id=1, source_target_pairs={{0,3},{1,2},{2,1},{3,0},{4,7},{5,6},{6,5},{7,4},{8,11},{9,10},{10,... | collective-permute-start | bytes 49160 | tf_op jit(solution)/shard_map/ppermute | solution.py:518
  19.8 1.4 %collective-permute-start.5 = (f32[32,896]{1,0:T(8,128)S(1)}, f32[32,896]{1,0:T(8,128)S(1)}, u32[]{:S(2)}, u32[]{:S(2)}) collective-permute-start(f32[32,896]{1,0:T(8,128)S(1)} %get-tuple-element.60), channel_id=1, source_target_pairs={{0,8},{1,9},{2,10},{3,11},{4,12},{5,13},{6,14},{7,15},{8,0},{9,1},... | collective-permute-start | bytes 344072 | tf_op jit(solution)/shard_map/ppermute | solution.py:518
  21.3 5.3 %collective-permute-start.8 = (bf16[32,896]{1,0:T(8,128)(2,1)S(1)}, bf16[32,896]{1,0:T(8,128)(2,1)S(1)}, u32[]{:S(2)}, u32[]{:S(2)}) collective-permute-start(bf16[32,896]{1,0:T(8,128)(2,1)S(1)} %add.3.refs_0_), channel_id=1, source_target_pairs={{0,17},{1,16},{2,19},{3,18},{4,21},{5,20},{6,23},{7,22},{8,25},{9,... | collective-permute-start | bytes 172040 | tf_op jit(solution)/shard_map/ppermute | solution.py:518
  22.9 4.6 %collective-permute-start.7 = (bf16[32,896]{1,0:T(8,128)(2,1)S(1)}, bf16[32,896]{1,0:T(8,128)(2,1)S(1)}, u32[]{:S(2)}, u32[]{:S(2)}) collective-permute-start(bf16[32,896]{1,0:T(8,128)(2,1)S(1)} %add.3.refs_0_), channel_id=1, source_target_pairs={{0,16},{1,17},{2,18},{3,19},{4,20},{5,21},{6,22},{7,23},{8,24},{9,... | collective-permute-start | bytes 172040 | tf_op jit(solution)/shard_map/ppermute | solution.py:518
  23.4 4.2 %collective-permute-start.6 = (bf16[32,896]{1,0:T(8,128)(2,1)S(1)}, bf16[32,896]{1,0:T(8,128)(2,1)S(1)}, u32[]{:S(2)}, u32[]{:S(2)}) collective-permute-start(bf16[32,896]{1,0:T(8,128)(2,1)S(1)} %add.3.refs_0_), channel_id=1, source_target_pairs={{0,1},{1,0},{2,3},{3,2},{4,5},{5,4},{6,7},{7,6},{8,9},{9,8},{10,11... | collective-permute-start | bytes 172040 | tf_op jit(solution)/shard_map/ppermute | solution.py:518
  24.8 7.3 %copy-start.1 = (f32[32]{0:T(128)S(1)}, f32[32]{0:T(128)}, u32[]{:S(2)}) copy-start(f32[32]{0:T(128)} %param.10) | copy-start | bytes 388
  27.7 6.5 %collective-permute-start.11 = (bf16[32,896]{1,0:T(8,128)(2,1)S(1)}, bf16[32,896]{1,0:T(8,128)(2,1)S(1)}, u32[]{:S(2)}, u32[]{:S(2)}) collective-permute-start(bf16[32,896]{1,0:T(8,128)(2,1)S(1)} %add.4.refs_0_), channel_id=1, source_target_pairs={{0,6},{1,7},{2,4},{3,5},{4,2},{5,3},{6,0},{7,1},{8,14},{9,15},{10,... | collective-permute-start | bytes 172040 | tf_op jit(solution)/shard_map/ppermute | solution.py:518
  29.6 6.3 %collective-permute-start.10 = (bf16[32,896]{1,0:T(8,128)(2,1)S(1)}, bf16[32,896]{1,0:T(8,128)(2,1)S(1)}, u32[]{:S(2)}, u32[]{:S(2)}) collective-permute-start(bf16[32,896]{1,0:T(8,128)(2,1)S(1)} %add.4.refs_0_), channel_id=1, source_target_pairs={{0,4},{1,5},{2,6},{3,7},{4,0},{5,1},{6,2},{7,3},{8,12},{9,13},{10,... | collective-permute-start | bytes 172040 | tf_op jit(solution)/shard_map/ppermute | solution.py:518
  30.0 5.8 %collective-permute-start.9 = (bf16[32,896]{1,0:T(8,128)(2,1)S(1)}, bf16[32,896]{1,0:T(8,128)(2,1)S(1)}, u32[]{:S(2)}, u32[]{:S(2)}) collective-permute-start(bf16[32,896]{1,0:T(8,128)(2,1)S(1)} %add.4.refs_0_), channel_id=1, source_target_pairs={{0,2},{1,3},{2,0},{3,1},{4,6},{5,7},{6,4},{7,5},{8,10},{9,11},{10,... | collective-permute-start | bytes 172040 | tf_op jit(solution)/shard_map/ppermute | solution.py:518
  35.9 1.3 %collective-permute-start.12 = (f32[32,896]{1,0:T(8,128)S(1)}, f32[32,896]{1,0:T(8,128)S(1)}, u32[]{:S(2)}, u32[]{:S(2)}) collective-permute-start(f32[32,896]{1,0:T(8,128)S(1)} %add.5.mine_ref), channel_id=1, source_target_pairs={{0,8},{1,9},{2,10},{3,11},{4,12},{5,13},{6,14},{7,15},{8,0},{9,1},... | collective-permute-start | bytes 344072 | tf_op jit(solution)/shard_map/ppermute | solution.py:518

commit v7 on v6

--- a/solution.py
+++ b/solution.py
@@ -585,33 +585,46 @@
     return mine, swapped(mine, sizes, near), output
 
 
-def spread_kernel(ch, mine_ref, other_ref, first_ref, first_bias_ref, second_ref, second_bias_ref):
-    even = is_even("smp")
-    mine, other = mine_ref[...], other_ref[...]
+def spread_kernel(ch, own, terms_ref, *refs):
+    first, first_bias, second, second_bias, taps, bias, sems = refs[-7:]
+    for tap in range(27):
+        at = tap * ch
+        block = terms_ref[:, at // LANES * LANES : (at // LANES + 1) * LANES]
+        taps[tap // 9, tap // 3 % 3, tap % 3] = lane_to(block, at % LANES, 0)[:, :ch]
+    tail = lane_to(terms_ref[:, TERMS - LANES :], 27 * ch % LANES, 0)[:, 0:1]
     r, k = iota((ch, LANES), 0), iota((ch, LANES), 1)
-    for terms, out, bias in (
-        (jnp.where(even, other, mine), first_ref, first_bias_ref),
-        (jnp.where(even, mine, other), second_ref, second_bias_ref),
-    ):
-        for tap in range(27):
-            at = tap * ch
-            block = terms[:, at // LANES * LANES : (at // LANES + 1) * LANES]
-            out[tap // 9, tap // 3 % 3, tap % 3] = lane_to(block, at % LANES, 0)[:, :ch]
-        tail = lane_to(terms[:, TERMS - LANES :], 27 * ch % LANES, 0)[:, 0:1]
-        bias[...] = jnp.sum(jnp.where(r == k, tail, 0.0), axis=0, keepdims=True)[:, :ch]
-
-
-def spread(mine, other, ch):
-    sds = jax.ShapeDtypeStruct
-    taps, bias = sds((3, 3, 3, ch, ch), F32), sds((1, ch), F32)
-    first, first_bias, second, second_bias = pl.pallas_call(
-        functools.partial(spread_kernel, ch),
+    bias[...] = jnp.sum(jnp.where(r == k, tail, 0.0), axis=0, keepdims=True)[:, :ch]
+
+    def write(out, bias_out):
+        copies = [pltpu.make_async_copy(taps, out, sems.at[0]), pltpu.make_async_copy(bias, bias_out, sems.at[1])]
+        for copy in copies:
+            copy.start()
+        for copy in copies:
+            copy.wait()
+
+    to_second = is_even("smp") if own else ~is_even("smp")
+    pl.when(to_second)(lambda: write(second, second_bias))
+    pl.when(~to_second)(lambda: write(first, first_bias))
+
+
+def spread(terms, ch, written=()):
+    taps, bias = pltpu.HBM((3, 3, 3, ch, ch), F32), pltpu.HBM((1, ch), F32)
+    anywhere = pl.BlockSpec(memory_space=pl.ANY)
+    return pl.pallas_call(
+        functools.partial(spread_kernel, ch, not written),
         out_shape=(taps, bias, taps, bias),
-        compiler_params=params(4),
+        in_specs=[pl.BlockSpec(memory_space=pltpu.VMEM)] + [anywhere] * len(written),
+        out_specs=(anywhere,) * 4,
+        input_output_aliases={1 + i: i for i in range(len(written))},
+        scratch_shapes=[
+            pltpu.VMEM((3, 3, 3, ch, ch), F32),
+            pltpu.VMEM((1, ch), F32),
+            pltpu.SemaphoreType.DMA((2,)),
+        ],
+        compiler_params=params(3),
+        cost_estimate=pl.CostEstimate(flops=1_000_000_000, bytes_accessed=2_000_000, transcendentals=0),
         name="spread",
-    )(*in_vmem(mine, other))
-    laid = lambda grad: jnp.transpose(grad, (3, 0, 1, 2, 4))
-    return laid(first), first_bias.reshape(ch), laid(second), second_bias.reshape(ch)
+    )(*in_vmem(terms), *written)
 
 
 def shards(sizes, features, first_weight, first_bias, second_weight, second_bias, cotangent):
@@ -634,7 +647,9 @@
     )
     hs = rim(t1, hidden, hidden_end, fs, fe, field, above, below, near, corner_one, corner_two, bias1, ch, ny)
     mine, other, output = sum_all(keep, give, sizes, hs, lambda hs: residual(t2, hs, field, bias2, ch, ny))
-    return output, *spread(mine, other, ch)
+    first, first_bias, second, second_bias = spread(other, ch, spread(mine, ch))
+    laid = lambda grad: jnp.transpose(grad, (3, 0, 1, 2, 4))
+    return output, laid(first), first_bias.reshape(ch), laid(second), second_bias.reshape(ch)
 
 
 def solution(mesh):

time: 38.6 us -> 38.4 us (level)
  waiting for transfers between devices: 6.85 us -> 5.88 us
  Pallas kernels: 13.8 us -> 14.5 us
    ppermute x13, waiting for transfers between devices: 6.85 us -> 5.88 us  [moved(): return lax.ppermute(array, AXES, pairs)]
    pallas_call x1 -> x2, Pallas kernels: 1.2 us -> 1.93 us  [spread(): pl.pallas_call(functools.partial(spread_kernel, ch, not written), out_sha...]
  transfers between devices with their start and end apart: 13 -> 13, of which waited for: 6 -> 6; matrix products, arithmetic and copies ran while one was open for 0% -> 0% of each run, Pallas kernels for 24% -> 26%
where the time goes in v7:
time: 38.4 us; the launch traced here: 38.2 us
  starting transfers between devices  17.1 us (45%)
  Pallas kernels  14.5 us (38%)
  waiting for transfers between devices  5.88 us (15%)
  between operations  0.74 us (2%)
    ppermute x13, starting transfers between devices, moved(): return lax.ppermute(array, AXES, pairs)  17.1 us
    ppermute x13, waiting for transfers between devices, moved(): return lax.ppermute(array, AXES, pairs)  5.88 us
    pallas_call x1, Pallas kernels, inner(): pl.pallas_call(functools.partial(inner_kernel, nx, ch, ny), out_shape=(sd...  3.59 us
    pallas_call x1, Pallas kernels, residual(): pl.pallas_call(functools.partial(residual_kernel, nx, ch, ny), out_shape=...  2.06 us
    pallas_call x2, Pallas kernels, spread(): pl.pallas_call(functools.partial(spread_kernel, ch, not written), out_sha...  1.93 us
    pallas_call x1, Pallas kernels, rim(): pl.pallas_call(functools.partial(rim_kernel, nx, ch, ny), out_shape=pltpu...  1.8 us
    pallas_call x1, Pallas kernels, outer(): pl.pallas_call(functools.partial(outer_kernel, nx, ch, ny, scale), out_sh...  1.64 us
    pallas_call x1, Pallas kernels, faces(): pl.pallas_call(functools.partial(faces_kernel, nx, ch, ny), out_shape=(sd...  1.44 us
  transfers between devices with their start and end apart: 13, of which 6 were waited for; matrix products, arithmetic and copies ran while one was open for 0% of the time, Pallas kernels for 26%

profile of v7, /device:TPU:0, one launch (start us, length us, event | category | flops | bytes accessed | tf_op | source)
XLA Modules:
  0.0 38.2 jit_solution(3389813366770643444)
XLA Ops:
  0.6 1.4 %faces.1 = (bf16[768,128]{1,0:T(8,128)(2,1)S(1)}, bf16[768,128]{1,0:T(8,128)(2,1)S(1)}, bf16[2,5,32,8,128]{4,3,2,1,0:T(8,128)(2,1)S(1)}, bf16[3,3,3,32,32]{4,3,2...) custom-call(bf16[1,32,5,8,128]{4,3,2,1,0:T(8,128)(2,1)} %f_any.1, bf16[1,32,5,8,128]{4,3,2,1,0:T(8,128)(2,1)} %g_any.1, ...), custom_call_target="tpu_custom_call" | custom-call | tf_op jit(solution)/shard_map/faces/pallas_call | solution.py:84
  2.1 3.1 %collective-permute-start.1 = (bf16[768,128]{1,0:T(8,128)(2,1)S(1)}, bf16[768,128]{1,0:T(8,128)(2,1)S(1)}, u32[]{:S(2)}, u32[]{:S(2)}) collective-permute-start(bf16[768,128]{1,0:T(8,128)(2,1)S(1)} %get-tuple-element.60), channel_id=1, source_target_pairs={{0,2},{1,3},{2,4},{3,5},{4,6},{5,7},{6,0},{7,1},{8,10},{9,11},{10,... | collective-permute-start | bytes 589832 | tf_op jit(solution)/shard_map/ppermute | solution.py:518
  5.2 2.1 %collective-permute-start.2 = (bf16[768,128]{1,0:T(8,128)(2,1)S(1)}, bf16[768,128]{1,0:T(8,128)(2,1)S(1)}, u32[]{:S(2)}, u32[]{:S(2)}) collective-permute-start(bf16[768,128]{1,0:T(8,128)(2,1)S(1)} %get-tuple-element.61), channel_id=1, source_target_pairs={{0,6},{1,7},{2,0},{3,1},{4,2},{5,3},{6,4},{7,5},{8,14},{9,15},{10,... | collective-permute-start | bytes 589832 | tf_op jit(solution)/shard_map/ppermute | solution.py:518
  7.2 0.8 %pack.1 = (bf16[256,640]{1,0:T(8,128)(2,1)S(1)}, bf16[256,640]{1,0:T(8,128)(2,1)S(1)}, bf16[32,256]{1,0:T(8,128)(2,1)S(1)}) custom-call(bf16[2,5,32,8,128]{4,3,2,1,0:T(8,128)(2,1)S(1)} %get-tuple-element.48.held), custom_call_target="tpu_custom_call" | custom-call | flops 500000000 | bytes 1000000 | tf_op jit(solution)/shard_map/pack/pallas_call | solution.py:122
  8.1 1.7 %collective-permute-start = (bf16[32,256]{1,0:T(8,128)(2,1)S(1)}, bf16[32,256]{1,0:T(8,128)(2,1)S(1)}, u32[]{:S(2)}, u32[]{:S(2)}) collective-permute-start(bf16[32,256]{1,0:T(8,128)(2,1)S(1)} %get-tuple-element.49.edge_ref), channel_id=1, source_target_pairs={{0,1},{1,0},{2,3},{3,2},{4,5},{5,4},{6,7},{7,6},{8,9},{9,8},{10,11... | collective-permute-start | bytes 49160 | tf_op jit(solution)/shard_map/ppermute | solution.py:518
  9.7 0.6 %bands.1 = (bf16[3,256,768]{2,1,0:T(8,128)(2,1)S(1)}, bf16[3,256,768]{2,1,0:T(8,128)(2,1)S(1)}, bf16[3,256,768]{2,1,0:T(8,128)(2,1)S(1)}, bf16[32,256]{1,0:T(8,128)(2,1)S(1)}) custom-call(bf16[3,3,3,32,32]{4,3,2,1,0:T(8,128)(2,1)S(1)} %get-tuple-element.46.w1_ref, bf16[3,3,3,32,32]{4,3,2,1,0:T(8,128)(2,1)S(1)} %get-tuple-element.47.w2_ref, ...), custom_call_target="tpu_custom_call" | custom-call | flops 1000000000 | bytes 4000000 | tf_op jit(solution)/shard_map/bands/pallas_call | solution.py:170
  10.3 1.8 %collective-permute-start.4 = (bf16[32,256]{1,0:T(8,128)(2,1)S(1)}, bf16[32,256]{1,0:T(8,128)(2,1)S(1)}, u32[]{:S(2)}, u32[]{:S(2)}) collective-permute-start(bf16[32,256]{1,0:T(8,128)(2,1)S(1)} %get-tuple-element.62), channel_id=1, source_target_pairs={{0,7},{1,6},{2,5},{3,4},{4,3},{5,2},{6,1},{7,0},{8,15},{9,14},{10,... | collective-permute-start | bytes 49160 | tf_op jit(solution)/shard_map/ppermute | solution.py:518
  12.1 0.5 %collective-permute-start.3 = (bf16[32,256]{1,0:T(8,128)(2,1)S(1)}, bf16[32,256]{1,0:T(8,128)(2,1)S(1)}, u32[]{:S(2)}, u32[]{:S(2)}) collective-permute-start(bf16[32,256]{1,0:T(8,128)(2,1)S(1)} %get-tuple-element.62), channel_id=1, source_target_pairs={{0,3},{1,2},{2,1},{3,0},{4,7},{5,6},{6,5},{7,4},{8,11},{9,10},{10,... | collective-permute-start | bytes 49160 | tf_op jit(solution)/shard_map/ppermute | solution.py:518
  12.6 3.6 %inner.1 = (bf16[768,640]{1,0:T(8,128)(2,1)S(1)}, bf16[768,640]{1,0:T(8,128)(2,1)S(1)}, f32[256,640]{1,0:T(8,128)S(1)}, f32[256,640]{1,0:T(8,128)S(1)}, bf16[256...) custom-call(bf16[3,256,768]{2,1,0:T(8,128)(2,1)S(1)} %get-tuple-element.50.t1_ref, ...), custom_call_target="tpu_custom_call" | custom-call | flops 1000 | bytes 1000 | tf_op jit(solution)/shard_map/inner/pallas_call | solution.py:338
  16.2 1.7 %collective-permute-done.4.two_ref.corner_two_ref = bf16[32,256]{1,0:T(8,128)(2,1)S(1)} collective-permute-done((bf16[32,256]{1,0:T(8,128)(2,1)S(1)}, bf16[32,256]{1,0:T(8,128)(2,1)S(1)}, u32[]{:S(2)}, u32[]{:S(2)}) %collective-permute-start.4) | collective-permute-done | bytes 16416 | tf_op jit(solution)/shard_map/ppermute | solution.py:518
  17.9 0.2 corners.1.columns_ref
  18.2 1.6 %outer.1 = (bf16[256,256]{1,0:T(8,128)(2,1)S(1)}, bf16[768,256]{1,0:T(8,128)(2,1)S(1)}, f32[32,896]{1,0:T(8,128)S(1)}, f32[32,896]{1,0:T(8,128)S(1)}) custom-call(bf16[3,256,768]{2,1,0:T(8,128)(2,1)S(1)} %get-tuple-element.50.t1_ref, bf16[3,256,768]{2,1,0:T(8,128)(2,1)S(1)} %get-tuple-element.51.tv_ref, bf16[768,640]{1,0:T(8,128)(2,1)S(1)} %get-tuple-element.54.fs.fs_ref, ...), custom_call_target="tpu_custom_call" | custom-call | tf_op jit(solution)/shard_map/outer/pallas_call | solution.py:412
  19.8 0.1 collective-permute-start.5
  19.9 1.3 %collective-permute-done.5.refs_1_ = f32[32,896]{1,0:T(8,128)S(1)} collective-permute-done((f32[32,896]{1,0:T(8,128)S(1)}, f32[32,896]{1,0:T(8,128)S(1)}, u32[]{:S(2)}, u32[]{:S(2)}) %collective-permute-start.5) | collective-permute-done | bytes 114720 | tf_op jit(solution)/shard_map/ppermute | solution.py:518
  21.2 0.1 add.3.refs_0_
  21.3 1.5 %collective-permute-start.8 = (bf16[32,896]{1,0:T(8,128)(2,1)S(1)}, bf16[32,896]{1,0:T(8,128)(2,1)S(1)}, u32[]{:S(2)}, u32[]{:S(2)}) collective-permute-start(bf16[32,896]{1,0:T(8,128)(2,1)S(1)} %add.3.refs_0_), channel_id=1, source_target_pairs={{0,17},{1,16},{2,19},{3,18},{4,21},{5,20},{6,23},{7,22},{8,25},{9,... | collective-permute-start | bytes 172040 | tf_op jit(solution)/shard_map/ppermute | solution.py:518
  22.9 0.5 %collective-permute-start.7 = (bf16[32,896]{1,0:T(8,128)(2,1)S(1)}, bf16[32,896]{1,0:T(8,128)(2,1)S(1)}, u32[]{:S(2)}, u32[]{:S(2)}) collective-permute-start(bf16[32,896]{1,0:T(8,128)(2,1)S(1)} %add.3.refs_0_), channel_id=1, source_target_pairs={{0,16},{1,17},{2,18},{3,19},{4,20},{5,21},{6,22},{7,23},{8,24},{9,... | collective-permute-start | bytes 172040 | tf_op jit(solution)/shard_map/ppermute | solution.py:518
  23.4 1.5 %collective-permute-start.6 = (bf16[32,896]{1,0:T(8,128)(2,1)S(1)}, bf16[32,896]{1,0:T(8,128)(2,1)S(1)}, u32[]{:S(2)}, u32[]{:S(2)}) collective-permute-start(bf16[32,896]{1,0:T(8,128)(2,1)S(1)} %add.3.refs_0_), channel_id=1, source_target_pairs={{0,1},{1,0},{2,3},{3,2},{4,5},{5,4},{6,7},{7,6},{8,9},{9,8},{10,11... | collective-permute-start | bytes 172040 | tf_op jit(solution)/shard_map/ppermute | solution.py:518
  24.8 1.8 %rim.1.hs = bf16[768,896]{1,0:T(8,128)(2,1)S(1)} custom-call(bf16[3,256,768]{2,1,0:T(8,128)(2,1)S(1)} %get-tuple-element.50.t1_ref, bf16[256,384]{1,0:T(8,128)(2,1)S(1)} %get-tuple-element.65.h_ref, bf16[256,256]{1,0:T(8,128)(2,1)S(1)} %get-tuple-element.66.h_end_ref, bf16[768,640]{1,0:T(8,128)(2,1)S(1)} %get-tuple-element.54.fs.fs_ref, ...), custom_call_target="tpu_custom_call" | custom-call | flops 1000000000 | bytes 3000000 | tf_op jit(solution)/shard_map/rim/pallas_call | solution.py:475
  26.6 0.8 %collective-permute-done.7.refs_2_ = bf16[32,896]{1,0:T(8,128)(2,1)S(1)} collective-permute-done((bf16[32,896]{1,0:T(8,128)(2,1)S(1)}, bf16[32,896]{1,0:T(8,128)(2,1)S(1)}, u32[]{:S(2)}, u32[]{:S(2)}) %collective-permute-start.7) | collective-permute-done | bytes 57376 | tf_op jit(solution)/shard_map/ppermute | solution.py:518
  27.4 0.1 collective-permute-done.6.refs_1_
  27.5 0.2 add.4.refs_0_
  27.7 1.8 %collective-permute-start.11 = (bf16[32,896]{1,0:T(8,128)(2,1)S(1)}, bf16[32,896]{1,0:T(8,128)(2,1)S(1)}, u32[]{:S(2)}, u32[]{:S(2)}) collective-permute-start(bf16[32,896]{1,0:T(8,128)(2,1)S(1)} %add.4.refs_0_), channel_id=1, source_target_pairs={{0,6},{1,7},{2,4},{3,5},{4,2},{5,3},{6,0},{7,1},{8,14},{9,15},{10,... | collective-permute-start | bytes 172040 | tf_op jit(solution)/shard_map/ppermute | solution.py:518
  29.6 0.4 %collective-permute-start.10 = (bf16[32,896]{1,0:T(8,128)(2,1)S(1)}, bf16[32,896]{1,0:T(8,128)(2,1)S(1)}, u32[]{:S(2)}, u32[]{:S(2)}) collective-permute-start(bf16[32,896]{1,0:T(8,128)(2,1)S(1)} %add.4.refs_0_), channel_id=1, source_target_pairs={{0,4},{1,5},{2,6},{3,7},{4,0},{5,1},{6,2},{7,3},{8,12},{9,13},{10,... | collective-permute-start | bytes 172040 | tf_op jit(solution)/shard_map/ppermute | solution.py:518
  30.0 2.1 %collective-permute-start.9 = (bf16[32,896]{1,0:T(8,128)(2,1)S(1)}, bf16[32,896]{1,0:T(8,128)(2,1)S(1)}, u32[]{:S(2)}, u32[]{:S(2)}) collective-permute-start(bf16[32,896]{1,0:T(8,128)(2,1)S(1)} %add.4.refs_0_), channel_id=1, source_target_pairs={{0,2},{1,3},{2,0},{3,1},{4,6},{5,7},{6,4},{7,5},{8,10},{9,11},{10,... | collective-permute-start | bytes 172040 | tf_op jit(solution)/shard_map/ppermute | solution.py:518
  32.1 2.1 %residual.1 = bf16[1,32,5,8,128]{4,3,2,1,0:T(8,128)(2,1)} custom-call(bf16[3,256,768]{2,1,0:T(8,128)(2,1)S(1)} %get-tuple-element.72.t2_ref, bf16[768,896]{1,0:T(8,128)(2,1)S(1)} %rim.1.hs, bf16[256,640]{1,0:T(8,128)(2,1)S(1)} %get-tuple-element.52.f_ref, f32[1,32]{1,0:T(1,128)S(1)} %bitcast.10), custom_call_target="tpu_custom_call" | custom-call | flops 3000000000 | bytes 3000000 | tf_op jit(solution)/shard_map/residual/pallas_call | solution.py:501
  34.2 1.7 %collective-permute-done.10.refs_2_ = bf16[32,896]{1,0:T(8,128)(2,1)S(1)} collective-permute-done((bf16[32,896]{1,0:T(8,128)(2,1)S(1)}, bf16[32,896]{1,0:T(8,128)(2,1)S(1)}, u32[]{:S(2)}, u32[]{:S(2)}) %collective-permute-start.10) | collective-permute-done | bytes 57376 | tf_op jit(solution)/shard_map/ppermute | solution.py:518
  35.8 0.1 add.5.terms_ref
  35.9 0.0 collective-permute-start.12
  35.9 1.0 %spread.2 = (f32[3,3,3,32,32]{4,3,2,1,0:T(8,128)}, f32[1,32]{1,0:T(1,128)}, f32[3,3,3,32,32]{4,3,2,1,0:T(8,128)}, f32[1,32]{1,0:T(1,128)}) custom-call(f32[32,896]{1,0:T(8,128)S(1)} %add.5.terms_ref), custom_call_target="tpu_custom_call" | custom-call | flops 1000000000 | bytes 2000000 | tf_op jit(solution)/shard_map/spread/pallas_call | solution.py:613
  36.9 0.3 collective-permute-done.12.terms_ref
  37.3 1.0 %spread.3 = (f32[3,3,3,32,32]{4,3,2,1,0:T(8,128)}, f32[1,32]{1,0:T(1,128)}, f32[3,3,3,32,32]{4,3,2,1,0:T(8,128)}, f32[1,32]{1,0:T(1,128)}) custom-call(f32[32,896]{1,0:T(8,128)S(1)} %collective-permute-done.12.terms_ref, f32[3,3,3,32,32]{4,3,2,1,0:T(8,128)} %get-tuple-element.79.refs_0_, ...), custom_call_target="tpu_custom_call", output_to_operand_aliasing={{0}: (1, {}), {1}: (2, {}), {2}: (3, {}), {3}: (4, {})} | custom-call | flops 1000000000 | bytes 2000000 | tf_op jit(solution)/shard_map/spread/pallas_call | solution.py:613
  (11 shorter events, 0.0 us)
Async XLA Ops:
  2.1 16.1 %collective-permute-start.1 = (bf16[768,128]{1,0:T(8,128)(2,1)S(1)}, bf16[768,128]{1,0:T(8,128)(2,1)S(1)}, u32[]{:S(2)}, u32[]{:S(2)}) collective-permute-start(bf16[768,128]{1,0:T(8,128)(2,1)S(1)} %get-tuple-element.60), channel_id=1, source_target_pairs={{0,2},{1,3},{2,4},{3,5},{4,6},{5,7},{6,0},{7,1},{8,10},{9,11},{10,... | collective-permute-start | bytes 589832 | tf_op jit(solution)/shard_map/ppermute | solution.py:518
  5.2 13.0 %collective-permute-start.2 = (bf16[768,128]{1,0:T(8,128)(2,1)S(1)}, bf16[768,128]{1,0:T(8,128)(2,1)S(1)}, u32[]{:S(2)}, u32[]{:S(2)}) collective-permute-start(bf16[768,128]{1,0:T(8,128)(2,1)S(1)} %get-tuple-element.61), channel_id=1, source_target_pairs={{0,6},{1,7},{2,0},{3,1},{4,2},{5,3},{6,4},{7,5},{8,14},{9,15},{10,... | collective-permute-start | bytes 589832 | tf_op jit(solution)/shard_map/ppermute | solution.py:518
  8.1 4.6 %collective-permute-start = (bf16[32,256]{1,0:T(8,128)(2,1)S(1)}, bf16[32,256]{1,0:T(8,128)(2,1)S(1)}, u32[]{:S(2)}, u32[]{:S(2)}) collective-permute-start(bf16[32,256]{1,0:T(8,128)(2,1)S(1)} %get-tuple-element.49.edge_ref), channel_id=1, source_target_pairs={{0,1},{1,0},{2,3},{3,2},{4,5},{5,4},{6,7},{7,6},{8,9},{9,8},{10,11... | collective-permute-start | bytes 49160 | tf_op jit(solution)/shard_map/ppermute | solution.py:518
  9.7 2.9 %copy-start = (f32[32]{0:T(128)S(1)}, f32[32]{0:T(128)}, u32[]{:S(2)}) copy-start(f32[32]{0:T(128)} %param.8) | copy-start | bytes 388
  10.3 7.6 %collective-permute-start.4 = (bf16[32,256]{1,0:T(8,128)(2,1)S(1)}, bf16[32,256]{1,0:T(8,128)(2,1)S(1)}, u32[]{:S(2)}, u32[]{:S(2)}) collective-permute-start(bf16[32,256]{1,0:T(8,128)(2,1)S(1)} %get-tuple-element.62), channel_id=1, source_target_pairs={{0,7},{1,6},{2,5},{3,4},{4,3},{5,2},{6,1},{7,0},{8,15},{9,14},{10,... | collective-permute-start | bytes 49160 | tf_op jit(solution)/shard_map/ppermute | solution.py:518
  12.1 5.8 %collective-permute-start.3 = (bf16[32,256]{1,0:T(8,128)(2,1)S(1)}, bf16[32,256]{1,0:T(8,128)(2,1)S(1)}, u32[]{:S(2)}, u32[]{:S(2)}) collective-permute-start(bf16[32,256]{1,0:T(8,128)(2,1)S(1)} %get-tuple-element.62), channel_id=1, source_target_pairs={{0,3},{1,2},{2,1},{3,0},{4,7},{5,6},{6,5},{7,4},{8,11},{9,10},{10,... | collective-permute-start | bytes 49160 | tf_op jit(solution)/shard_map/ppermute | solution.py:518
  19.8 1.4 %collective-permute-start.5 = (f32[32,896]{1,0:T(8,128)S(1)}, f32[32,896]{1,0:T(8,128)S(1)}, u32[]{:S(2)}, u32[]{:S(2)}) collective-permute-start(f32[32,896]{1,0:T(8,128)S(1)} %get-tuple-element.64), channel_id=1, source_target_pairs={{0,8},{1,9},{2,10},{3,11},{4,12},{5,13},{6,14},{7,15},{8,0},{9,1},... | collective-permute-start | bytes 344072 | tf_op jit(solution)/shard_map/ppermute | solution.py:518
  21.3 5.3 %collective-permute-start.8 = (bf16[32,896]{1,0:T(8,128)(2,1)S(1)}, bf16[32,896]{1,0:T(8,128)(2,1)S(1)}, u32[]{:S(2)}, u32[]{:S(2)}) collective-permute-start(bf16[32,896]{1,0:T(8,128)(2,1)S(1)} %add.3.refs_0_), channel_id=1, source_target_pairs={{0,17},{1,16},{2,19},{3,18},{4,21},{5,20},{6,23},{7,22},{8,25},{9,... | collective-permute-start | bytes 172040 | tf_op jit(solution)/shard_map/ppermute | solution.py:518
  22.9 4.6 %collective-permute-start.7 = (bf16[32,896]{1,0:T(8,128)(2,1)S(1)}, bf16[32,896]{1,0:T(8,128)(2,1)S(1)}, u32[]{:S(2)}, u32[]{:S(2)}) collective-permute-start(bf16[32,896]{1,0:T(8,128)(2,1)S(1)} %add.3.refs_0_), channel_id=1, source_target_pairs={{0,16},{1,17},{2,18},{3,19},{4,20},{5,21},{6,22},{7,23},{8,24},{9,... | collective-permute-start | bytes 172040 | tf_op jit(solution)/shard_map/ppermute | solution.py:518
  23.4 4.2 %collective-permute-start.6 = (bf16[32,896]{1,0:T(8,128)(2,1)S(1)}, bf16[32,896]{1,0:T(8,128)(2,1)S(1)}, u32[]{:S(2)}, u32[]{:S(2)}) collective-permute-start(bf16[32,896]{1,0:T(8,128)(2,1)S(1)} %add.3.refs_0_), channel_id=1, source_target_pairs={{0,1},{1,0},{2,3},{3,2},{4,5},{5,4},{6,7},{7,6},{8,9},{9,8},{10,11... | collective-permute-start | bytes 172040 | tf_op jit(solution)/shard_map/ppermute | solution.py:518
  24.8 7.3 %copy-start.1 = (f32[32]{0:T(128)S(1)}, f32[32]{0:T(128)}, u32[]{:S(2)}) copy-start(f32[32]{0:T(128)} %param.10) | copy-start | bytes 388
  27.7 6.5 %collective-permute-start.11 = (bf16[32,896]{1,0:T(8,128)(2,1)S(1)}, bf16[32,896]{1,0:T(8,128)(2,1)S(1)}, u32[]{:S(2)}, u32[]{:S(2)}) collective-permute-start(bf16[32,896]{1,0:T(8,128)(2,1)S(1)} %add.4.refs_0_), channel_id=1, source_target_pairs={{0,6},{1,7},{2,4},{3,5},{4,2},{5,3},{6,0},{7,1},{8,14},{9,15},{10,... | collective-permute-start | bytes 172040 | tf_op jit(solution)/shard_map/ppermute | solution.py:518
  29.6 6.3 %collective-permute-start.10 = (bf16[32,896]{1,0:T(8,128)(2,1)S(1)}, bf16[32,896]{1,0:T(8,128)(2,1)S(1)}, u32[]{:S(2)}, u32[]{:S(2)}) collective-permute-start(bf16[32,896]{1,0:T(8,128)(2,1)S(1)} %add.4.refs_0_), channel_id=1, source_target_pairs={{0,4},{1,5},{2,6},{3,7},{4,0},{5,1},{6,2},{7,3},{8,12},{9,13},{10,... | collective-permute-start | bytes 172040 | tf_op jit(solution)/shard_map/ppermute | solution.py:518
  30.0 5.8 %collective-permute-start.9 = (bf16[32,896]{1,0:T(8,128)(2,1)S(1)}, bf16[32,896]{1,0:T(8,128)(2,1)S(1)}, u32[]{:S(2)}, u32[]{:S(2)}) collective-permute-start(bf16[32,896]{1,0:T(8,128)(2,1)S(1)} %add.4.refs_0_), channel_id=1, source_target_pairs={{0,2},{1,3},{2,0},{3,1},{4,6},{5,7},{6,4},{7,5},{8,10},{9,11},{10,... | collective-permute-start | bytes 172040 | tf_op jit(solution)/shard_map/ppermute | solution.py:518
  35.9 1.3 %collective-permute-start.12 = (f32[32,896]{1,0:T(8,128)S(1)}, f32[32,896]{1,0:T(8,128)S(1)}, u32[]{:S(2)}, u32[]{:S(2)}) collective-permute-start(f32[32,896]{1,0:T(8,128)S(1)} %add.5.terms_ref), channel_id=1, source_target_pairs={{0,8},{1,9},{2,10},{3,11},{4,12},{5,13},{6,14},{7,15},{8,0},{9,1},... | collective-permute-start | bytes 344072 | tf_op jit(solution)/shard_map/ppermute | solution.py:518

commit v8 on v7

--- a/solution.py
+++ b/solution.py
@@ -352,40 +352,74 @@
     )(*in_vmem(t1, tv, field, cot, near, bias))
 
 
-def corners_kernel(nx, one_ref, two_ref, columns_ref):
+def corners_kernel(nx, one_ref, two_ref, after_ref, columns_ref):
     before, after = sides(one_ref[...], two_ref[...])
     columns_ref[...] = end_columns(nx, ((0, nx - 1, 1, before), (1, 0, 1, after))).T
 
 
-def corners(one, two, nx):
+def corners(one, two, after, nx):
     return pl.pallas_call(
         functools.partial(corners_kernel, nx),
         out_shape=pltpu.VMEM((one.shape[1], LANES), F32),
         compiler_params=params(1),
         name="corners",
-    )(*in_vmem(one, two))
+    )(*in_vmem(one, two, after))
+
+
+def ahead_kernel(nx, t1_ref, tv_ref, pre, grad, above_ref, below_ref, pre_end, grad_end, fe, ge):
+    rows = above_ref.shape[0] // 3
+    last = (nx - 1) * LANES
+    none = jnp.zeros((rows, LANES), F32)
+    for i, (t, own, out, end) in enumerate(((t1_ref, pre, pre_end, fe), (tv_ref, grad, grad_end, ge))):
+        for j, (src, at) in enumerate(((above_ref, 0), (below_ref, last))):
+            shifted_rows(end, j, src[(i + 1) * rows : (i + 2) * rows], none, rows)
+            block = slice(j * LANES, (j + 1) * LANES)
+            out[:, block] = own[:, at : at + LANES] + mm(t[2 * j], end[:, block])
+
+
+def ahead(t1, tv, pre, grad, above, below):
+    rows = above.shape[0] // 3
+    nx = pre.shape[1] // LANES
+    sds = pltpu.VMEM
+    sums, windows = sds((rows, 2 * LANES), F32), sds((3 * rows, 2 * LANES), BF)
+    return pl.pallas_call(
+        functools.partial(ahead_kernel, nx),
+        out_shape=(sums, sums, windows, windows),
+        compiler_params=params(2),
+        cost_estimate=pl.CostEstimate(flops=1000, bytes_accessed=1000, transcendentals=0),
+        name="ahead",
+    )(*in_vmem(t1, tv, pre, grad, above, below))
 
 
 def outer_kernel(
     nx, ch, ny, scale,
-    t1_ref, tv_ref, fs, gs, pre, grad, part_second_ref, part_first_ref, above_ref, below_ref, columns_ref,
+    t1_ref, tv_ref, fs, gs, pre_end, grad_end, fe_in, ge_in, part_second_ref, part_first_ref, columns_ref,
     hid_ref, fe, keep_ref, give_ref,
     ge,
 ):
     rows = ch * ny
+    last = (nx - 1) * LANES
     columns = columns_ref[...]
-    for i, dst in enumerate((fe, ge)):
-        for j, src in enumerate((above_ref, below_ref)):
-            block = src[(i + 1) * rows : (i + 2) * rows]
-            shifted_rows(dst, j, block, lane_to(columns, 64 * i + 2 * j + 1, 0), rows)
-
-    last = (nx - 1) * LANES
-    ends = lambda ref: jnp.concatenate([ref[:, 0:LANES], ref[:, last:]], axis=1)
-    both = lambda t, e: jnp.concatenate([mm(t[0], e[:, 0:LANES]), mm(t[2], e[:, LANES:])], axis=1)
-    preact = ends(pre) + both(t1_ref, fe)
+    lane = iota((rows, LANES), 1)
+    sums = []
+    for i, (t, own, old, new) in enumerate(((t1_ref, pre_end, fe_in, fe), (tv_ref, grad_end, ge_in, ge))):
+        parts = []
+        for j in range(2):
+            block = slice(j * LANES, (j + 1) * LANES)
+            corner = lane_to(columns, 64 * i + 2 * j + 1, 0)
+            part = own[:, block]
+            for c, hit in ((0, lane == 0), (2, lane == LANES - 1)):
+                at = slice(c * rows, (c + 1) * rows)
+                window = old[at, block].astype(F32)
+                new[at, block] = jnp.where(hit, corner, window).astype(BF)
+                part = part + mm(t[2 * j, :, at], jnp.where(hit, corner, 0.0).astype(BF))
+            new[rows : 2 * rows, block] = old[rows : 2 * rows, block]
+            parts.append(part)
+        sums.append(jnp.concatenate(parts, axis=1))
+    preact, hidden_grad = sums
     q = logistic(preact)
     hid_ref[...] = (preact * q).astype(BF)
-    preact_grad = gate(ends(grad) + both(tv_ref, ge), preact, q)
+    preact_grad = gate(hidden_grad, preact, q)
 
     def window(own, end, a, c):
         at = slice(c * rows, (c + 1) * rows)
@@ -405,7 +439,7 @@
         give_ref[:, at] = jnp.where(mine, part_first, part_second)
 
 
-def outer(t1, tv, fs, gs, pre, grad, second, first, above, below, columns, ch, ny, scale):
+def outer(t1, tv, fs, gs, pre_end, grad_end, fe, ge, second, first, columns, ch, ny, scale):
     rows = ch * ny
     nx = fs.shape[1] // LANES
     sds = pltpu.VMEM
@@ -420,7 +454,7 @@
         scratch_shapes=[pltpu.VMEM((3 * rows, 2 * LANES), BF)],
         compiler_params=params(6),
         name="outer",
-    )(*in_vmem(t1, tv, fs, gs, pre, grad, second, first, above, below, columns))
+    )(*in_vmem(t1, tv, fs, gs, pre_end, grad_end, fe, ge, second, first, columns))
 
 
 def rim_kernel(
@@ -559,11 +593,12 @@
     )(*in_vmem(*terms))
 
 
-def exchange(sent, sizes, pair):
+def exchange(sent, sizes, pair, far_first):
     steps = [(0, 0, 0)]
     for bits in pair:
         steps = steps + [tuple(p ^ q for p, q in zip(bits, step)) for step in steps]
-    return [sent] + [swapped(sent, sizes, step) for step in steps[1:]]
+    order = steps[:0:-1] if far_first else steps[2:] + steps[1:2]
+    return [sent] + [swapped(sent, sizes, step) for step in order]
 
 
 def sum_all(keep, give, sizes, hs, finish):
@@ -575,7 +610,7 @@
     terms = [keep, swapped(give, sizes, near)]
     output = None
     for i, group in enumerate(groups):
-        terms = exchange(add(terms, BF), sizes, group)
+        terms = exchange(add(terms, BF), sizes, group, i == 0)
         if i == 0:
             *terms, hs = lax.optimization_barrier((*terms, hs))
             output = finish(hs)
@@ -641,9 +676,10 @@
     corner_two, corner_one = diagonal(edge, sizes, 1), diagonal(edge, sizes, 0)
     bias1, bias2 = first_bias.reshape(1, ch), second_bias.reshape(1, ch)
     fs, gs, pre, grad, hidden, second, first = inner(t1, tv, field, cot, near, bias1, ch, ny)
-    columns = corners(corner_one, corner_two, nx)
+    pre_end, grad_end, fe, ge = ahead(t1, tv, pre, grad, above, below)
+    columns = corners(corner_one, corner_two, pre_end, nx)
     hidden_end, fe, keep, give = outer(
-        t1, tv, fs, gs, pre, grad, second, first, above, below, columns, ch, ny, scale
+        t1, tv, fs, gs, pre_end, grad_end, fe, ge, second, first, columns, ch, ny, scale
     )
     hs = rim(t1, hidden, hidden_end, fs, fe, field, above, below, near, corner_one, corner_two, bias1, ch, ny)
     mine, other, output = sum_all(keep, give, sizes, hs, lambda hs: residual(t2, hs, field, bias2, ch, ny))

time: 38.4 us -> 37.6 us (0.979)
  waiting for transfers between devices: 5.88 us -> 3.72 us
  starting transfers between devices: 17.1 us -> 18 us
  Pallas kernels: 14.5 us -> 14.9 us
    ppermute x13, waiting for transfers between devices: 5.88 us -> 3.72 us  [moved(): return lax.ppermute(array, AXES, pairs)]
    ppermute x13, starting transfers between devices: 17.1 us -> 18 us  [moved(): return lax.ppermute(array, AXES, pairs)]
    pallas_call x0 -> x1, Pallas kernels: none -> 0.67 us  [ahead(): pl.pallas_call(functools.partial(ahead_kernel, nx), out_shape=(sums, sums...]
  transfers between devices with their start and end apart: 13 -> 13, of which waited for: 6 -> 7; matrix products, arithmetic and copies ran while one was open for 0% -> 0% of each run, Pallas kernels for 26% -> 28%
where the time goes in v8:
time: 37.6 us; the launch traced here: 37.4 us
  starting transfers between devices  18 us (48%)
  Pallas kernels  14.9 us (40%)
  waiting for transfers between devices  3.72 us (10%)
  between operations  0.76 us (2%)
    ppermute x13, starting transfers between devices, moved(): return lax.ppermute(array, AXES, pairs)  18 us
    ppermute x13, waiting for transfers between devices, moved(): return lax.ppermute(array, AXES, pairs)  3.72 us
    pallas_call x1, Pallas kernels, inner(): pl.pallas_call(functools.partial(inner_kernel, nx, ch, ny), out_shape=(sd...  3.58 us
    pallas_call x1, Pallas kernels, residual(): pl.pallas_call(functools.partial(residual_kernel, nx, ch, ny), out_shape=...  2.06 us
    pallas_call x2, Pallas kernels, spread(): pl.pallas_call(functools.partial(spread_kernel, ch, not written), out_sha...  1.93 us
    pallas_call x1, Pallas kernels, rim(): pl.pallas_call(functools.partial(rim_kernel, nx, ch, ny), out_shape=pltpu...  1.8 us
    pallas_call x1, Pallas kernels, faces(): pl.pallas_call(functools.partial(faces_kernel, nx, ch, ny), out_shape=(sd...  1.44 us
    pallas_call x1, Pallas kernels, outer(): pl.pallas_call(functools.partial(outer_kernel, nx, ch, ny, scale), out_sh...  1.42 us
  transfers between devices with their start and end apart: 13, of which 7 were waited for; matrix products, arithmetic and copies ran while one was open for 0% of the time, Pallas kernels for 28%

profile of v8, /device:TPU:0, one launch (start us, length us, event | category | flops | bytes accessed | tf_op | source)
XLA Modules:
  0.0 37.4 jit_solution(1971286957743669447)
XLA Ops:
  0.6 1.4 %faces.1 = (bf16[768,128]{1,0:T(8,128)(2,1)S(1)}, bf16[768,128]{1,0:T(8,128)(2,1)S(1)}, bf16[2,5,32,8,128]{4,3,2,1,0:T(8,128)(2,1)S(1)}, bf16[3,3,3,32,32]{4,3,2...) custom-call(bf16[1,32,5,8,128]{4,3,2,1,0:T(8,128)(2,1)} %f_any.1, bf16[1,32,5,8,128]{4,3,2,1,0:T(8,128)(2,1)} %g_any.1, ...), custom_call_target="tpu_custom_call" | custom-call | tf_op jit(solution)/shard_map/faces/pallas_call | solution.py:84
  2.1 3.1 %collective-permute-start.1 = (bf16[768,128]{1,0:T(8,128)(2,1)S(1)}, bf16[768,128]{1,0:T(8,128)(2,1)S(1)}, u32[]{:S(2)}, u32[]{:S(2)}) collective-permute-start(bf16[768,128]{1,0:T(8,128)(2,1)S(1)} %get-tuple-element.62), channel_id=1, source_target_pairs={{0,2},{1,3},{2,4},{3,5},{4,6},{5,7},{6,0},{7,1},{8,10},{9,11},{10,... | collective-permute-start | bytes 589832 | tf_op jit(solution)/shard_map/ppermute | solution.py:552
  5.2 2.1 %collective-permute-start.2 = (bf16[768,128]{1,0:T(8,128)(2,1)S(1)}, bf16[768,128]{1,0:T(8,128)(2,1)S(1)}, u32[]{:S(2)}, u32[]{:S(2)}) collective-permute-start(bf16[768,128]{1,0:T(8,128)(2,1)S(1)} %get-tuple-element.63), channel_id=1, source_target_pairs={{0,6},{1,7},{2,0},{3,1},{4,2},{5,3},{6,4},{7,5},{8,14},{9,15},{10,... | collective-permute-start | bytes 589832 | tf_op jit(solution)/shard_map/ppermute | solution.py:552
  7.2 0.8 %pack.1 = (bf16[256,640]{1,0:T(8,128)(2,1)S(1)}, bf16[256,640]{1,0:T(8,128)(2,1)S(1)}, bf16[32,256]{1,0:T(8,128)(2,1)S(1)}) custom-call(bf16[2,5,32,8,128]{4,3,2,1,0:T(8,128)(2,1)S(1)} %get-tuple-element.52.held), custom_call_target="tpu_custom_call" | custom-call | flops 500000000 | bytes 1000000 | tf_op jit(solution)/shard_map/pack/pallas_call | solution.py:122
  8.1 1.7 %collective-permute-start = (bf16[32,256]{1,0:T(8,128)(2,1)S(1)}, bf16[32,256]{1,0:T(8,128)(2,1)S(1)}, u32[]{:S(2)}, u32[]{:S(2)}) collective-permute-start(bf16[32,256]{1,0:T(8,128)(2,1)S(1)} %get-tuple-element.53.edge_ref), channel_id=1, source_target_pairs={{0,1},{1,0},{2,3},{3,2},{4,5},{5,4},{6,7},{7,6},{8,9},{9,8},{10,11... | collective-permute-start | bytes 49160 | tf_op jit(solution)/shard_map/ppermute | solution.py:552
  9.7 0.6 %bands.1 = (bf16[3,256,768]{2,1,0:T(8,128)(2,1)S(1)}, bf16[3,256,768]{2,1,0:T(8,128)(2,1)S(1)}, bf16[3,256,768]{2,1,0:T(8,128)(2,1)S(1)}, bf16[32,256]{1,0:T(8,128)(2,1)S(1)}) custom-call(bf16[3,3,3,32,32]{4,3,2,1,0:T(8,128)(2,1)S(1)} %get-tuple-element.50.w1_ref, bf16[3,3,3,32,32]{4,3,2,1,0:T(8,128)(2,1)S(1)} %get-tuple-element.51.w2_ref, ...), custom_call_target="tpu_custom_call" | custom-call | flops 1000000000 | bytes 4000000 | tf_op jit(solution)/shard_map/bands/pallas_call | solution.py:170
  10.3 0.1 collective-permute-start.3
  10.4 3.1 %collective-permute-start.4 = (bf16[32,256]{1,0:T(8,128)(2,1)S(1)}, bf16[32,256]{1,0:T(8,128)(2,1)S(1)}, u32[]{:S(2)}, u32[]{:S(2)}) collective-permute-start(bf16[32,256]{1,0:T(8,128)(2,1)S(1)} %get-tuple-element.70), channel_id=1, source_target_pairs={{0,7},{1,6},{2,5},{3,4},{4,3},{5,2},{6,1},{7,0},{8,15},{9,14},{10,... | collective-permute-start | bytes 49160 | tf_op jit(solution)/shard_map/ppermute | solution.py:552
  13.5 3.6 %inner.1 = (bf16[768,640]{1,0:T(8,128)(2,1)S(1)}, bf16[768,640]{1,0:T(8,128)(2,1)S(1)}, f32[256,640]{1,0:T(8,128)S(1)}, f32[256,640]{1,0:T(8,128)S(1)}, bf16[256...) custom-call(bf16[3,256,768]{2,1,0:T(8,128)(2,1)S(1)} %get-tuple-element.54.t1_ref, ...), custom_call_target="tpu_custom_call" | custom-call | flops 1000 | bytes 1000 | tf_op jit(solution)/shard_map/inner/pallas_call | solution.py:338
  17.1 0.7 %ahead.1 = (f32[256,256]{1,0:T(8,128)S(1)}, f32[256,256]{1,0:T(8,128)S(1)}, bf16[768,256]{1,0:T(8,128)(2,1)S(1)}, bf16[768,256]{1,0:T(8,128)(2,1)S(1)}) custom-call(bf16[3,256,768]{2,1,0:T(8,128)(2,1)S(1)} %get-tuple-element.54.t1_ref, bf16[3,256,768]{2,1,0:T(8,128)(2,1)S(1)} %get-tuple-element.55.tv_ref, f32[256,640]{1,0:T(8,128)S(1)} %get-tuple-element.60.pre, ...), custom_call_target="tpu_custom_call" | custom-call | flops 1000 | bytes 1000 | tf_op jit(solution)/shard_map/ahead/pallas_call | solution.py:385
  17.8 0.1 collective-permute-done.4.two_ref.corner_two_ref
  18.0 0.2 corners.1.columns_ref
  18.2 1.4 %outer.1 = (bf16[256,256]{1,0:T(8,128)(2,1)S(1)}, bf16[768,256]{1,0:T(8,128)(2,1)S(1)}, f32[32,896]{1,0:T(8,128)S(1)}, f32[32,896]{1,0:T(8,128)S(1)}) custom-call(bf16[3,256,768]{2,1,0:T(8,128)(2,1)S(1)} %get-tuple-element.54.t1_ref, bf16[3,256,768]{2,1,0:T(8,128)(2,1)S(1)} %get-tuple-element.55.tv_ref, bf16[768,640]{1,0:T(8,128)(2,1)S(1)} %get-tuple-element.58.fs.fs_ref, ...), custom_call_target="tpu_custom_call" | custom-call | tf_op jit(solution)/shard_map/outer/pallas_call | solution.py:446
  19.6 0.1 collective-permute-start.5
  19.7 1.3 %collective-permute-done.5.refs_1_ = f32[32,896]{1,0:T(8,128)S(1)} collective-permute-done((f32[32,896]{1,0:T(8,128)S(1)}, f32[32,896]{1,0:T(8,128)S(1)}, u32[]{:S(2)}, u32[]{:S(2)}) %collective-permute-start.5) | collective-permute-done | bytes 114720 | tf_op jit(solution)/shard_map/ppermute | solution.py:552
  21.0 0.1 add.3.refs_0_
  21.2 1.5 %collective-permute-start.6 = (bf16[32,896]{1,0:T(8,128)(2,1)S(1)}, bf16[32,896]{1,0:T(8,128)(2,1)S(1)}, u32[]{:S(2)}, u32[]{:S(2)}) collective-permute-start(bf16[32,896]{1,0:T(8,128)(2,1)S(1)} %add.3.refs_0_), channel_id=1, source_target_pairs={{0,17},{1,16},{2,19},{3,18},{4,21},{5,20},{6,23},{7,22},{8,25},{9,... | collective-permute-start | bytes 172040 | tf_op jit(solution)/shard_map/ppermute | solution.py:552
  22.7 0.5 %collective-permute-start.7 = (bf16[32,896]{1,0:T(8,128)(2,1)S(1)}, bf16[32,896]{1,0:T(8,128)(2,1)S(1)}, u32[]{:S(2)}, u32[]{:S(2)}) collective-permute-start(bf16[32,896]{1,0:T(8,128)(2,1)S(1)} %add.3.refs_0_), channel_id=1, source_target_pairs={{0,16},{1,17},{2,18},{3,19},{4,20},{5,21},{6,22},{7,23},{8,24},{9,... | collective-permute-start | bytes 172040 | tf_op jit(solution)/shard_map/ppermute | solution.py:552
  23.2 1.5 %collective-permute-start.8 = (bf16[32,896]{1,0:T(8,128)(2,1)S(1)}, bf16[32,896]{1,0:T(8,128)(2,1)S(1)}, u32[]{:S(2)}, u32[]{:S(2)}) collective-permute-start(bf16[32,896]{1,0:T(8,128)(2,1)S(1)} %add.3.refs_0_), channel_id=1, source_target_pairs={{0,1},{1,0},{2,3},{3,2},{4,5},{5,4},{6,7},{7,6},{8,9},{9,8},{10,11... | collective-permute-start | bytes 172040 | tf_op jit(solution)/shard_map/ppermute | solution.py:552
  24.7 1.8 %rim.1.hs = bf16[768,896]{1,0:T(8,128)(2,1)S(1)} custom-call(bf16[3,256,768]{2,1,0:T(8,128)(2,1)S(1)} %get-tuple-element.54.t1_ref, bf16[256,384]{1,0:T(8,128)(2,1)S(1)} %get-tuple-element.73.h_ref, bf16[256,256]{1,0:T(8,128)(2,1)S(1)} %get-tuple-element.74.h_end_ref, bf16[768,640]{1,0:T(8,128)(2,1)S(1)} %get-tuple-element.58.fs.fs_ref, ...), custom_call_target="tpu_custom_call" | custom-call | flops 1000000000 | bytes 3000000 | tf_op jit(solution)/shard_map/rim/pallas_call | solution.py:509
  26.5 0.8 %collective-permute-done.7.refs_2_ = bf16[32,896]{1,0:T(8,128)(2,1)S(1)} collective-permute-done((bf16[32,896]{1,0:T(8,128)(2,1)S(1)}, bf16[32,896]{1,0:T(8,128)(2,1)S(1)}, u32[]{:S(2)}, u32[]{:S(2)}) %collective-permute-start.7) | collective-permute-done | bytes 57376 | tf_op jit(solution)/shard_map/ppermute | solution.py:552
  27.3 0.1 collective-permute-done.8.refs_3_
  27.4 0.2 add.4.refs_0_
  27.5 2.1 %collective-permute-start.10 = (bf16[32,896]{1,0:T(8,128)(2,1)S(1)}, bf16[32,896]{1,0:T(8,128)(2,1)S(1)}, u32[]{:S(2)}, u32[]{:S(2)}) collective-permute-start(bf16[32,896]{1,0:T(8,128)(2,1)S(1)} %add.4.refs_0_), channel_id=1, source_target_pairs={{0,6},{1,7},{2,4},{3,5},{4,2},{5,3},{6,0},{7,1},{8,14},{9,15},{10,... | collective-permute-start | bytes 172040 | tf_op jit(solution)/shard_map/ppermute | solution.py:552
  29.6 2.3 %collective-permute-start.9 = (bf16[32,896]{1,0:T(8,128)(2,1)S(1)}, bf16[32,896]{1,0:T(8,128)(2,1)S(1)}, u32[]{:S(2)}, u32[]{:S(2)}) collective-permute-start(bf16[32,896]{1,0:T(8,128)(2,1)S(1)} %add.4.refs_0_), channel_id=1, source_target_pairs={{0,4},{1,5},{2,6},{3,7},{4,0},{5,1},{6,2},{7,3},{8,12},{9,13},{10,... | collective-permute-start | bytes 172040 | tf_op jit(solution)/shard_map/ppermute | solution.py:552
  31.9 2.1 %residual.1 = bf16[1,32,5,8,128]{4,3,2,1,0:T(8,128)(2,1)} custom-call(bf16[3,256,768]{2,1,0:T(8,128)(2,1)S(1)} %get-tuple-element.80.t2_ref, bf16[768,896]{1,0:T(8,128)(2,1)S(1)} %rim.1.hs, bf16[256,640]{1,0:T(8,128)(2,1)S(1)} %get-tuple-element.56.f_ref, f32[1,32]{1,0:T(1,128)S(1)} %bitcast.10), custom_call_target="tpu_custom_call" | custom-call | flops 3000000000 | bytes 3000000 | tf_op jit(solution)/shard_map/residual/pallas_call | solution.py:535
  34.0 0.5 %collective-permute-done.11.refs_3_ = bf16[32,896]{1,0:T(8,128)(2,1)S(1)} collective-permute-done((bf16[32,896]{1,0:T(8,128)(2,1)S(1)}, bf16[32,896]{1,0:T(8,128)(2,1)S(1)}, u32[]{:S(2)}, u32[]{:S(2)}) %collective-permute-start.11) | collective-permute-done | bytes 57376 | tf_op jit(solution)/shard_map/ppermute | solution.py:552
  34.5 0.6 %collective-permute-done.9.refs_1_ = bf16[32,896]{1,0:T(8,128)(2,1)S(1)} collective-permute-done((bf16[32,896]{1,0:T(8,128)(2,1)S(1)}, bf16[32,896]{1,0:T(8,128)(2,1)S(1)}, u32[]{:S(2)}, u32[]{:S(2)}) %collective-permute-start.9) | collective-permute-done | bytes 57376 | tf_op jit(solution)/shard_map/ppermute | solution.py:552
  35.0 0.1 add.5.terms_ref
  35.2 1.0 %spread.2 = (f32[3,3,3,32,32]{4,3,2,1,0:T(8,128)}, f32[1,32]{1,0:T(1,128)}, f32[3,3,3,32,32]{4,3,2,1,0:T(8,128)}, f32[1,32]{1,0:T(1,128)}) custom-call(f32[32,896]{1,0:T(8,128)S(1)} %add.5.terms_ref), custom_call_target="tpu_custom_call" | custom-call | flops 1000000000 | bytes 2000000 | tf_op jit(solution)/shard_map/spread/pallas_call | solution.py:648
  36.1 0.3 collective-permute-done.12.terms_ref
  36.5 1.0 %spread.3 = (f32[3,3,3,32,32]{4,3,2,1,0:T(8,128)}, f32[1,32]{1,0:T(1,128)}, f32[3,3,3,32,32]{4,3,2,1,0:T(8,128)}, f32[1,32]{1,0:T(1,128)}) custom-call(f32[32,896]{1,0:T(8,128)S(1)} %collective-permute-done.12.terms_ref, f32[3,3,3,32,32]{4,3,2,1,0:T(8,128)} %get-tuple-element.87.refs_0_, ...), custom_call_target="tpu_custom_call", output_to_operand_aliasing={{0}: (1, {}), {1}: (2, {}), {2}: (3, {}), {3}: (4, {})} | custom-call | flops 1000000000 | bytes 2000000 | tf_op jit(solution)/shard_map/spread/pallas_call | solution.py:648
  (12 shorter events, 0.0 us)
Async XLA Ops:
  2.1 15.0 %collective-permute-start.1 = (bf16[768,128]{1,0:T(8,128)(2,1)S(1)}, bf16[768,128]{1,0:T(8,128)(2,1)S(1)}, u32[]{:S(2)}, u32[]{:S(2)}) collective-permute-start(bf16[768,128]{1,0:T(8,128)(2,1)S(1)} %get-tuple-element.62), channel_id=1, source_target_pairs={{0,2},{1,3},{2,4},{3,5},{4,6},{5,7},{6,0},{7,1},{8,10},{9,11},{10,... | collective-permute-start | bytes 589832 | tf_op jit(solution)/shard_map/ppermute | solution.py:552
  5.2 12.0 %collective-permute-start.2 = (bf16[768,128]{1,0:T(8,128)(2,1)S(1)}, bf16[768,128]{1,0:T(8,128)(2,1)S(1)}, u32[]{:S(2)}, u32[]{:S(2)}) collective-permute-start(bf16[768,128]{1,0:T(8,128)(2,1)S(1)} %get-tuple-element.63), channel_id=1, source_target_pairs={{0,6},{1,7},{2,0},{3,1},{4,2},{5,3},{6,4},{7,5},{8,14},{9,15},{10,... | collective-permute-start | bytes 589832 | tf_op jit(solution)/shard_map/ppermute | solution.py:552
  8.1 5.5 %collective-permute-start = (bf16[32,256]{1,0:T(8,128)(2,1)S(1)}, bf16[32,256]{1,0:T(8,128)(2,1)S(1)}, u32[]{:S(2)}, u32[]{:S(2)}) collective-permute-start(bf16[32,256]{1,0:T(8,128)(2,1)S(1)} %get-tuple-element.53.edge_ref), channel_id=1, source_target_pairs={{0,1},{1,0},{2,3},{3,2},{4,5},{5,4},{6,7},{7,6},{8,9},{9,8},{10,11... | collective-permute-start | bytes 49160 | tf_op jit(solution)/shard_map/ppermute | solution.py:552
  9.7 3.8 %copy-start = (f32[32]{0:T(128)S(1)}, f32[32]{0:T(128)}, u32[]{:S(2)}) copy-start(f32[32]{0:T(128)} %param.8) | copy-start | bytes 388
  10.3 7.5 %collective-permute-start.3 = (bf16[32,256]{1,0:T(8,128)(2,1)S(1)}, bf16[32,256]{1,0:T(8,128)(2,1)S(1)}, u32[]{:S(2)}, u32[]{:S(2)}) collective-permute-start(bf16[32,256]{1,0:T(8,128)(2,1)S(1)} %get-tuple-element.70), channel_id=1, source_target_pairs={{0,3},{1,2},{2,1},{3,0},{4,7},{5,6},{6,5},{7,4},{8,11},{9,10},{10,... | collective-permute-start | bytes 49160 | tf_op jit(solution)/shard_map/ppermute | solution.py:552
  10.4 7.6 %collective-permute-start.4 = (bf16[32,256]{1,0:T(8,128)(2,1)S(1)}, bf16[32,256]{1,0:T(8,128)(2,1)S(1)}, u32[]{:S(2)}, u32[]{:S(2)}) collective-permute-start(bf16[32,256]{1,0:T(8,128)(2,1)S(1)} %get-tuple-element.70), channel_id=1, source_target_pairs={{0,7},{1,6},{2,5},{3,4},{4,3},{5,2},{6,1},{7,0},{8,15},{9,14},{10,... | collective-permute-start | bytes 49160 | tf_op jit(solution)/shard_map/ppermute | solution.py:552
  19.6 1.4 %collective-permute-start.5 = (f32[32,896]{1,0:T(8,128)S(1)}, f32[32,896]{1,0:T(8,128)S(1)}, u32[]{:S(2)}, u32[]{:S(2)}) collective-permute-start(f32[32,896]{1,0:T(8,128)S(1)} %get-tuple-element.72), channel_id=1, source_target_pairs={{0,8},{1,9},{2,10},{3,11},{4,12},{5,13},{6,14},{7,15},{8,0},{9,1},... | collective-permute-start | bytes 344072 | tf_op jit(solution)/shard_map/ppermute | solution.py:552
  21.2 5.3 %collective-permute-start.6 = (bf16[32,896]{1,0:T(8,128)(2,1)S(1)}, bf16[32,896]{1,0:T(8,128)(2,1)S(1)}, u32[]{:S(2)}, u32[]{:S(2)}) collective-permute-start(bf16[32,896]{1,0:T(8,128)(2,1)S(1)} %add.3.refs_0_), channel_id=1, source_target_pairs={{0,17},{1,16},{2,19},{3,18},{4,21},{5,20},{6,23},{7,22},{8,25},{9,... | collective-permute-start | bytes 172040 | tf_op jit(solution)/shard_map/ppermute | solution.py:552
  22.7 4.6 %collective-permute-start.7 = (bf16[32,896]{1,0:T(8,128)(2,1)S(1)}, bf16[32,896]{1,0:T(8,128)(2,1)S(1)}, u32[]{:S(2)}, u32[]{:S(2)}) collective-permute-start(bf16[32,896]{1,0:T(8,128)(2,1)S(1)} %add.3.refs_0_), channel_id=1, source_target_pairs={{0,16},{1,17},{2,18},{3,19},{4,20},{5,21},{6,22},{7,23},{8,24},{9,... | collective-permute-start | bytes 172040 | tf_op jit(solution)/shard_map/ppermute | solution.py:552
  23.2 4.2 %collective-permute-start.8 = (bf16[32,896]{1,0:T(8,128)(2,1)S(1)}, bf16[32,896]{1,0:T(8,128)(2,1)S(1)}, u32[]{:S(2)}, u32[]{:S(2)}) collective-permute-start(bf16[32,896]{1,0:T(8,128)(2,1)S(1)} %add.3.refs_0_), channel_id=1, source_target_pairs={{0,1},{1,0},{2,3},{3,2},{4,5},{5,4},{6,7},{7,6},{8,9},{9,8},{10,11... | collective-permute-start | bytes 172040 | tf_op jit(solution)/shard_map/ppermute | solution.py:552
  24.7 7.3 %copy-start.1 = (f32[32]{0:T(128)S(1)}, f32[32]{0:T(128)}, u32[]{:S(2)}) copy-start(f32[32]{0:T(128)} %param.10) | copy-start | bytes 388
  27.5 6.5 %collective-permute-start.10 = (bf16[32,896]{1,0:T(8,128)(2,1)S(1)}, bf16[32,896]{1,0:T(8,128)(2,1)S(1)}, u32[]{:S(2)}, u32[]{:S(2)}) collective-permute-start(bf16[32,896]{1,0:T(8,128)(2,1)S(1)} %add.4.refs_0_), channel_id=1, source_target_pairs={{0,6},{1,7},{2,4},{3,5},{4,2},{5,3},{6,0},{7,1},{8,14},{9,15},{10,... | collective-permute-start | bytes 172040 | tf_op jit(solution)/shard_map/ppermute | solution.py:552
  29.6 4.8 %collective-permute-start.11 = (bf16[32,896]{1,0:T(8,128)(2,1)S(1)}, bf16[32,896]{1,0:T(8,128)(2,1)S(1)}, u32[]{:S(2)}, u32[]{:S(2)}) collective-permute-start(bf16[32,896]{1,0:T(8,128)(2,1)S(1)} %add.4.refs_0_), channel_id=1, source_target_pairs={{0,2},{1,3},{2,0},{3,1},{4,6},{5,7},{6,4},{7,5},{8,10},{9,11},{10,... | collective-permute-start | bytes 172040 | tf_op jit(solution)/shard_map/ppermute | solution.py:552
  29.6 5.4 %collective-permute-start.9 = (bf16[32,896]{1,0:T(8,128)(2,1)S(1)}, bf16[32,896]{1,0:T(8,128)(2,1)S(1)}, u32[]{:S(2)}, u32[]{:S(2)}) collective-permute-start(bf16[32,896]{1,0:T(8,128)(2,1)S(1)} %add.4.refs_0_), channel_id=1, source_target_pairs={{0,4},{1,5},{2,6},{3,7},{4,0},{5,1},{6,2},{7,3},{8,12},{9,13},{10,... | collective-permute-start | bytes 172040 | tf_op jit(solution)/shard_map/ppermute | solution.py:552
  35.1 1.3 %collective-permute-start.12 = (f32[32,896]{1,0:T(8,128)S(1)}, f32[32,896]{1,0:T(8,128)S(1)}, u32[]{:S(2)}, u32[]{:S(2)}) collective-permute-start(f32[32,896]{1,0:T(8,128)S(1)} %add.5.terms_ref), channel_id=1, source_target_pairs={{0,8},{1,9},{2,10},{3,11},{4,12},{5,13},{6,14},{7,15},{8,0},{9,1},... | collective-permute-start | bytes 344072 | tf_op jit(solution)/shard_map/ppermute | solution.py:552
